TPU v7x, 128 devices: a whole 4x4x4 slice. The times are simulated.
128 devices in a mesh: dp: 4 (over y_lo, core), cent: 32 (over y_hi, x, z).
Axes of the slice: x: 4, y: 4 (y_hi: 2, y_lo: 2; y = y_hi * 2 + y_lo), z: 4, core: 2. Of those that a mesh axis runs over, the one named last changes fastest.
Arguments:
- embeddings: bfloat16 [8192, 1024], P(('dp', 'cent')), may hold values from -3 to 3
- centroids: bfloat16 [65536, 1024], P('cent'), as said below
Outputs:
- assignments: bfloat16 [8192, 65536], P('dp', 'cent')
- counts: float32 [65536], P('cent')
- centroids_next: bfloat16 [1024, 65536], P('dp', 'cent')
Inputs may be any that keep to these rules, and one draw needn't show every extreme that they name: `centroids`: every entry has magnitude at most 6 / sqrt(1024).
All inputs are finite; a program needn't handle non-finite values.
Results may differ from a plain program's by a relative error of at most 0.014.
Values may be sent and summed in bfloat16 or wider, within the bound.
No kernel may reach another device: no remote copies, remote signals or barrier semaphores. Data moves between devices by JAX's collectives and lax.ppermute only.
A program may use at most 128 MiB of HBM per device.

v0:
```python
import jax
import jax.numpy as jnp
from jax import lax
from jax.sharding import PartitionSpec as P

TEMP_INV = 2.0
PRIOR = 0.05


def on_device(embeddings, centroids):
    gathered = lax.all_gather(embeddings, "cent", axis=0, tiled=True)
    logits = (
        lax.dot_general(
            gathered, centroids, (((1,), (1,)), ((), ())), preferred_element_type=jnp.float32
        )
        * TEMP_INV
    )
    peak = lax.pmax(jnp.max(logits, axis=1), "cent")
    total = lax.psum(jnp.sum(jnp.exp(logits - peak[:, None]), axis=1), "cent")
    lse = peak + jnp.log(total)
    assignments = jnp.exp(logits - lse[:, None]).astype(jnp.bfloat16)
    local_mass = jnp.sum(assignments, axis=0, dtype=jnp.float32)
    width = gathered.shape[1] // lax.axis_size("dp")
    offset = lax.axis_index("dp") * width
    sums = lax.psum_scatter(
        lax.dot_general(
            gathered, assignments, (((0,), (0,)), ((), ())), preferred_element_type=jnp.float32
        ).astype(jnp.bfloat16),
        "dp",
        scatter_dimension=0,
        tiled=True,
    ).astype(jnp.float32)
    counts = lax.psum(local_mass, "dp")
    previous = lax.dynamic_slice_in_dim(centroids, offset, width, 1).astype(jnp.float32).T
    centroids_next = ((sums + PRIOR * previous) / (counts + PRIOR)[None, :]).astype(jnp.bfloat16)
    return (assignments, counts, centroids_next)


def solution(mesh):
    placed = (P(("dp", "cent"), None), P("cent", None))
    return jax.shard_map(
        on_device,
        mesh=mesh,
        in_specs=placed,
        out_specs=(P("dp", "cent"), P("cent"), P("dp", "cent")),
        check_vma=False,
    )
```

profile of v0, /device:TPU:1, one launch (start us, length us, event | category | flops | bytes accessed | tf_op | source)
XLA Modules:
  0.0 376.5 jit_solution(15947120071432678742)
XLA Ops:
  7.2 0.0 all-gather.2.cloned.1.call-start
  7.2 0.7 all-gather.2.cloned.1.call-update
  7.9 0.0 reduce-scatter.2.cloned.1.call-start
  7.9 86.4 %all-gather.2.cloned.1.call-done = bf16[2048,1024]{1,0:T(8,128)(2,1)} async-done(((bf16[64,1024]{1,0:T(8,128)(2,1)}), bf16[2048,1024]{1,0:T(8,128)(2,1)}) %all-gather.2.cloned.1.call-update) | async-done | bytes 4194320 | tf_op jit(solution)/shard_map/all_gather | solution.py:11
  94.4 15.1 %multiply_reduce_fusion = (f32[2048]{0:T(1024)S(1)}, f32[2048,2048]{0,1:T(8,128)}) fusion(bf16[2048,1024]{1,0:T(8,128)(2,1)} %all-gather.2.cloned.1.call-done, bf16[2048,1024]{1,0:T(8,128)(2,1)} %param.3), kind=kOutput, calls=%fused_computation.3 | convolution fusion | flops 8598321152 | bytes 25174016 | tf_op jit(solution)/shard_map/dot_general | solution.py:13
  109.5 78.6 %pmax.7 = f32[2048]{0:T(1024)S(1)} all-reduce(f32[2048]{0:T(1024)S(1)} %get-tuple-element.8), channel_id=1, replica_groups=mesh['dp'=4,'cent'=32] {'cent'}, use_global_device_ids=true, to_apply=%region_1.0 | all-reduce | flops 2048 | bytes 16384 | tf_op jit(solution)/shard_map/pmax | solution.py:18
  188.1 8.5 %exponential_reduce_fusion = f32[2048]{0:T(1024)S(1)} fusion(f32[2048,2048]{0,1:T(8,128)} %get-tuple-element.9, f32[2048]{0:T(1024)S(1)} %pmax.7), kind=kLoop, calls=%fused_computation.2 | loop fusion | flops 12580864 | bytes 16793600 | tf_op jit(solution)/shard_map/reduce_sum | solution.py:19
  196.6 76.0 %psum.14 = f32[2048]{0:T(1024)S(1)} all-reduce(f32[2048]{0:T(1024)S(1)} %exponential_reduce_fusion), channel_id=1, replica_groups=mesh['dp'=4,'cent'=32] {'cent'}, use_global_device_ids=true, to_apply=%region_3.0 | all-reduce | flops 2048 | bytes 16384 | tf_op jit(solution)/shard_map/psum | solution.py:19
  272.6 0.0 copy-start.2
  272.6 7.8 %convert_reduce_fusion = (f32[2048]{0:T(1024)S(1)}, bf16[2048,2048]{0,1:T(8,128)(2,1)S(1)}) fusion(f32[2048]{0:T(1024)S(1)} %log_add_fusion, f32[2048,2048]{0,1:T(8,128)} %get-tuple-element.9), kind=kLoop, calls=%fused_computation | loop fusion | flops 20969472 | bytes 25182208 | tf_op jit(solution)/shard_map/reduce_sum | solution.py:22
  280.4 0.0 copy-start
  280.4 3.2 copy-done
  283.6 0.0 copy-done.2
  283.6 10.4 %convert_bitcast_fusion = bf16[1024,2048]{0,1:T(8,128)(2,1)} fusion(bf16[2048,2048]{0,1:T(8,128)(2,1)S(1)} %get-tuple-element.7, bf16[2048,1024]{1,0:T(8,128)(2,1)S(1)} %copy-done.2), kind=kOutput, calls=%fused_computation.4 | convolution fusion | flops 8592031744 | bytes 16777216 | tf_op jit(solution)/shard_map/dot_general | solution.py:26
  294.0 0.0 reduce-scatter.2.cloned.1.call-update
  294.0 12.2 %copy.5 = bf16[2048,2048]{1,0:T(8,128)(2,1)} copy(bf16[2048,2048]{0,1:T(8,128)(2,1)} %copy-done) | data formatting | bytes 16777216
  306.3 34.3 %psum.15 = f32[2048]{0:T(1024)S(1)} all-reduce(f32[2048]{0:T(1024)S(1)} %get-tuple-element.6), channel_id=1, replica_groups=mesh['dp'=4,'cent'=32] {'dp'}, use_global_device_ids=true, to_apply=%region_5.0 | all-reduce | flops 2048 | bytes 16384 | tf_op jit(solution)/shard_map/psum | solution.py:33
  340.5 0.0 copy-start.1
  340.6 25.7 %reduce-scatter.2.cloned.1.call-done = bf16[256,2048]{0,1:T(8,128)(2,1)} async-done(((bf16[1024,2048]{0,1:T(8,128)(2,1)}), bf16[256,2048]{0,1:T(8,128)(2,1)}) %reduce-scatter.2.cloned.1.call-update) | async-done | bytes 1048592 | tf_op jit(solution)/shard_map/reduce_scatter | solution.py:25
  366.3 2.0 fusion.1
  368.3 1.4 copy.6
  369.7 0.0 copy-done.1
  (2 shorter events, 0.0 us)
Async XLA Ops:
  7.2 87.2 %all-gather.2.cloned.1.call-start = ((), (), s32[]{:S(2)}) async-start(), calls=%async_computation.1 | async-start | bytes 4325376 | tf_op jit(solution)/shard_map/all_gather | solution.py:11
  7.9 358.4 %reduce-scatter.2.cloned.1.call-start = ((), (), s32[]{:S(2)}) async-start(), calls=%async_computation.2 | async-start | bytes 5242880 | tf_op jit(solution)/shard_map/reduce_scatter | solution.py:25
  272.6 11.0 %copy-start.2 = (bf16[2048,1024]{1,0:T(8,128)(2,1)S(1)}, bf16[2048,1024]{1,0:T(8,128)(2,1)}, u32[]{:S(2)}) copy-start(bf16[2048,1024]{1,0:T(8,128)(2,1)} %all-gather.2.cloned.1.call-done) | copy-start | bytes 12582916
  280.4 3.2 copy-start
  340.5 29.1 %copy-start.1 = (f32[2048]{0:T(1024)}, f32[2048]{0:T(1024)S(1)}, u32[]{:S(2)}) copy-start(f32[2048]{0:T(1024)S(1)} %psum.15) | copy-start | bytes 24580
Sparse Core Ops, SparseCore 0:
  11.2 83.1 all-gather.1
  294.1 72.1 reduce-scatter.1
where the time goes:
time: 377 us
  blocking collectives  189 us (50%)
  waiting for transfers between devices  113 us (30%)
  matrix products  25.5 us (7%)
  other arithmetic  18.3 us (5%)
  local copies, waits for them, and re-layouts  16.9 us (4%)
  between operations  14.1 us (4%)
    all_gather x1, waiting for transfers between devices, on_device(): gathered = lax.all_gather(embeddings, 'cent', axis=0, tiled=True)  86.4 us
    pmax x1, blocking collectives, on_device(): peak = lax.pmax(jnp.max(logits, axis=1), 'cent')  78.6 us
    psum x1, blocking collectives, on_device(): total = lax.psum(jnp.sum(jnp.exp(logits - peak[:, None]), axis=1), 'cent')  76 us
    psum x1, blocking collectives, on_device(): counts = lax.psum(local_mass, 'dp')  34.3 us
    reduce_scatter x1, waiting for transfers between devices, on_device(): lax.psum_scatter(lax.dot_general(gathered, assignments, (((0,), (0,)), ((...  25.7 us
    unnamed x8, local copies, waits for them, and re-layouts  16.9 us
    dot_general x1, matrix products, on_device(): lax.dot_general(gathered, centroids, (((1,), (1,)), ((), ())), preferred_...  15.1 us
    dot_general x1, matrix products, on_device(): lax.dot_general(gathered, assignments, (((0,), (0,)), ((), ())), preferre...  10.4 us
  transfers between devices with their start and end apart: 2, of which 2 were waited for; matrix products, arithmetic and copies ran while one was open for 3% of the time, Pallas kernels for 0%

commit v1 on v0

v1 whole, which is shorter than its diff:
```python
import functools
import math

import jax
import jax.numpy as jnp
from jax import lax
from jax.experimental import pallas as pl
from jax.experimental.pallas import tpu as pltpu
from jax.sharding import PartitionSpec as P

TEMP_INV = 2.0
PRIOR = 0.05
SCALE = TEMP_INV * math.log2(math.e)
AXES = ("dp", "cent")
VMEM = pl.BlockSpec(memory_space=pltpu.VMEM)
SMEM = pl.BlockSpec(memory_space=pltpu.SMEM)
ANY = pl.BlockSpec(memory_space=pl.ANY)
LIMIT = 40 * 2**20
TILE = 256


def _perm(move):
    pairs = []
    for dp in range(4):
        for cent in range(32):
            core = dp & 1
            yh, x, z = cent >> 4, (cent >> 2) & 3, cent & 3
            first, second = (x, z) if core == 0 else (z, x)
            yh2, first, second = move(yh, first, second)
            x2, z2 = (first, second) if core == 0 else (second, first)
            pairs.append((dp * 32 + cent, dp * 32 + (yh2 % 2) * 16 + (x2 % 4) * 4 + z2 % 4))
    return pairs


def _first(k):
    return _perm(lambda h, a, b: (h, a + k, b))


def _second(k):
    return _perm(lambda h, a, b: (h, a, b + k))


FAR = _perm(lambda h, a, b: (h + 1, a, b))
CORE = [(i, i ^ 1) for i in range(4)]
NEAR = [(i, i ^ 2) for i in range(4)]


def _send(value, pairs):
    return lax.ppermute(value, AXES, pairs)


def _soft_body(e_ref, c_ref, p_ref, peak_ref, part_ref, lg):
    for i in range(e_ref.shape[0] // TILE):
        rows = pl.ds(i * TILE, TILE)
        e = e_ref[rows, :]
        top = None
        for j in range(4):
            part = lax.dot_general(
                e, c_ref[j * 512:(j + 1) * 512, :], (((1,), (1,)), ((), ())),
                preferred_element_type=jnp.float32,
            )
            lg[:, j * 512:(j + 1) * 512] = part
            for q in range(4):
                piece = part[:, q * 128:(q + 1) * 128]
                top = piece if top is None else jnp.maximum(top, piece)
        peak = jnp.max(top, axis=1, keepdims=True)
        total = None
        for j in range(16):
            cols = slice(j * 128, (j + 1) * 128)
            value = jnp.exp2((lg[:, cols] - peak) * SCALE)
            total = value if total is None else total + value
            p_ref[rows, cols] = value
        total = jnp.sum(total, axis=1, keepdims=True)
        peak = jnp.transpose(jnp.broadcast_to(peak * SCALE, (TILE, 128)))
        total = jnp.transpose(jnp.broadcast_to(total, (TILE, 128)))
        for q in range(TILE // 128):
            row = pl.ds(i * (TILE // 128) + q, 1)
            peak_ref[row, :] = peak[:1, q * 128:(q + 1) * 128]
            part_ref[row, :] = peak[:1, q * 128:(q + 1) * 128] + jnp.log2(
                total[:1, q * 128:(q + 1) * 128]
            )


def _soft(e, c):
    rows = e.shape[0]
    stat = jax.ShapeDtypeStruct((rows // 128, 128), jnp.float32)
    return pl.pallas_call(
        _soft_body,
        out_shape=(jax.ShapeDtypeStruct((rows, 2048), jnp.float32), stat, stat),
        in_specs=[VMEM, VMEM],
        out_specs=(VMEM, VMEM, VMEM),
        scratch_shapes=[pltpu.VMEM((TILE, 2048), jnp.float32)],
        compiler_params=pltpu.CompilerParams(vmem_limit_bytes=LIMIT),
        cost_estimate=pl.CostEstimate(
            flops=2 * rows * 2048 * 1024, bytes_accessed=rows * 2048 * 4, transcendentals=rows * 2048
        ),
        name="soft",
    )(e, c)


def _assign_body(p0, p1, p2, p3, scale_ref, a_ref, mass_ref):
    mass = [jnp.zeros((8, 128), jnp.float32) for _ in range(16)]
    for g in range(16):
        p_ref = (p0, p1, p2, p3)[g // 4]
        scale = jnp.transpose(jnp.broadcast_to(scale_ref[g:g + 1, :], (128, 128)))
        for j in range(16):
            cols = slice(j * 128, (j + 1) * 128)
            value = (p_ref[(g % 4) * 128:(g % 4 + 1) * 128, cols] * scale).astype(jnp.bfloat16)
            a_ref[g * 128:(g + 1) * 128, cols] = value
            mass[j] = mass[j] + jnp.sum(value.astype(jnp.float32).reshape(16, 8, 128), axis=0)
    for j in range(16):
        mass_ref[:, j * 128:(j + 1) * 128] = jnp.sum(mass[j], axis=0, keepdims=True)


def _assign(pieces, scale):
    return pl.pallas_call(
        _assign_body,
        out_shape=(
            jax.ShapeDtypeStruct((2048, 2048), jnp.bfloat16),
            jax.ShapeDtypeStruct((1, 2048), jnp.float32),
        ),
        in_specs=[VMEM] * 5,
        out_specs=(VMEM, VMEM),
        compiler_params=pltpu.CompilerParams(vmem_limit_bytes=LIMIT),
        name="assign",
    )(*pieces, scale)


def _sums_body(offset_ref, e_ref, a_ref, out_ref):
    e = e_ref[:, pl.ds(pl.multiple_of(offset_ref[0], 256), 256)]
    for j in range(4):
        cols = slice(j * 512, (j + 1) * 512)
        out_ref[:, cols] = lax.dot_general(
            e, a_ref[:, cols], (((0,), (0,)), ((), ())), preferred_element_type=jnp.float32
        ).astype(out_ref.dtype)


def _sums(offset, e, a):
    return pl.pallas_call(
        _sums_body,
        out_shape=jax.ShapeDtypeStruct((256, 2048), jnp.bfloat16),
        in_specs=[SMEM, VMEM, VMEM],
        out_specs=VMEM,
        compiler_params=pltpu.CompilerParams(vmem_limit_bytes=LIMIT),
        cost_estimate=pl.CostEstimate(
            flops=2 * 256 * 2048 * 2048, bytes_accessed=2**23, transcendentals=0
        ),
        name="sums",
    )(offset.reshape(1), e, a)


def _place_body(where_ref, a_ref, out_ref, sem):
    copies = [
        pltpu.make_async_copy(
            a_ref.at[pl.ds(i * 64, 64)],
            out_ref.at[pl.ds(pl.multiple_of(where_ref[i] * 64, 64), 64)],
            sem.at[i],
        )
        for i in range(32)
    ]
    for copy in copies:
        copy.start()
    for copy in copies:
        copy.wait()


def _place(where, a):
    return pl.pallas_call(
        _place_body,
        out_shape=jax.ShapeDtypeStruct(a.shape, a.dtype),
        in_specs=[SMEM, ANY],
        out_specs=ANY,
        scratch_shapes=[pltpu.SemaphoreType.DMA((32,))],
        name="place",
    )(where, a)


def _merge(values):
    top = functools.reduce(jnp.maximum, values)
    return top + jnp.log2(sum(jnp.exp2(v - top) for v in values))


def _row_total(part):
    near = part.reshape(4, 4, 128)
    near = _merge([near] + [
        jnp.roll(_send(part, _first(-k)).reshape(4, 4, 128), k, axis=1) for k in (1, -1, 2)
    ])
    part = near.reshape(16, 128)
    wide = part.reshape(4, 512)
    wide = _merge([wide] + [
        jnp.roll(_send(part, _second(-k)).reshape(4, 512), k, axis=0) for k in (1, -1, 2)
    ])
    part = wide.reshape(16, 128)
    return _merge([part, jnp.roll(_send(part, FAR), 64, axis=1)])


def on_device(embeddings, centroids):
    dp, cent = lax.axis_index("dp"), lax.axis_index("cent")
    near, core = dp // 2, dp % 2
    far, x, z = cent // 16, (cent // 4) % 4, cent % 4

    e0 = jnp.concatenate([embeddings, _send(embeddings, FAR)])
    e0 = jnp.concatenate([e0] + [_send(e0, _first(-k)) for k in (1, 2, 3)])
    e1, e3 = _send(e0, _second(-1)), _send(e0, _second(1))
    e2 = jnp.concatenate([_send(e3[:256], _second(1)), _send(e1[256:], _second(-1))])
    pieces = [_soft(e, centroids) for e in (e0, e1, e2, e3)]
    rows = jnp.concatenate([e0, e1, e2, e3])

    peak = jnp.concatenate([p[1] for p in pieces])
    total = _row_total(jnp.concatenate([p[2] for p in pieces]))
    assigned, mass = _assign([p[0] for p in pieces], jnp.exp2(peak - total))

    width = 256
    away, home = (1 - near) * 2, near * 2
    arrived = lax.ppermute(_sums((away + 1 - core) * width, rows, assigned), "dp", CORE)
    kept = _sums((away + core) * width, rows, assigned)
    outgoing = (kept.astype(jnp.float32) + arrived.astype(jnp.float32)).astype(jnp.bfloat16)
    incoming = lax.ppermute(outgoing, "dp", NEAR)
    arrived = lax.ppermute(_sums((home + 1 - core) * width, rows, assigned), "dp", CORE)
    kept = _sums((home + core) * width, rows, assigned)
    mass = mass + lax.ppermute(mass, "dp", CORE)
    mass = mass + lax.ppermute(mass, "dp", NEAR)

    index = jnp.arange(32)
    b, a, h = index // 8, (index // 2) % 4, index % 2
    px = (x + jnp.where(core == 0, a, b)) % 4
    pz = (z + jnp.where(core == 0, b, a)) % 4
    where = (far ^ h) * 16 + px * 4 + pz
    placed = _place(where.astype(jnp.int32), assigned)

    previous = lax.dynamic_slice_in_dim(centroids, dp * width, width, 1).astype(jnp.float32).T
    sums = kept.astype(jnp.float32) + arrived.astype(jnp.float32) + incoming.astype(jnp.float32)
    centroids_next = ((sums + PRIOR * previous) / (mass + PRIOR)).astype(jnp.bfloat16)
    return placed, mass.reshape(2048), centroids_next


def solution(mesh):
    placed = (P(("dp", "cent"), None), P("cent", None))
    return jax.shard_map(
        on_device,
        mesh=mesh,
        in_specs=placed,
        out_specs=(P("dp", "cent"), P("cent"), P("dp", "cent")),
        check_vma=False,
    )
```

time: 377 us -> 392 us (1.040)
  Pallas kernels: 0 us -> 294 us
  blocking collectives: 189 us -> 0 us
  waiting for transfers between devices: 113 us -> 19.9 us
  starting transfers between devices: 0.08 us -> 33 us
  matrix products: 25.5 us -> 0 us
  local copies, waits for them, and re-layouts: 16.9 us -> 37.5 us
  between operations: 14.1 us -> 0.87 us
  other arithmetic: 18.3 us -> 6.07 us
    pallas_call x0 -> x10, Pallas kernels: none -> 294 us  [the longest x1 256 us: _place(): pl.pallas_call(_place_body, out_shape=jax.ShapeDtypeStruct(a.shape, a.dty...]
    psum x2 -> x0, blocking collectives: 110 us -> none  [the longest x1 76 us: on_device(): total = lax.psum(jnp.sum(jnp.exp(logits - peak[:, None]), axis=1), 'cent')]
    all_gather x1 -> x0, waiting for transfers between devices: 86.4 us -> none  [on_device(): gathered = lax.all_gather(embeddings, 'cent', axis=0, tiled=True)]
    pmax x1 -> x0, blocking collectives: 78.6 us -> none  [on_device(): peak = lax.pmax(jnp.max(logits, axis=1), 'cent')]
    ppermute x0 -> x20, starting transfers between devices: none -> 33 us  [the longest x15 21.7 us: _send(): return lax.ppermute(value, AXES, pairs)]
    reduce_scatter x1 -> x0, waiting for transfers between devices: 25.7 us -> none  [on_device(): lax.psum_scatter(lax.dot_general(gathered, assignments, (((0,), (0,)), ((...]
    dot_general x2 -> x0, matrix products: 25.5 us -> none  [the longest x1 15.1 us: on_device(): lax.dot_general(gathered, centroids, (((1,), (1,)), ((), ())), preferred_...]
    ppermute x0 -> x20, waiting for transfers between devices: none -> 19.9 us  [the longest x15 19.9 us: _send(): return lax.ppermute(value, AXES, pairs)]
  transfers between devices with their start and end apart: 2 -> 20, of which waited for: 2 -> 10; matrix products, arithmetic and copies ran while one was open for 3% -> 3% of each run, Pallas kernels for 0% -> 71%
where the time goes in v1:
time: 392 us
  Pallas kernels  294 us (75%)
  local copies, waits for them, and re-layouts  37.5 us (10%)
  starting transfers between devices  33 us (8%)
  waiting for transfers between devices  19.9 us (5%)
  other arithmetic  6.07 us (2%)
    pallas_call x1, Pallas kernels, _place(): pl.pallas_call(_place_body, out_shape=jax.ShapeDtypeStruct(a.shape, a.dty...  256 us
    unnamed x33, local copies, waits for them, and re-layouts  34.9 us
    ppermute x15, starting transfers between devices, _send(): return lax.ppermute(value, AXES, pairs)  21.7 us
    ppermute x15, waiting for transfers between devices, _send(): return lax.ppermute(value, AXES, pairs)  19.9 us
    pallas_call x4, Pallas kernels, _sums(): pl.pallas_call(_sums_body, out_shape=jax.ShapeDtypeStruct((256, 2048), jn...  18.3 us
    pallas_call x4, Pallas kernels, _soft(): pl.pallas_call(_soft_body, out_shape=(jax.ShapeDtypeStruct((rows, 2048),...  11.9 us
    ppermute x1, starting transfers between devices, on_device(): lax.ppermute(_sums((away + 1 - core) * width, rows, assigned), 'dp', CORE)  8.5 us
    pallas_call x1, Pallas kernels, _assign(): pl.pallas_call(_assign_body, out_shape=(jax.ShapeDtypeStruct((2048, 2048)...  8.12 us
  transfers between devices with their start and end apart: 20, of which 10 were waited for; matrix products, arithmetic and copies ran while one was open for 3% of the time, Pallas kernels for 71%

profile of v1, /device:TPU:1, one launch (start us, length us, event | category | flops | bytes accessed | tf_op | source)
XLA Modules:
  0.0 391.7 jit_solution(7702899933305688639)
XLA Ops:
  0.6 3.8 collective-permute-start
  8.3 3.8 collective-permute-start.1
  12.8 5.4 %collective-permute-done.1 = bf16[128,1024]{1,0:T(8,128)(2,1)S(1)} collective-permute-done((bf16[128,1024]{1,0:T(8,128)(2,1)S(1)}, bf16[128,1024]{1,0:T(8,128)(2,1)S(1)}, u32[]{:S(2)}, u32[]{:S(2)}) %collective-permute-start.1) | collective-permute-done | bytes 262176 | tf_op jit(solution)/shard_map/ppermute | solution.py:49
  19.9 1.7 collective-permute-done.3
  23.3 1.8 collective-permute-start.4
  25.1 2.2 copy-done.10
  27.2 3.0 soft.4
  30.2 2.0 copy-done.3
  32.2 5.3 %collective-permute-done.5.e_ref = bf16[512,1024]{1,0:T(8,128)(2,1)S(1)} collective-permute-done((bf16[512,1024]{1,0:T(8,128)(2,1)S(1)}, bf16[512,1024]{1,0:T(8,128)(2,1)S(1)}, u32[]{:S(2)}, u32[]{:S(2)}) %collective-permute-start.5) | collective-permute-done | bytes 1048608 | tf_op jit(solution)/shard_map/ppermute | solution.py:49
  37.7 2.9 collective-permute-start.7
  41.6 2.9 soft.5
  44.6 2.0 copy-done.5
  46.6 3.0 soft.7
  49.6 2.1 copy-done.7
  51.8 3.0 soft.6
  54.8 2.0 copy-done.8
  66.5 2.3 collective-permute-done.13
  68.8 3.2 collective-permute-start.14
  73.3 2.2 copy-done.4
  75.5 2.2 copy-done.6
  77.7 2.2 copy-done.9
  79.9 8.1 %assign.1 = (bf16[2048,2048]{1,0:T(8,128)(2,1)}, f32[1,2048]{1,0:T(1,128)S(1)}) custom-call(f32[512,2048]{1,0:T(8,128)S(1)} %copy-done.4, f32[512,2048]{1,0:T(8,128)S(1)} %copy-done.6, f32[512,2048]{1,0:T(8,128)S(1)} %copy-done.9, f32[512,2048]{1,0:T(8,128)} %copy-done.7, f32[16,128]{1,0:T(8,128)S(1)} %fusion.3.scale_ref), custom_call_target="tpu_custom_call" | custom-call | tf_op jit(solution)/shard_map/assign/pallas_call | solution.py:116
  88.0 3.4 copy-done
  91.4 4.6 %sums.7 = bf16[256,2048]{1,0:T(8,128)(2,1)S(1)} custom-call(s32[1]{0:T(128)} %bitcast.12.offset_ref, bf16[2048,1024]{1,0:T(8,128)(2,1)} %constant_dynamic-update-slice_fusion.7.e_ref, bf16[2048,2048]{1,0:T(8,128)(2,1)S(1)} %copy-done), custom_call_target="tpu_custom_call" | custom-call | flops 2147483648 | bytes 8388608 | tf_op jit(solution)/shard_map/sums/pallas_call | solution.py:139
  96.0 8.5 %collective-permute-start.18 = (bf16[256,2048]{1,0:T(8,128)(2,1)S(1)}, bf16[256,2048]{1,0:T(8,128)(2,1)S(1)}, u32[]{:S(2)}, u32[]{:S(2)}) collective-permute-start(bf16[256,2048]{1,0:T(8,128)(2,1)S(1)} %sums.7), channel_id=1, source_target_pairs={{0,32},{32,0},{64,96},{96,64},{1,33},{33,1},{65,97},{97,65},{2,34}... | collective-permute-start | bytes 3145736 | tf_op jit(solution)/shard_map/ppermute | solution.py:215
  104.5 3.4 copy-done.1
  107.8 4.6 %sums.5 = bf16[256,2048]{1,0:T(8,128)(2,1)S(1)} custom-call(s32[1]{0:T(128)} %bitcast.10.offset_ref, bf16[2048,1024]{1,0:T(8,128)(2,1)} %constant_dynamic-update-slice_fusion.7.e_ref, bf16[2048,2048]{1,0:T(8,128)(2,1)S(1)} %copy-done.1), custom_call_target="tpu_custom_call" | custom-call | flops 2147483648 | bytes 8388608 | tf_op jit(solution)/shard_map/sums/pallas_call | solution.py:139
  112.6 4.6 %sums.6 = bf16[256,2048]{1,0:T(8,128)(2,1)S(1)} custom-call(s32[1]{0:T(128)} %bitcast.11.offset_ref, bf16[2048,1024]{1,0:T(8,128)(2,1)} %constant_dynamic-update-slice_fusion.7.e_ref, bf16[2048,2048]{1,0:T(8,128)(2,1)S(1)} %copy-done.1), custom_call_target="tpu_custom_call" | custom-call | flops 2147483648 | bytes 8388608 | tf_op jit(solution)/shard_map/sums/pallas_call | solution.py:139
  123.6 3.4 copy-done.2
  127.0 4.6 %sums.4 = bf16[256,2048]{1,0:T(8,128)(2,1)S(1)} custom-call(s32[1]{0:T(128)} %bitcast.9.offset_ref, bf16[2048,1024]{1,0:T(8,128)(2,1)} %constant_dynamic-update-slice_fusion.7.e_ref, bf16[2048,2048]{1,0:T(8,128)(2,1)S(1)} %copy-done.2), custom_call_target="tpu_custom_call" | custom-call | flops 2147483648 | bytes 8388608 | tf_op jit(solution)/shard_map/sums/pallas_call | solution.py:139
  131.6 256.2 %place.1 = bf16[2048,2048]{1,0:T(8,128)(2,1)} custom-call(s32[32]{0:T(128)} %fusion.6.where_ref, bf16[2048,2048]{1,0:T(8,128)(2,1)} %get-tuple-element.29.a_ref), custom_call_target="tpu_custom_call" | custom-call | tf_op jit(solution)/shard_map/place/pallas_call | solution.py:168
  388.4 3.3 fusion.1
  (87 shorter events, 27.5 us)
Async XLA Ops:
  0.6 7.0 %collective-permute-start = (bf16[64,1024]{1,0:T(8,128)(2,1)}, bf16[64,1024]{1,0:T(8,128)(2,1)S(1)}, u32[]{:S(2)}, u32[]{:S(2)}) collective-permute-start(bf16[64,1024]{1,0:T(8,128)(2,1)} %param.2), channel_id=1, source_target_pairs={{0,16},{1,17},{2,18},{3,19},{4,20},{5,21},{6,22},{7,23},{8,24},{9,... | collective-permute-start | bytes 393224 | tf_op jit(solution)/shard_map/ppermute | solution.py:49
  8.3 9.9 %collective-permute-start.1 = (bf16[128,1024]{1,0:T(8,128)(2,1)S(1)}, bf16[128,1024]{1,0:T(8,128)(2,1)S(1)}, u32[]{:S(2)}, u32[]{:S(2)}) collective-permute-start(bf16[128,1024]{1,0:T(8,128)(2,1)S(1)} %get-tuple-element.41), channel_id=1, source_target_pairs={{0,12},{1,13},{2,14},{3,15},{4,0},{5,1},{6,2},{7,3},{8,4},{9,5},{1... | collective-permute-start | bytes 786440 | tf_op jit(solution)/shard_map/ppermute | solution.py:49
  12.1 7.1 %collective-permute-start.2 = (bf16[128,1024]{1,0:T(8,128)(2,1)S(1)}, bf16[128,1024]{1,0:T(8,128)(2,1)S(1)}, u32[]{:S(2)}, u32[]{:S(2)}) collective-permute-start(bf16[128,1024]{1,0:T(8,128)(2,1)S(1)} %get-tuple-element.41), channel_id=1, source_target_pairs={{0,8},{1,9},{2,10},{3,11},{4,12},{5,13},{6,14},{7,15},{8,0},{9,1},... | collective-permute-start | bytes 786440 | tf_op jit(solution)/shard_map/ppermute | solution.py:49
  12.1 9.5 %collective-permute-start.3 = (bf16[128,1024]{1,0:T(8,128)(2,1)S(1)}, bf16[128,1024]{1,0:T(8,128)(2,1)S(1)}, u32[]{:S(2)}, u32[]{:S(2)}) collective-permute-start(bf16[128,1024]{1,0:T(8,128)(2,1)S(1)} %get-tuple-element.41), channel_id=1, source_target_pairs={{0,4},{1,5},{2,6},{3,7},{4,8},{5,9},{6,10},{7,11},{8,12},{9,13},{1... | collective-permute-start | bytes 786440 | tf_op jit(solution)/shard_map/ppermute | solution.py:49
  22.4 15.2 %collective-permute-start.5 = (bf16[512,1024]{1,0:T(8,128)(2,1)S(1)}, bf16[512,1024]{1,0:T(8,128)(2,1)S(1)}, u32[]{:S(2)}, u32[]{:S(2)}) collective-permute-start(bf16[512,1024]{1,0:T(8,128)(2,1)S(1)} %get-tuple-element.34.e_ref), channel_id=1, source_target_pairs={{0,1},{1,2},{2,3},{3,0},{4,5},{5,6},{6,7},{7,4},{8,9},{9,10},{10,1... | collective-permute-start | bytes 3145736 | tf_op jit(solution)/shard_map/ppermute | solution.py:49
  23.3 14.4 %collective-permute-start.4 = (bf16[512,1024]{1,0:T(8,128)(2,1)S(1)}, bf16[512,1024]{1,0:T(8,128)(2,1)S(1)}, u32[]{:S(2)}, u32[]{:S(2)}) collective-permute-start(bf16[512,1024]{1,0:T(8,128)(2,1)S(1)} %get-tuple-element.34.e_ref), channel_id=1, source_target_pairs={{0,3},{1,0},{2,1},{3,2},{4,7},{5,4},{6,5},{7,6},{8,11},{9,8},{10,9... | collective-permute-start | bytes 3145736 | tf_op jit(solution)/shard_map/ppermute | solution.py:49
  25.0 2.2 copy-start.10
  30.2 2.0 copy-start.3
  37.6 14.1 %collective-permute-start.6 = (bf16[256,1024]{1,0:T(8,128)(2,1)S(1)}, bf16[256,1024]{1,0:T(8,128)(2,1)S(1)}, u32[]{:S(2)}, u32[]{:S(2)}) collective-permute-start(bf16[256,1024]{1,0:T(8,128)(2,1)S(1)} %slice.102), channel_id=1, source_target_pairs={{0,1},{1,2},{2,3},{3,0},{4,5},{5,6},{6,7},{7,4},{8,9},{9,10},{10,1... | collective-permute-start | bytes 1572872 | tf_op jit(solution)/shard_map/ppermute | solution.py:49
  37.7 14.0 %collective-permute-start.7 = (bf16[256,1024]{1,0:T(8,128)(2,1)S(1)}, bf16[256,1024]{1,0:T(8,128)(2,1)S(1)}, u32[]{:S(2)}, u32[]{:S(2)}) collective-permute-start(bf16[256,1024]{1,0:T(8,128)(2,1)S(1)} %slice.103), channel_id=1, source_target_pairs={{0,3},{1,0},{2,1},{3,2},{4,7},{5,4},{6,5},{7,6},{8,11},{9,8},{10,9... | collective-permute-start | bytes 1572872 | tf_op jit(solution)/shard_map/ppermute | solution.py:49
  44.6 2.1 copy-start.5
  46.6 5.1 %copy-start.11 = (bf16[2048,1024]{1,0:T(8,128)(2,1)S(1)}, bf16[2048,1024]{1,0:T(8,128)(2,1)}, u32[]{:S(2)}) copy-start(bf16[2048,1024]{1,0:T(8,128)(2,1)} %c_ref.7) | copy-start | bytes 12582916
  49.6 2.1 copy-start.7
  54.7 2.0 copy-start.8
  56.7 5.3 %collective-permute-start.8 = (f32[16,128]{1,0:T(8,128)S(1)}, f32[16,128]{1,0:T(8,128)S(1)}, u32[]{:S(2)}, u32[]{:S(2)}) collective-permute-start(f32[16,128]{1,0:T(8,128)S(1)} %pad_maximum_fusion.1), channel_id=1, source_target_pairs={{0,12},{1,13},{2,14},{3,15},{4,0},{5,1},{6,2},{7,3},{8,4},{9,5},{1... | collective-permute-start | bytes 24584 | tf_op jit(solution)/shard_map/ppermute | solution.py:49
  58.3 3.7 collective-permute-start.9
  58.3 4.0 %collective-permute-start.10 = (f32[16,128]{1,0:T(8,128)S(1)}, f32[16,128]{1,0:T(8,128)S(1)}, u32[]{:S(2)}, u32[]{:S(2)}) collective-permute-start(f32[16,128]{1,0:T(8,128)S(1)} %pad_maximum_fusion.1), channel_id=1, source_target_pairs={{0,8},{1,9},{2,10},{3,11},{4,12},{5,13},{6,14},{7,15},{8,0},{9,1},... | collective-permute-start | bytes 24584 | tf_op jit(solution)/shard_map/ppermute | solution.py:49
  62.4 2.6 collective-permute-start.11
  62.5 3.9 collective-permute-start.12
  64.8 4.0 %collective-permute-start.13 = (f32[16,128]{1,0:T(8,128)S(1)}, f32[16,128]{1,0:T(8,128)S(1)}, u32[]{:S(2)}, u32[]{:S(2)}) collective-permute-start(f32[16,128]{1,0:T(8,128)S(1)} %multiply_add_fusion.1), channel_id=1, source_target_pairs={{0,2},{1,3},{2,0},{3,1},{4,6},{5,7},{6,4},{7,5},{8,10},{9,11},{10,... | collective-permute-start | bytes 24584 | tf_op jit(solution)/shard_map/ppermute | solution.py:49
  68.8 4.3 %collective-permute-start.14 = (f32[16,128]{1,0:T(8,128)S(1)}, f32[16,128]{1,0:T(8,128)S(1)}, u32[]{:S(2)}, u32[]{:S(2)}) collective-permute-start(f32[16,128]{1,0:T(8,128)S(1)} %multiply_add_fusion), channel_id=1, source_target_pairs={{0,16},{1,17},{2,18},{3,19},{4,20},{5,21},{6,22},{7,23},{8,24},{9,... | collective-permute-start | bytes 24584 | tf_op jit(solution)/shard_map/ppermute | solution.py:49
  73.3 2.2 copy-start.4
  75.5 2.2 copy-start.6
  77.7 2.2 copy-start.9
  88.0 3.4 copy-start
  96.0 21.2 %collective-permute-start.18 = (bf16[256,2048]{1,0:T(8,128)(2,1)S(1)}, bf16[256,2048]{1,0:T(8,128)(2,1)S(1)}, u32[]{:S(2)}, u32[]{:S(2)}) collective-permute-start(bf16[256,2048]{1,0:T(8,128)(2,1)S(1)} %sums.7), channel_id=1, source_target_pairs={{0,32},{32,0},{64,96},{96,64},{1,33},{33,1},{65,97},{97,65},{2,34}... | collective-permute-start | bytes 3145736 | tf_op jit(solution)/shard_map/ppermute | solution.py:215
  104.5 3.4 copy-start.1
  112.4 276.0 %collective-permute-start.17 = (bf16[256,2048]{1,0:T(8,128)(2,1)S(1)}, bf16[256,2048]{1,0:T(8,128)(2,1)}, u32[]{:S(2)}, u32[]{:S(2)}) collective-permute-start(bf16[256,2048]{1,0:T(8,128)(2,1)S(1)} %sums.5), channel_id=1, source_target_pairs={{0,32},{32,0},{64,96},{96,64},{1,33},{33,1},{65,97},{97,65},{2,34}... | collective-permute-start | bytes 3145736 | tf_op jit(solution)/shard_map/ppermute | solution.py:219
  118.5 269.9 %collective-permute-start.19 = (bf16[256,2048]{1,0:T(8,128)(2,1)}, bf16[256,2048]{1,0:T(8,128)(2,1)}, u32[]{:S(2)}, u32[]{:S(2)}) collective-permute-start(bf16[256,2048]{1,0:T(8,128)(2,1)} %add_convert_fusion), channel_id=1, source_target_pairs={{0,64},{32,96},{64,0},{96,32},{1,65},{33,97},{65,1},{97,33},{2,66}... | collective-permute-start | bytes 3145736 | tf_op jit(solution)/shard_map/ppermute | solution.py:218
  121.1 2.0 collective-permute-start.15
  123.1 264.6 %collective-permute-start.16 = (f32[1,2048]{1,0:T(1,128)S(1)}, f32[1,2048]{1,0:T(1,128)S(1)}, u32[]{:S(2)}, u32[]{:S(2)}) collective-permute-start(f32[1,2048]{1,0:T(1,128)S(1)} %add.161), channel_id=1, source_target_pairs={{0,64},{32,96},{64,0},{96,32},{1,65},{33,97},{65,1},{97,33},{2,66}... | collective-permute-start | bytes 24584 | tf_op jit(solution)/shard_map/ppermute | solution.py:222
  123.6 3.4 copy-start.2

commit v2 on v0

v2 whole, which is shorter than its diff:
```python
import functools
import math

import jax
import jax.numpy as jnp
from jax import lax
from jax.experimental import pallas as pl
from jax.experimental.pallas import tpu as pltpu
from jax.sharding import PartitionSpec as P

TEMP_INV = 2.0
PRIOR = 0.05
SCALE = TEMP_INV * math.log2(math.e)
AXES = ("dp", "cent")
VMEM = pl.BlockSpec(memory_space=pltpu.VMEM)
ANY = pl.BlockSpec(memory_space=pl.ANY)
LIMIT = 10 * 2**20
F32, BF16 = jnp.float32, jnp.bfloat16


def _perm(move):
    pairs = []
    for dp in range(4):
        for cent in range(32):
            core = dp & 1
            far, x, z = cent >> 4, (cent >> 2) & 3, cent & 3
            first, second = (x, z) if core == 0 else (z, x)
            far, first, second = move(far, first, second)
            x, z = (first, second) if core == 0 else (second, first)
            pairs.append((dp * 32 + cent, dp * 32 + (far % 2) * 16 + (x % 4) * 4 + z % 4))
    return pairs


def _first(k):
    return _perm(lambda h, a, b: (h, a + k, b))


def _second(k):
    return _perm(lambda h, a, b: (h, a, b + k))


FAR = _perm(lambda h, a, b: (h + 1, a, b))
CORE = [(i, i ^ 1) for i in range(4)]
NEAR = [(i, i ^ 2) for i in range(4)]


def _send(value, pairs):
    return lax.ppermute(value, AXES, pairs)


def _kernel(body, outs, inputs, name, flops=0, moved=0, exps=0, scratch=(), out_specs=None):
    return pl.pallas_call(
        body,
        out_shape=outs,
        in_specs=[VMEM] * len(inputs),
        out_specs=out_specs if out_specs is not None else jax.tree.map(lambda _: VMEM, outs),
        scratch_shapes=list(scratch),
        compiler_params=pltpu.CompilerParams(vmem_limit_bytes=LIMIT),
        cost_estimate=pl.CostEstimate(flops=flops, bytes_accessed=moved, transcendentals=exps),
        name=name,
    )(*inputs)


def _shape(*dims, dtype=BF16):
    return jax.ShapeDtypeStruct(dims, dtype)


def _place_of(a, b):
    core, cent = lax.axis_index("dp") & 1, lax.axis_index("cent")
    x, z = (cent >> 2) & 3, cent & 3
    first = (jnp.where(core == 0, x, z) + a) & 3
    second = (jnp.where(core == 0, z, x) + b) & 3
    return jnp.where(core == 0, first, second) * 4 + jnp.where(core == 0, second, first)


def _swap_far(row):
    return jnp.where(lax.axis_index("cent") >= 16, pltpu.roll(row, 64, axis=1), row)


def _join_body(*refs):
    start = 0
    for ref in refs[:-1]:
        refs[-1][start:start + ref.shape[0], :] = ref[...]
        start += ref.shape[0]


def _join(*parts):
    rows = sum(p.shape[0] for p in parts)
    return _kernel(_join_body, _shape(rows, parts[0].shape[1]), parts, "join", moved=rows * 4096)


def _soft_body(n, *refs):
    e_refs, c_ref, p_refs, (peak_ref, part_ref, lg) = refs[:n], refs[n], refs[n + 1:2 * n + 1], refs[2 * n + 1:]
    for i in range(n):
        e = e_refs[i][...]
        top = None
        for j in range(4):
            part = lax.dot_general(
                e, c_ref[j * 512:(j + 1) * 512, :], (((1,), (1,)), ((), ())),
                preferred_element_type=F32,
            )
            lg[:, j * 512:(j + 1) * 512] = part
            for q in range(4):
                piece = part[:, q * 128:(q + 1) * 128]
                top = piece if top is None else jnp.maximum(top, piece)
        peak = jnp.max(top, axis=1, keepdims=True)
        total = None
        for j in range(16):
            cols = slice(j * 128, (j + 1) * 128)
            value = jnp.exp2((lg[:, cols] - peak) * SCALE)
            total = value if total is None else total + value
            p_refs[i][:, cols] = value
        total = jnp.sum(total, axis=1, keepdims=True)
        peak = jnp.transpose(jnp.broadcast_to(peak * SCALE, (256, 128)))
        total = jnp.transpose(jnp.broadcast_to(total, (256, 128)))
        for q in range(2):
            lanes = slice(q * 128, (q + 1) * 128)
            row = slice(i * 2 + q, i * 2 + q + 1)
            peak_ref[row, :] = peak[:1, lanes]
            part_ref[row, :] = peak[:1, lanes] + jnp.log2(total[:1, lanes])


def _soft(pieces, c):
    n = len(pieces)
    stat = _shape(2 * n, 128, dtype=F32)
    outs = _kernel(
        functools.partial(_soft_body, n), [_shape(256, 2048, dtype=F32)] * n + [stat, stat], [*pieces, c], "soft",
        flops=n * 2**30, exps=n * 2**19, scratch=[pltpu.VMEM((256, 2048), F32)],
    )
    return outs[:n], outs[n], outs[n + 1]


def _pack_body(places, *refs):
    for ref, slots in zip(refs[:-1], places):
        for i, (a, b) in enumerate(slots):
            refs[-1][pl.ds(_place_of(a, b), 1), :] = _swap_far(ref[i:i + 1, :])


def _pack(parts, places):
    return _kernel(functools.partial(_pack_body, places), _shape(16, 128, dtype=F32), parts, "pack")


def _merge_body(*refs):
    values = [r[...] for r in refs[:-1]]
    top = functools.reduce(jnp.maximum, values)
    refs[-1][...] = top + jnp.log2(sum(jnp.exp2(v - top) for v in values))


def _merge(*values):
    return _kernel(_merge_body, _shape(16, 128, dtype=F32), values, "merge")


def _add_body(a_ref, b_ref, out_ref):
    out_ref[...] = (a_ref[...].astype(F32) + b_ref[...].astype(F32)).astype(out_ref.dtype)


def _add(a, b):
    return _kernel(_add_body, _shape(*a.shape, dtype=a.dtype), [a, b], "add")


def _flip_body(*refs):
    for i, ref in enumerate(refs[:-1]):
        refs[-1][:, i * 256:(i + 1) * 256] = jnp.transpose(ref[...])


def _flip(pieces):
    return _kernel(_flip_body, _shape(1024, 2048), pieces, "flip", moved=2**22)


def _rows_of(et_ref, home):
    dp = lax.axis_index("dp")
    near, core = dp >> 1, dp & 1
    base = (near if home else 1 - near) * 512
    sent = et_ref[pl.ds(pl.multiple_of(base + (1 - core) * 256, 256), 256), :]
    kept = et_ref[pl.ds(pl.multiple_of(base + core * 256, 256), 256), :]
    return [sent, kept]


def _assign_body(start, width, places, *refs):
    p_refs, (n0, n1, n2, n3, total_ref, et_ref, a_ref, sent_ref, kept_ref, mass_ref) = refs[:8], refs[8:]
    for g in range(16):
        call, i, a, b = places[g]
        peak = (n0, n1, n2, n3)[call][i:i + 1, :]
        row = _swap_far(total_ref[pl.ds(_place_of(a, b), 1), :])
        scale = jnp.transpose(jnp.broadcast_to(jnp.exp2(peak - row), (128, 128)))
        for j in range(width // 128):
            cols = slice(start + j * 128, start + (j + 1) * 128)
            value = p_refs[g // 2][(g % 2) * 128:(g % 2 + 1) * 128, cols] * scale
            a_ref[g * 128:(g + 1) * 128, j * 128:(j + 1) * 128] = value.astype(BF16)
    rows = jnp.concatenate(_rows_of(et_ref, False) + [jnp.ones((16, 2048), BF16)], axis=0)
    for n in range(width // 512):
        cols = slice(n * 512, (n + 1) * 512)
        out = jnp.dot(rows, a_ref[:, cols], preferred_element_type=F32)
        sent_ref[:, cols] = out[:256].astype(BF16)
        kept_ref[:, cols] = out[256:512].astype(BF16)
        mass_ref[:, cols] = out[512:513]


def _assign(start, width, places, ps, peaks, total, et):
    return _kernel(
        functools.partial(_assign_body, start, width, places),
        [_shape(2048, width), _shape(256, width), _shape(256, width), _shape(1, width, dtype=F32)],
        [*ps, *peaks, total, et], "assign", flops=2**21 * width, moved=2**12 * width,
    )


def _home_body(et_ref, a0, a1, m0, m1, sent_ref, kept_ref, mass_ref):
    rows = jnp.concatenate(_rows_of(et_ref, True), axis=0)
    for n in range(4):
        cols = slice(n * 512, (n + 1) * 512)
        half = slice((n % 2) * 512, (n % 2 + 1) * 512)
        out = jnp.dot(rows, (a0, a1)[n // 2][:, half], preferred_element_type=F32)
        sent_ref[:, cols] = out[:256].astype(BF16)
        kept_ref[:, cols] = out[256:].astype(BF16)
    mass_ref[:, :1024] = m0[...]
    mass_ref[:, 1024:] = m1[...]


def _home(et, a0, a1, m0, m1):
    return _kernel(
        _home_body, [_shape(256, 2048), _shape(256, 2048), _shape(1, 2048, dtype=F32)],
        [et, a0, a1, m0, m1], "home", flops=2**32, moved=2**23,
    )


def _place_body(a0, a1, out_ref, sem):
    far = lax.axis_index("cent") >> 4
    copies = []
    for i in range(32):
        b, a, h = i // 8, (i // 2) % 4, i % 2
        row = pl.multiple_of(((far ^ h) * 16 + _place_of(a, b)) * 64, 64)
        for n, ref in enumerate((a0, a1)):
            copies.append(pltpu.make_async_copy(
                ref.at[pl.ds(i * 64, 64)], out_ref.at[pl.ds(row, 64), pl.ds(n * 1024, 1024)], sem.at[2 * i + n]
            ))
    for copy in copies:
        copy.start()
    for copy in copies:
        copy.wait()


def _place(a0, a1):
    return _kernel(
        _place_body, _shape(2048, 2048), [a0, a1], "place", moved=2**24,
        scratch=[pltpu.SemaphoreType.DMA((64,))], out_specs=ANY,
    )


def _base_body(kept_ref, arrived_ref, c_ref, out_ref):
    dp = lax.axis_index("dp")
    previous = jnp.transpose(c_ref[:, pl.ds(pl.multiple_of(dp * 256, 256), 256)])
    out_ref[...] = kept_ref[...].astype(F32) + arrived_ref[...].astype(F32) + PRIOR * previous.astype(F32)


def _base(kept, arrived, c):
    return _kernel(_base_body, _shape(256, 2048, dtype=F32), [kept, arrived, c], "base", moved=2**22)


def _final_body(base_ref, in0, in1, mass_ref, out_ref):
    for n, ref in enumerate((in0, in1)):
        cols = slice(n * 1024, (n + 1) * 1024)
        out_ref[:, cols] = ((base_ref[:, cols] + ref[...].astype(F32)) / (mass_ref[:, cols] + PRIOR)).astype(BF16)


def _final(base, in0, in1, mass):
    return _kernel(_final_body, _shape(256, 2048), [base, in0, in1, mass], "final", moved=2**22)


def on_device(embeddings, centroids):
    start = _join(embeddings, _send(embeddings, FAR))
    one, two, three = (_send(start, _first(-k)) for k in (1, 2, 3))
    e0a, e0b = _join(start, one), _join(two, three)
    e3a, e1b = _send(e0a, _second(1)), _send(e0b, _second(-1))
    e3b, e1a = _send(e0b, _second(1)), _send(e0a, _second(-1))
    e2a, e2b = _send(e3a, _second(1)), _send(e1b, _second(-1))

    calls = [[(0, 0, e0a), (0, 1, e0b)], [(3, 0, e3a), (1, 1, e1b)], [(3, 1, e3b), (1, 0, e1a)], [(2, 0, e2a), (2, 1, e2b)]]
    pieces, probs, where, peaks, parts, slots = {}, {}, {}, [], [], []
    for n, call in enumerate(calls):
        p, peak, part = _soft([e for _, _, e in call], centroids)
        for i, (b, half, e) in enumerate(call):
            pieces[b, half], probs[b, half] = e, p[i]
            for q in range(2):
                where[b, half, q] = (n, 2 * i + q, 2 * half + q, b)
        peaks.append(peak)
        parts.append(part)
        slots.append([(2 * half + q, b) for b, half, _ in call for q in range(2)])
    order = [(b, half) for b in range(4) for half in range(2)]
    where = [where[b, half, q] for b, half in order for q in range(2)]

    part = _pack(parts, slots)
    et = _flip([pieces[k] for k in order])
    part = _merge(part, *(_send(part, _first(k)) for k in (1, 2, 3)))
    part = _merge(part, *(_send(part, _second(k)) for k in (1, 2, 3)))
    total = _merge(part, _send(part, FAR))

    ps = [probs[k] for k in order]
    a0, sent, kept, m0 = _assign(0, 1024, where, ps, peaks, total, et)
    out0 = _add(kept, lax.ppermute(sent, "dp", CORE))
    out0, total = lax.optimization_barrier((out0, total))
    in0 = lax.ppermute(out0, "dp", NEAR)
    a1, sent, kept, m1 = _assign(1024, 1024, where, ps, peaks, total, et)
    out1 = _add(kept, lax.ppermute(sent, "dp", CORE))
    out1, a1 = lax.optimization_barrier((out1, a1))
    in1 = lax.ppermute(out1, "dp", NEAR)

    sent, kept, mass = _home(et, a0, a1, m0, m1)
    arrived = lax.ppermute(sent, "dp", CORE)
    mass = _add(mass, lax.ppermute(mass, "dp", CORE))
    mass = _add(mass, lax.ppermute(mass, "dp", NEAR))
    base = _base(kept, arrived, centroids)
    placed = _place(a0, a1)
    return placed, mass.reshape(2048), _final(base, in0, in1, mass)


def solution(mesh):
    placed = (P(("dp", "cent"), None), P("cent", None))
    return jax.shard_map(
        on_device,
        mesh=mesh,
        in_specs=placed,
        out_specs=(P("dp", "cent"), P("cent"), P("dp", "cent")),
        check_vma=False,
    )
```

time: 377 us -> 114 us (0.30)
  blocking collectives: 189 us -> 0 us
  waiting for transfers between devices: 113 us -> 42.1 us
  starting transfers between devices: 0.08 us -> 37.1 us
  Pallas kernels: 0 us -> 30.3 us
  matrix products: 25.5 us -> 0 us
  other arithmetic: 18.3 us -> 0 us
  local copies, waits for them, and re-layouts: 16.9 us -> 3.21 us
  between operations: 14.1 us -> 0.77 us
    psum x2 -> x0, blocking collectives: 110 us -> none  [the longest x1 76 us: on_device(): total = lax.psum(jnp.sum(jnp.exp(logits - peak[:, None]), axis=1), 'cent')]
    all_gather x1 -> x0, waiting for transfers between devices: 86.4 us -> none  [on_device(): gathered = lax.all_gather(embeddings, 'cent', axis=0, tiled=True)]
    pmax x1 -> x0, blocking collectives: 78.6 us -> none  [on_device(): peak = lax.pmax(jnp.max(logits, axis=1), 'cent')]
    ppermute x0 -> x24, waiting for transfers between devices: none -> 42.1 us  [the longest x17 21.5 us: _send(): return lax.ppermute(value, AXES, pairs)]
    ppermute x0 -> x24, starting transfers between devices: none -> 37.1 us  [the longest x17 23.6 us: _send(): return lax.ppermute(value, AXES, pairs)]
    pallas_call x0 -> x22, Pallas kernels: none -> 30.3 us  [_kernel(): pl.pallas_call(body, out_shape=outs, in_specs=[VMEM] * len(inputs), out_s...]
    reduce_scatter x1 -> x0, waiting for transfers between devices: 25.7 us -> none  [on_device(): lax.psum_scatter(lax.dot_general(gathered, assignments, (((0,), (0,)), ((...]
    dot_general x2 -> x0, matrix products: 25.5 us -> none  [the longest x1 15.1 us: on_device(): lax.dot_general(gathered, centroids, (((1,), (1,)), ((), ())), preferred_...]
  transfers between devices with their start and end apart: 2 -> 24, of which waited for: 2 -> 14; matrix products, arithmetic and copies ran while one was open for 3% -> 0% of each run, Pallas kernels for 0% -> 13%
where the time goes in v2:
time: 114 us
  waiting for transfers between devices  42.1 us (37%)
  starting transfers between devices  37.1 us (33%)
  Pallas kernels  30.3 us (27%)
  local copies, waits for them, and re-layouts  3.21 us (3%)
    pallas_call x22, Pallas kernels, _kernel(): pl.pallas_call(body, out_shape=outs, in_specs=[VMEM] * len(inputs), out_s...  30.3 us
    ppermute x17, starting transfers between devices, _send(): return lax.ppermute(value, AXES, pairs)  23.6 us
    ppermute x17, waiting for transfers between devices, _send(): return lax.ppermute(value, AXES, pairs)  21.5 us
    ppermute x1, waiting for transfers between devices, on_device(): mass = _add(mass, lax.ppermute(mass, 'dp', NEAR))  16.7 us
    ppermute x1, starting transfers between devices, on_device(): out0 = _add(kept, lax.ppermute(sent, 'dp', CORE))  9.17 us
    unnamed x8, local copies, waits for them, and re-layouts  3.21 us
  transfers between devices with their start and end apart: 24, of which 14 were waited for; matrix products, arithmetic and copies ran while one was open for 0% of the time, Pallas kernels for 13%

profile of v2, /device:TPU:1, one launch (start us, length us, event | category | flops | bytes accessed | tf_op | source)
XLA Modules:
  0.0 113.6 jit_solution(13818240630244060621)
XLA Ops:
  0.6 3.8 %collective-permute-start = (bf16[64,1024]{1,0:T(8,128)(2,1)}, bf16[64,1024]{1,0:T(8,128)(2,1)S(1)}, u32[]{:S(2)}, u32[]{:S(2)}) collective-permute-start(bf16[64,1024]{1,0:T(8,128)(2,1)} %refs_0_.1), channel_id=1, source_target_pairs={{0,16},{1,17},{2,18},{3,19},{4,20},{5,21},{6,22},{7,23},{8,24},{9,... | collective-permute-start | bytes 393224 | tf_op jit(solution)/shard_map/ppermute | solution.py:48
  4.5 3.2 %collective-permute-done.refs_1_ = bf16[64,1024]{1,0:T(8,128)(2,1)S(1)} collective-permute-done((bf16[64,1024]{1,0:T(8,128)(2,1)}, bf16[64,1024]{1,0:T(8,128)(2,1)S(1)}, u32[]{:S(2)}, u32[]{:S(2)}) %collective-permute-start) | collective-permute-done | bytes 131104 | tf_op jit(solution)/shard_map/ppermute | solution.py:48
  8.5 3.8 %collective-permute-start.1 = (bf16[128,1024]{1,0:T(8,128)(2,1)S(1)}, bf16[128,1024]{1,0:T(8,128)(2,1)S(1)}, u32[]{:S(2)}, u32[]{:S(2)}) collective-permute-start(bf16[128,1024]{1,0:T(8,128)(2,1)S(1)} %join.3.refs_0_), channel_id=1, source_target_pairs={{0,12},{1,13},{2,14},{3,15},{4,0},{5,1},{6,2},{7,3},{8,4},{9,5},{1... | collective-permute-start | bytes 786440 | tf_op jit(solution)/shard_map/ppermute | solution.py:48
  12.4 1.3 %collective-permute-start.2 = (bf16[128,1024]{1,0:T(8,128)(2,1)S(1)}, bf16[128,1024]{1,0:T(8,128)(2,1)S(1)}, u32[]{:S(2)}, u32[]{:S(2)}) collective-permute-start(bf16[128,1024]{1,0:T(8,128)(2,1)S(1)} %join.3.refs_0_), channel_id=1, source_target_pairs={{0,8},{1,9},{2,10},{3,11},{4,12},{5,13},{6,14},{7,15},{8,0},{9,1},... | collective-permute-start | bytes 786440 | tf_op jit(solution)/shard_map/ppermute | solution.py:48
  13.7 2.0 %collective-permute-done.1.refs_1_ = bf16[128,1024]{1,0:T(8,128)(2,1)S(1)} collective-permute-done((bf16[128,1024]{1,0:T(8,128)(2,1)S(1)}, bf16[128,1024]{1,0:T(8,128)(2,1)S(1)}, u32[]{:S(2)}, u32[]{:S(2)}) %collective-permute-start.1) | collective-permute-done | bytes 262176 | tf_op jit(solution)/shard_map/ppermute | solution.py:48
  15.7 1.3 %collective-permute-start.6 = (bf16[256,1024]{1,0:T(8,128)(2,1)S(1)}, bf16[256,1024]{1,0:T(8,128)(2,1)S(1)}, u32[]{:S(2)}, u32[]{:S(2)}) collective-permute-start(bf16[256,1024]{1,0:T(8,128)(2,1)S(1)} %join.4.refs_0_), channel_id=1, source_target_pairs={{0,1},{1,2},{2,3},{3,0},{4,5},{5,6},{6,7},{7,4},{8,9},{9,10},{10,1... | collective-permute-start | bytes 1572872 | tf_op jit(solution)/shard_map/ppermute | solution.py:48
  17.0 4.9 %collective-permute-done.3.refs_1_ = bf16[128,1024]{1,0:T(8,128)(2,1)S(1)} collective-permute-done((bf16[128,1024]{1,0:T(8,128)(2,1)S(1)}, bf16[128,1024]{1,0:T(8,128)(2,1)S(1)}, u32[]{:S(2)}, u32[]{:S(2)}) %collective-permute-start.3) | collective-permute-done | bytes 262176 | tf_op jit(solution)/shard_map/ppermute | solution.py:48
  22.0 2.3 %collective-permute-start.7 = (bf16[256,1024]{1,0:T(8,128)(2,1)S(1)}, bf16[256,1024]{1,0:T(8,128)(2,1)S(1)}, u32[]{:S(2)}, u32[]{:S(2)}) collective-permute-start(bf16[256,1024]{1,0:T(8,128)(2,1)S(1)} %join.5.refs_1_), channel_id=1, source_target_pairs={{0,3},{1,0},{2,1},{3,2},{4,7},{5,4},{6,5},{7,6},{8,11},{9,8},{10,9... | collective-permute-start | bytes 1572872 | tf_op jit(solution)/shard_map/ppermute | solution.py:48
  25.7 2.6 %collective-permute-done.6.refs_0_.refs_6_ = bf16[256,1024]{1,0:T(8,128)(2,1)S(1)} collective-permute-done((bf16[256,1024]{1,0:T(8,128)(2,1)S(1)}, bf16[256,1024]{1,0:T(8,128)(2,1)S(1)}, u32[]{:S(2)}, u32[]{:S(2)}) %collective-permute-start.6) | collective-permute-done | bytes 524320 | tf_op jit(solution)/shard_map/ppermute | solution.py:48
  28.2 2.1 %collective-permute-done.7.refs_1_.refs_3_ = bf16[256,1024]{1,0:T(8,128)(2,1)S(1)} collective-permute-done((bf16[256,1024]{1,0:T(8,128)(2,1)S(1)}, bf16[256,1024]{1,0:T(8,128)(2,1)S(1)}, u32[]{:S(2)}, u32[]{:S(2)}) %collective-permute-start.7) | collective-permute-done | bytes 524320 | tf_op jit(solution)/shard_map/ppermute | solution.py:48
  30.3 3.4 %collective-permute-start.9 = (bf16[256,1024]{1,0:T(8,128)(2,1)S(1)}, bf16[256,1024]{1,0:T(8,128)(2,1)S(1)}, u32[]{:S(2)}, u32[]{:S(2)}) collective-permute-start(bf16[256,1024]{1,0:T(8,128)(2,1)S(1)} %collective-permute-done.7.refs_1_.refs_3_), channel_id=1, source_target_pairs={{0,3},{1,0},{2,1},{3,2},{4,7},{5,4},{6,5},{7,6},{8,11},{9,8},{10,9... | collective-permute-start | bytes 1572872 | tf_op jit(solution)/shard_map/ppermute | solution.py:48
  33.7 2.2 %copy-done = bf16[2048,1024]{1,0:T(8,128)(2,1)S(1)} copy-done((bf16[2048,1024]{1,0:T(8,128)(2,1)S(1)}, bf16[2048,1024]{1,0:T(8,128)(2,1)}, u32[]{:S(2)}) %copy-start) | copy-done | bytes 4194328
  35.9 3.0 %soft.4 = (f32[256,2048]{1,0:T(8,128)S(1)}, f32[256,2048]{1,0:T(8,128)S(1)}, f32[4,128]{1,0:T(4,128)S(1)}, f32[4,128]{1,0:T(4,128)S(1)}) custom-call(bf16[256,1024]{1,0:T(8,128)(2,1)S(1)} %join.4.refs_0_, bf16[256,1024]{1,0:T(8,128)(2,1)S(1)} %join.5.refs_1_, bf16[2048,1024]{1,0:T(8,128)(2,1)S(1)} %copy-done), custom_call_target="tpu_custom_call" | custom-call | flops 2147483648 | tf_op jit(solution)/shard_map/soft/pallas_call | solution.py:52
  38.9 3.0 %soft.6 = (f32[256,2048]{1,0:T(8,128)S(1)}, f32[256,2048]{1,0:T(8,128)S(1)}, f32[4,128]{1,0:T(4,128)S(1)}, f32[4,128]{1,0:T(4,128)S(1)}) custom-call(bf16[256,1024]{1,0:T(8,128)(2,1)S(1)} %collective-permute-done.6.refs_0_.refs_6_, bf16[256,1024]{1,0:T(8,128)(2,1)S(1)} %collective-permute-done.7.refs_1_.refs_3_, bf16[2048,1024]{1,0:T(8,128)(2,1)S(1)} %copy-done), custom_call_target="tpu_custom_call" | custom-call | flops 2147483648 | tf_op jit(solution)/shard_map/soft/pallas_call | solution.py:52
  42.0 3.0 %soft.5 = (f32[256,2048]{1,0:T(8,128)S(1)}, f32[256,2048]{1,0:T(8,128)S(1)}, f32[4,128]{1,0:T(4,128)S(1)}, f32[4,128]{1,0:T(4,128)S(1)}) custom-call(bf16[256,1024]{1,0:T(8,128)(2,1)S(1)} %collective-permute-done.4.refs_0_.refs_7_, bf16[256,1024]{1,0:T(8,128)(2,1)S(1)} %collective-permute-done.5.refs_1_.refs_2_, bf16[2048,1024]{1,0:T(8,128)(2,1)S(1)} %copy-done.1), custom_call_target="tpu_custom_call" | custom-call | flops 2147483648 | tf_op jit(solution)/shard_map/soft/pallas_call | solution.py:52
  45.0 3.1 %soft.7 = (f32[256,2048]{1,0:T(8,128)S(1)}, f32[256,2048]{1,0:T(8,128)S(1)}, f32[4,128]{1,0:T(4,128)S(1)}, f32[4,128]{1,0:T(4,128)S(1)}) custom-call(bf16[256,1024]{1,0:T(8,128)(2,1)S(1)} %collective-permute-done.8.refs_0_.refs_4_, bf16[256,1024]{1,0:T(8,128)(2,1)S(1)} %collective-permute-done.9.refs_1_.refs_5_, bf16[2048,1024]{1,0:T(8,128)(2,1)S(1)} %copy-done.1), custom_call_target="tpu_custom_call" | custom-call | flops 2147483648 | tf_op jit(solution)/shard_map/soft/pallas_call | solution.py:52
  50.8 2.5 %collective-permute-done.11.refs_2_ = f32[16,128]{1,0:T(8,128)S(1)} collective-permute-done((f32[16,128]{1,0:T(8,128)S(1)}, f32[16,128]{1,0:T(8,128)S(1)}, u32[]{:S(2)}, u32[]{:S(2)}) %collective-permute-start.11) | collective-permute-done | bytes 8224 | tf_op jit(solution)/shard_map/ppermute | solution.py:48
  54.8 1.0 collective-permute-done.15.refs_3_
  55.9 1.6 %collective-permute-done.14.refs_2_ = f32[16,128]{1,0:T(8,128)S(1)} collective-permute-done((f32[16,128]{1,0:T(8,128)S(1)}, f32[16,128]{1,0:T(8,128)S(1)}, u32[]{:S(2)}, u32[]{:S(2)}) %collective-permute-start.14) | collective-permute-done | bytes 8224 | tf_op jit(solution)/shard_map/ppermute | solution.py:48
  58.3 3.0 %collective-permute-start.16 = (f32[16,128]{1,0:T(8,128)S(1)}, f32[16,128]{1,0:T(8,128)S(1)}, u32[]{:S(2)}, u32[]{:S(2)}) collective-permute-start(f32[16,128]{1,0:T(8,128)S(1)} %merge.4.refs_0_), channel_id=1, source_target_pairs={{0,16},{1,17},{2,18},{3,19},{4,20},{5,21},{6,22},{7,23},{8,24},{9,... | collective-permute-start | bytes 24584 | tf_op jit(solution)/shard_map/ppermute | solution.py:48
  61.3 1.2 %flip.1.refs_13_.et_ref = bf16[1024,2048]{1,0:T(8,128)(2,1)S(1)} custom-call(bf16[256,1024]{1,0:T(8,128)(2,1)S(1)} %join.4.refs_0_, bf16[256,1024]{1,0:T(8,128)(2,1)S(1)} %join.5.refs_1_, bf16[256,1024]{1,0:T(8,128)(2,1)S(1)} %collective-permute-done.5.refs_1_.refs_2_, bf16[256,1024]{1,0:T(8,128)(2,1)S(1)} %collective-permute-done.7.refs_1_.refs_3_, ...), custom_call_target="tpu_custom_call" | custom-call | bytes 4194304 | tf_op jit(solution)/shard_map/flip/pallas_call | solution.py:52
  62.5 2.9 %assign.2 = (bf16[2048,1024]{1,0:T(8,128)(2,1)S(1)}, bf16[256,1024]{1,0:T(8,128)(2,1)S(1)}, bf16[256,1024]{1,0:T(8,128)(2,1)S(1)}, f32[1,1024]{1,0:T(1,128)S(1)}) custom-call(f32[256,2048]{1,0:T(8,128)S(1)} %get-tuple-element.34.refs_0_, f32[256,2048]{1,0:T(8,128)S(1)} %get-tuple-element.35.refs_1_, f32[256,2048]{1,0:T(8,128)S(1)} %get-tuple-element.36.refs_2_, ...), custom_call_target="tpu_custom_call" | custom-call | flops 2147483648 | bytes 4194304 | tf_op jit(solution)/shard_map/assign/pallas_call | solution.py:52
  65.4 9.2 %collective-permute-start.17 = (bf16[256,1024]{1,0:T(8,128)(2,1)S(1)}, bf16[256,1024]{1,0:T(8,128)(2,1)S(1)}, u32[]{:S(2)}, u32[]{:S(2)}) collective-permute-start(bf16[256,1024]{1,0:T(8,128)(2,1)S(1)} %get-tuple-element.52), channel_id=1, source_target_pairs={{0,32},{32,0},{64,96},{96,64},{1,33},{33,1},{65,97},{97,65},{2,34}... | collective-permute-start | bytes 1572872 | tf_op jit(solution)/shard_map/ppermute | solution.py:299
  74.6 1.5 %collective-permute-done.17.b_ref = bf16[256,1024]{1,0:T(8,128)(2,1)S(1)} collective-permute-done((bf16[256,1024]{1,0:T(8,128)(2,1)S(1)}, bf16[256,1024]{1,0:T(8,128)(2,1)S(1)}, u32[]{:S(2)}, u32[]{:S(2)}) %collective-permute-start.17) | collective-permute-done | bytes 524320 | tf_op jit(solution)/shard_map/ppermute | solution.py:299
  76.2 2.9 %assign.3 = (bf16[2048,1024]{1,0:T(8,128)(2,1)S(1)}, bf16[256,1024]{1,0:T(8,128)(2,1)S(1)}, bf16[256,1024]{1,0:T(8,128)(2,1)S(1)}, f32[1,1024]{1,0:T(1,128)S(1)}) custom-call(f32[256,2048]{1,0:T(8,128)S(1)} %get-tuple-element.34.refs_0_, f32[256,2048]{1,0:T(8,128)S(1)} %get-tuple-element.35.refs_1_, f32[256,2048]{1,0:T(8,128)S(1)} %get-tuple-element.36.refs_2_, ...), custom_call_target="tpu_custom_call" | custom-call | flops 2147483648 | bytes 4194304 | tf_op jit(solution)/shard_map/assign/pallas_call | solution.py:52
  79.6 1.5 %collective-permute-done.18.b_ref = bf16[256,1024]{1,0:T(8,128)(2,1)S(1)} collective-permute-done((bf16[256,1024]{1,0:T(8,128)(2,1)S(1)}, bf16[256,1024]{1,0:T(8,128)(2,1)S(1)}, u32[]{:S(2)}, u32[]{:S(2)}) %collective-permute-start.18) | collective-permute-done | bytes 524320 | tf_op jit(solution)/shard_map/ppermute | solution.py:303
  81.3 4.5 %home.1 = (bf16[256,2048]{1,0:T(8,128)(2,1)S(1)}, bf16[256,2048]{1,0:T(8,128)(2,1)S(1)}, f32[1,2048]{1,0:T(1,128)S(1)}) custom-call(bf16[1024,2048]{1,0:T(8,128)(2,1)S(1)} %flip.1.refs_13_.et_ref, bf16[2048,1024]{1,0:T(8,128)(2,1)S(1)} %get-tuple-element.50.a0, bf16[2048,1024]{1,0:T(8,128)(2,1)S(1)} %get-tuple-element.57.a1, ...), custom_call_target="tpu_custom_call" | custom-call | flops 4294967296 | bytes 8388608 | tf_op jit(solution)/shard_map/home/pallas_call | solution.py:52
  86.2 1.3 %collective-permute-start.22 = (bf16[256,1024]{1,0:T(8,128)(2,1)S(1)}, bf16[256,1024]{1,0:T(8,128)(2,1)S(1)}, u32[]{:S(2)}, u32[]{:S(2)}) collective-permute-start(bf16[256,1024]{1,0:T(8,128)(2,1)S(1)} %add.4), channel_id=1, source_target_pairs={{0,64},{32,96},{64,0},{96,32},{1,65},{33,97},{65,1},{97,33},{2,66}... | collective-permute-start | bytes 1572872 | tf_op jit(solution)/shard_map/ppermute | solution.py:301
  89.3 1.3 %collective-permute-start.20 = (f32[1,2048]{1,0:T(1,128)S(1)}, f32[1,2048]{1,0:T(1,128)S(1)}, u32[]{:S(2)}, u32[]{:S(2)}) collective-permute-start(f32[1,2048]{1,0:T(1,128)S(1)} %add.6.a_ref), channel_id=1, source_target_pairs={{0,64},{32,96},{64,0},{96,32},{1,65},{33,97},{65,1},{97,33},{2,66}... | collective-permute-start | bytes 24584 | tf_op jit(solution)/shard_map/ppermute | solution.py:310
  90.6 3.8 %place.1 = bf16[2048,2048]{1,0:T(8,128)(2,1)} custom-call(bf16[2048,1024]{1,0:T(8,128)(2,1)S(1)} %get-tuple-element.50.a0, bf16[2048,1024]{1,0:T(8,128)(2,1)S(1)} %get-tuple-element.57.a1), custom_call_target="tpu_custom_call" | custom-call | bytes 16777216 | tf_op jit(solution)/shard_map/place/pallas_call | solution.py:52
  94.4 16.7 %collective-permute-done.20.b_ref = f32[1,2048]{1,0:T(1,128)S(1)} collective-permute-done((f32[1,2048]{1,0:T(1,128)S(1)}, f32[1,2048]{1,0:T(1,128)S(1)}, u32[]{:S(2)}, u32[]{:S(2)}) %collective-permute-start.20) | collective-permute-done | bytes 8224 | tf_op jit(solution)/shard_map/ppermute | solution.py:310
  112.3 1.2 %final.1 = bf16[256,2048]{1,0:T(8,128)(2,1)} custom-call(f32[256,2048]{1,0:T(8,128)S(1)} %base.1.base_ref, bf16[256,1024]{1,0:T(8,128)(2,1)S(1)} %collective-permute-done.22.in0, bf16[256,1024]{1,0:T(8,128)(2,1)S(1)} %collective-permute-done.23.in1, f32[1,2048]{1,0:T(1,128)S(1)} %copy-done.3), custom_call_target="tpu_custom_call" | custom-call | bytes 4194304 | tf_op jit(solution)/shard_map/final/pallas_call | solution.py:52
  (46 shorter events, 11.7 us)
Async XLA Ops:
  0.6 7.0 %collective-permute-start = (bf16[64,1024]{1,0:T(8,128)(2,1)}, bf16[64,1024]{1,0:T(8,128)(2,1)S(1)}, u32[]{:S(2)}, u32[]{:S(2)}) collective-permute-start(bf16[64,1024]{1,0:T(8,128)(2,1)} %refs_0_.1), channel_id=1, source_target_pairs={{0,16},{1,17},{2,18},{3,19},{4,20},{5,21},{6,22},{7,23},{8,24},{9,... | collective-permute-start | bytes 393224 | tf_op jit(solution)/shard_map/ppermute | solution.py:48
  7.6 0.9 copy-start.2
  8.5 7.2 %collective-permute-start.1 = (bf16[128,1024]{1,0:T(8,128)(2,1)S(1)}, bf16[128,1024]{1,0:T(8,128)(2,1)S(1)}, u32[]{:S(2)}, u32[]{:S(2)}) collective-permute-start(bf16[128,1024]{1,0:T(8,128)(2,1)S(1)} %join.3.refs_0_), channel_id=1, source_target_pairs={{0,12},{1,13},{2,14},{3,15},{4,0},{5,1},{6,2},{7,3},{8,4},{9,5},{1... | collective-permute-start | bytes 786440 | tf_op jit(solution)/shard_map/ppermute | solution.py:48
  12.4 9.5 %collective-permute-start.3 = (bf16[128,1024]{1,0:T(8,128)(2,1)S(1)}, bf16[128,1024]{1,0:T(8,128)(2,1)S(1)}, u32[]{:S(2)}, u32[]{:S(2)}) collective-permute-start(bf16[128,1024]{1,0:T(8,128)(2,1)S(1)} %join.3.refs_0_), channel_id=1, source_target_pairs={{0,4},{1,5},{2,6},{3,7},{4,8},{5,9},{6,10},{7,11},{8,12},{9,13},{1... | collective-permute-start | bytes 786440 | tf_op jit(solution)/shard_map/ppermute | solution.py:48
  12.4 9.5 %collective-permute-start.2 = (bf16[128,1024]{1,0:T(8,128)(2,1)S(1)}, bf16[128,1024]{1,0:T(8,128)(2,1)S(1)}, u32[]{:S(2)}, u32[]{:S(2)}) collective-permute-start(bf16[128,1024]{1,0:T(8,128)(2,1)S(1)} %join.3.refs_0_), channel_id=1, source_target_pairs={{0,8},{1,9},{2,10},{3,11},{4,12},{5,13},{6,14},{7,15},{8,0},{9,1},... | collective-permute-start | bytes 786440 | tf_op jit(solution)/shard_map/ppermute | solution.py:48
  15.7 12.5 %collective-permute-start.6 = (bf16[256,1024]{1,0:T(8,128)(2,1)S(1)}, bf16[256,1024]{1,0:T(8,128)(2,1)S(1)}, u32[]{:S(2)}, u32[]{:S(2)}) collective-permute-start(bf16[256,1024]{1,0:T(8,128)(2,1)S(1)} %join.4.refs_0_), channel_id=1, source_target_pairs={{0,1},{1,2},{2,3},{3,0},{4,5},{5,6},{6,7},{7,4},{8,9},{9,10},{10,1... | collective-permute-start | bytes 1572872 | tf_op jit(solution)/shard_map/ppermute | solution.py:48
  22.0 8.4 %collective-permute-start.7 = (bf16[256,1024]{1,0:T(8,128)(2,1)S(1)}, bf16[256,1024]{1,0:T(8,128)(2,1)S(1)}, u32[]{:S(2)}, u32[]{:S(2)}) collective-permute-start(bf16[256,1024]{1,0:T(8,128)(2,1)S(1)} %join.5.refs_1_), channel_id=1, source_target_pairs={{0,3},{1,0},{2,1},{3,2},{4,7},{5,4},{6,5},{7,6},{8,11},{9,8},{10,9... | collective-permute-start | bytes 1572872 | tf_op jit(solution)/shard_map/ppermute | solution.py:48
  24.2 17.7 %collective-permute-start.5 = (bf16[256,1024]{1,0:T(8,128)(2,1)S(1)}, bf16[256,1024]{1,0:T(8,128)(2,1)S(1)}, u32[]{:S(2)}, u32[]{:S(2)}) collective-permute-start(bf16[256,1024]{1,0:T(8,128)(2,1)S(1)} %join.4.refs_0_), channel_id=1, source_target_pairs={{0,3},{1,0},{2,1},{3,2},{4,7},{5,4},{6,5},{7,6},{8,11},{9,8},{10,9... | collective-permute-start | bytes 1572872 | tf_op jit(solution)/shard_map/ppermute | solution.py:48
  25.1 16.9 %collective-permute-start.4 = (bf16[256,1024]{1,0:T(8,128)(2,1)S(1)}, bf16[256,1024]{1,0:T(8,128)(2,1)S(1)}, u32[]{:S(2)}, u32[]{:S(2)}) collective-permute-start(bf16[256,1024]{1,0:T(8,128)(2,1)S(1)} %join.5.refs_1_), channel_id=1, source_target_pairs={{0,1},{1,2},{2,3},{3,0},{4,5},{5,6},{6,7},{7,4},{8,9},{9,10},{10,1... | collective-permute-start | bytes 1572872 | tf_op jit(solution)/shard_map/ppermute | solution.py:48
  28.2 16.8 %collective-permute-start.8 = (bf16[256,1024]{1,0:T(8,128)(2,1)S(1)}, bf16[256,1024]{1,0:T(8,128)(2,1)S(1)}, u32[]{:S(2)}, u32[]{:S(2)}) collective-permute-start(bf16[256,1024]{1,0:T(8,128)(2,1)S(1)} %collective-permute-done.6.refs_0_.refs_6_), channel_id=1, source_target_pairs={{0,1},{1,2},{2,3},{3,0},{4,5},{5,6},{6,7},{7,4},{8,9},{9,10},{10,1... | collective-permute-start | bytes 1572872 | tf_op jit(solution)/shard_map/ppermute | solution.py:48
  30.3 14.7 %collective-permute-start.9 = (bf16[256,1024]{1,0:T(8,128)(2,1)S(1)}, bf16[256,1024]{1,0:T(8,128)(2,1)S(1)}, u32[]{:S(2)}, u32[]{:S(2)}) collective-permute-start(bf16[256,1024]{1,0:T(8,128)(2,1)S(1)} %collective-permute-done.7.refs_1_.refs_3_), channel_id=1, source_target_pairs={{0,3},{1,0},{2,1},{3,2},{4,7},{5,4},{6,5},{7,6},{8,11},{9,8},{10,9... | collective-permute-start | bytes 1572872 | tf_op jit(solution)/shard_map/ppermute | solution.py:48
  33.7 2.2 %copy-start = (bf16[2048,1024]{1,0:T(8,128)(2,1)S(1)}, bf16[2048,1024]{1,0:T(8,128)(2,1)}, u32[]{:S(2)}) copy-start(bf16[2048,1024]{1,0:T(8,128)(2,1)} %c_ref.1) | copy-start | bytes 12582916
  38.9 3.1 %copy-start.1 = (bf16[2048,1024]{1,0:T(8,128)(2,1)S(1)}, bf16[2048,1024]{1,0:T(8,128)(2,1)}, u32[]{:S(2)}) copy-start(bf16[2048,1024]{1,0:T(8,128)(2,1)} %c_ref.1) | copy-start | bytes 12582916
  48.2 2.6 %collective-permute-start.12 = (f32[16,128]{1,0:T(8,128)S(1)}, f32[16,128]{1,0:T(8,128)S(1)}, u32[]{:S(2)}, u32[]{:S(2)}) collective-permute-start(f32[16,128]{1,0:T(8,128)S(1)} %pack.1.refs_0_), channel_id=1, source_target_pairs={{0,12},{1,13},{2,14},{3,15},{4,0},{5,1},{6,2},{7,3},{8,4},{9,5},{1... | collective-permute-start | bytes 24584 | tf_op jit(solution)/shard_map/ppermute | solution.py:48
  49.2 4.1 %collective-permute-start.11 = (f32[16,128]{1,0:T(8,128)S(1)}, f32[16,128]{1,0:T(8,128)S(1)}, u32[]{:S(2)}, u32[]{:S(2)}) collective-permute-start(f32[16,128]{1,0:T(8,128)S(1)} %pack.1.refs_0_), channel_id=1, source_target_pairs={{0,8},{1,9},{2,10},{3,11},{4,12},{5,13},{6,14},{7,15},{8,0},{9,1},... | collective-permute-start | bytes 24584 | tf_op jit(solution)/shard_map/ppermute | solution.py:48
  49.2 4.1 %collective-permute-start.10 = (f32[16,128]{1,0:T(8,128)S(1)}, f32[16,128]{1,0:T(8,128)S(1)}, u32[]{:S(2)}, u32[]{:S(2)}) collective-permute-start(f32[16,128]{1,0:T(8,128)S(1)} %pack.1.refs_0_), channel_id=1, source_target_pairs={{0,4},{1,5},{2,6},{3,7},{4,8},{5,9},{6,10},{7,11},{8,12},{9,13},{1... | collective-permute-start | bytes 24584 | tf_op jit(solution)/shard_map/ppermute | solution.py:48
  53.3 2.6 %collective-permute-start.15 = (f32[16,128]{1,0:T(8,128)S(1)}, f32[16,128]{1,0:T(8,128)S(1)}, u32[]{:S(2)}, u32[]{:S(2)}) collective-permute-start(f32[16,128]{1,0:T(8,128)S(1)} %merge.3.refs_0_), channel_id=1, source_target_pairs={{0,3},{1,0},{2,1},{3,2},{4,7},{5,4},{6,5},{7,6},{8,11},{9,8},{10,9... | collective-permute-start | bytes 24584 | tf_op jit(solution)/shard_map/ppermute | solution.py:48
  53.4 4.1 %collective-permute-start.14 = (f32[16,128]{1,0:T(8,128)S(1)}, f32[16,128]{1,0:T(8,128)S(1)}, u32[]{:S(2)}, u32[]{:S(2)}) collective-permute-start(f32[16,128]{1,0:T(8,128)S(1)} %merge.3.refs_0_), channel_id=1, source_target_pairs={{0,2},{1,3},{2,0},{3,1},{4,6},{5,7},{6,4},{7,5},{8,10},{9,11},{10,... | collective-permute-start | bytes 24584 | tf_op jit(solution)/shard_map/ppermute | solution.py:48
  53.9 4.4 %collective-permute-start.13 = (f32[16,128]{1,0:T(8,128)S(1)}, f32[16,128]{1,0:T(8,128)S(1)}, u32[]{:S(2)}, u32[]{:S(2)}) collective-permute-start(f32[16,128]{1,0:T(8,128)S(1)} %merge.3.refs_0_), channel_id=1, source_target_pairs={{0,1},{1,2},{2,3},{3,0},{4,5},{5,6},{6,7},{7,4},{8,9},{9,10},{10,1... | collective-permute-start | bytes 24584 | tf_op jit(solution)/shard_map/ppermute | solution.py:48
  58.3 4.2 %collective-permute-start.16 = (f32[16,128]{1,0:T(8,128)S(1)}, f32[16,128]{1,0:T(8,128)S(1)}, u32[]{:S(2)}, u32[]{:S(2)}) collective-permute-start(f32[16,128]{1,0:T(8,128)S(1)} %merge.4.refs_0_), channel_id=1, source_target_pairs={{0,16},{1,17},{2,18},{3,19},{4,20},{5,21},{6,22},{7,23},{8,24},{9,... | collective-permute-start | bytes 24584 | tf_op jit(solution)/shard_map/ppermute | solution.py:48
  65.4 10.7 %collective-permute-start.17 = (bf16[256,1024]{1,0:T(8,128)(2,1)S(1)}, bf16[256,1024]{1,0:T(8,128)(2,1)S(1)}, u32[]{:S(2)}, u32[]{:S(2)}) collective-permute-start(bf16[256,1024]{1,0:T(8,128)(2,1)S(1)} %get-tuple-element.52), channel_id=1, source_target_pairs={{0,32},{32,0},{64,96},{96,64},{1,33},{33,1},{65,97},{97,65},{2,34}... | collective-permute-start | bytes 1572872 | tf_op jit(solution)/shard_map/ppermute | solution.py:299
  79.2 2.0 %collective-permute-start.18 = (bf16[256,1024]{1,0:T(8,128)(2,1)S(1)}, bf16[256,1024]{1,0:T(8,128)(2,1)S(1)}, u32[]{:S(2)}, u32[]{:S(2)}) collective-permute-start(bf16[256,1024]{1,0:T(8,128)(2,1)S(1)} %get-tuple-element.55), channel_id=1, source_target_pairs={{0,32},{32,0},{64,96},{96,64},{1,33},{33,1},{65,97},{97,65},{2,34}... | collective-permute-start | bytes 1572872 | tf_op jit(solution)/shard_map/ppermute | solution.py:303
  85.8 25.8 %collective-permute-start.21 = (bf16[256,2048]{1,0:T(8,128)(2,1)S(1)}, bf16[256,2048]{1,0:T(8,128)(2,1)S(1)}, u32[]{:S(2)}, u32[]{:S(2)}) collective-permute-start(bf16[256,2048]{1,0:T(8,128)(2,1)S(1)} %get-tuple-element.62), channel_id=1, source_target_pairs={{0,32},{32,0},{64,96},{96,64},{1,33},{33,1},{65,97},{97,65},{2,34}... | collective-permute-start | bytes 3145736 | tf_op jit(solution)/shard_map/ppermute | solution.py:308
  86.2 26.0 %collective-permute-start.22 = (bf16[256,1024]{1,0:T(8,128)(2,1)S(1)}, bf16[256,1024]{1,0:T(8,128)(2,1)S(1)}, u32[]{:S(2)}, u32[]{:S(2)}) collective-permute-start(bf16[256,1024]{1,0:T(8,128)(2,1)S(1)} %add.4), channel_id=1, source_target_pairs={{0,64},{32,96},{64,0},{96,32},{1,65},{33,97},{65,1},{97,33},{2,66}... | collective-permute-start | bytes 1572872 | tf_op jit(solution)/shard_map/ppermute | solution.py:301
  87.5 24.7 %collective-permute-start.23 = (bf16[256,1024]{1,0:T(8,128)(2,1)S(1)}, bf16[256,1024]{1,0:T(8,128)(2,1)S(1)}, u32[]{:S(2)}, u32[]{:S(2)}) collective-permute-start(bf16[256,1024]{1,0:T(8,128)(2,1)S(1)} %add.5), channel_id=1, source_target_pairs={{0,64},{32,96},{64,0},{96,32},{1,65},{33,97},{65,1},{97,33},{2,66}... | collective-permute-start | bytes 1572872 | tf_op jit(solution)/shard_map/ppermute | solution.py:305
  87.7 1.6 %collective-permute-start.19 = (f32[1,2048]{1,0:T(1,128)S(1)}, f32[1,2048]{1,0:T(1,128)S(1)}, u32[]{:S(2)}, u32[]{:S(2)}) collective-permute-start(f32[1,2048]{1,0:T(1,128)S(1)} %get-tuple-element.60.a_ref), channel_id=1, source_target_pairs={{0,32},{32,0},{64,96},{96,64},{1,33},{33,1},{65,97},{97,65},{2,34}... | collective-permute-start | bytes 24584 | tf_op jit(solution)/shard_map/ppermute | solution.py:309
  89.3 21.8 %collective-permute-start.20 = (f32[1,2048]{1,0:T(1,128)S(1)}, f32[1,2048]{1,0:T(1,128)S(1)}, u32[]{:S(2)}, u32[]{:S(2)}) collective-permute-start(f32[1,2048]{1,0:T(1,128)S(1)} %add.6.a_ref), channel_id=1, source_target_pairs={{0,64},{32,96},{64,0},{96,32},{1,65},{33,97},{65,1},{97,33},{2,66}... | collective-permute-start | bytes 24584 | tf_op jit(solution)/shard_map/ppermute | solution.py:310
  111.6 0.7 copy-start.3

commit v3 on v0

v3 whole, which is shorter than its diff:
```python
import functools
import math

import jax
import jax.numpy as jnp
from jax import lax
from jax.experimental import pallas as pl
from jax.experimental.pallas import tpu as pltpu
from jax.sharding import PartitionSpec as P

TEMP_INV = 2.0
PRIOR = 0.05
SCALE = TEMP_INV * math.log2(math.e)
AXES = ("dp", "cent")
VMEM = pl.BlockSpec(memory_space=pltpu.VMEM)
HBM = pl.BlockSpec(memory_space=pltpu.HBM)
LIMIT = 16 * 2**20
F32, BF16 = jnp.float32, jnp.bfloat16


def _perm(move):
    pairs = []
    for dp in range(4):
        for cent in range(32):
            core = dp & 1
            far, x, z = cent >> 4, (cent >> 2) & 3, cent & 3
            first, second = (x, z) if core == 0 else (z, x)
            far, first, second = move(far, first, second)
            x, z = (first, second) if core == 0 else (second, first)
            pairs.append((dp * 32 + cent, dp * 32 + (far % 2) * 16 + (x % 4) * 4 + z % 4))
    return pairs


def _first(k):
    return _perm(lambda h, a, b: (h, a + k, b))


def _second(k):
    return _perm(lambda h, a, b: (h, a, b + k))


FAR = _perm(lambda h, a, b: (h + 1, a, b))
CORE = [(i, i ^ 1) for i in range(4)]
NEAR = [(i, i ^ 2) for i in range(4)]


def _send(value, pairs):
    return lax.ppermute(value, AXES, pairs)


def _shape(*dims, dtype=BF16):
    return jax.ShapeDtypeStruct(dims, dtype)


def _kernel(body, outs, inputs, name, scratch=(), hbm_in=(), hbm_out=(), aliases=None, limit=LIMIT, flops=0):
    return pl.pallas_call(
        body,
        out_shape=outs,
        in_specs=[HBM if i in hbm_in else VMEM for i in range(len(inputs))],
        out_specs=[HBM if i in hbm_out else VMEM for i in range(len(outs))],
        scratch_shapes=list(scratch),
        input_output_aliases=aliases or {},
        compiler_params=pltpu.CompilerParams(vmem_limit_bytes=limit),
        cost_estimate=pl.CostEstimate(flops=flops, bytes_accessed=0, transcendentals=0) if flops else None,
        name=name,
    )(*inputs)


def _place_of(a, b):
    core, cent = lax.axis_index("dp") & 1, lax.axis_index("cent")
    x, z = (cent >> 2) & 3, cent & 3
    first = (jnp.where(core == 0, x, z) + a) & 3
    second = (jnp.where(core == 0, z, x) + b) & 3
    return jnp.where(core == 0, first, second) * 4 + jnp.where(core == 0, second, first)


def _far():
    return lax.axis_index("cent") >> 4


def _swap_far(row):
    return jnp.where(_far() == 0, row, pltpu.roll(row, 64, axis=1))


def _join_body(*refs):
    start = 0
    for ref in refs[:-1]:
        refs[-1][start:start + ref.shape[0], :] = ref[...]
        start += ref.shape[0]


def _join(*parts):
    rows = sum(p.shape[0] for p in parts)
    return _kernel(_join_body, [_shape(rows, 1024)], parts, "join")[0]


def _load_body(e_in, c_ref, e_ref, previous_ref):
    e_ref[...] = e_in[...]
    width = previous_ref.shape[0]
    offset = pl.multiple_of(lax.axis_index("dp") * width, width)
    previous_ref[...] = jnp.transpose(c_ref[:, pl.ds(offset, width)])


def _load(e, c):
    return _kernel(_load_body, [_shape(*e.shape), _shape(256, 2048)], [e, c], "load")


def _soft_body(n, slots, first, *refs):
    e_refs, c_ref, refs = refs[:n], refs[n], refs[n + (1 if first else 2):]
    p_refs, (peak_ref, part_ref, et_ref, lg) = refs[:n], refs[n:]
    for i in range(n):
        e = e_refs[i][...]
        et_ref[:, slots[i] * 256:(slots[i] + 1) * 256] = jnp.transpose(e)
        top = None
        for j in range(4):
            part = lax.dot_general(
                e, c_ref[j * 512:(j + 1) * 512, :], (((1,), (1,)), ((), ())),
                preferred_element_type=F32,
            )
            lg[:, j * 512:(j + 1) * 512] = part
            for q in range(4):
                piece = part[:, q * 128:(q + 1) * 128]
                top = piece if top is None else jnp.maximum(top, piece)
        peak = jnp.max(top, axis=1, keepdims=True)
        total = None
        for j in range(16):
            cols = slice(j * 128, (j + 1) * 128)
            value = jnp.exp2((lg[:, cols] - peak) * SCALE)
            total = value if total is None else total + value
            p_refs[i][:, cols] = value
        total = jnp.sum(total, axis=1, keepdims=True)
        peak = jnp.transpose(jnp.broadcast_to(peak * SCALE, (256, 128)))
        total = jnp.transpose(jnp.broadcast_to(total, (256, 128)))
        for q in range(2):
            lanes = slice(q * 128, (q + 1) * 128)
            row = slice(i * 2 + q, i * 2 + q + 1)
            peak_ref[row, :] = peak[:1, lanes]
            part_ref[row, :] = peak[:1, lanes] + jnp.log2(total[:1, lanes])


def _soft(pieces, slots, c, et):
    n, first = len(pieces), et is None
    stat = _shape(2 * n, 128, dtype=F32)
    outs = [_shape(256, 2048, dtype=F32)] * n + [stat, stat, _shape(1024, 2048)]
    scratch = [pltpu.VMEM((256, 2048), F32)]
    body = functools.partial(_soft_body, n, slots, first)
    inputs, aliases = ([*pieces, c], None) if first else ([*pieces, c, et], {n + 1: n + 2})
    outs = _kernel(body, outs, inputs, "soft", scratch=scratch, aliases=aliases)
    return outs[:n], outs[n], outs[n + 1], outs[n + 2]


def _pack_body(where, *refs):
    out_ref, one = refs[-2], refs[-1]
    for b in range(4):
        for a in range(4):
            call, i = where[b * 4 + a]
            one[pl.ds(_place_of(a, b), 1), :] = _swap_far(refs[call][i:i + 1, :])
    packed = one[...]
    for i in range(32):
        out_ref[i] = packed


def _pack(parts, where):
    return _kernel(
        functools.partial(_pack_body, where), [_shape(32, 16, 128, dtype=F32)], parts, "pack",
        scratch=[pltpu.VMEM((16, 128), F32)],
    )[0]


def _merge_body(in_ref, out_ref):
    values = [in_ref[i] for i in range(32)]
    top = functools.reduce(jnp.maximum, values)
    out_ref[...] = top + jnp.log2(sum(jnp.exp2(v - top) for v in values))


def _merge(values):
    return _kernel(_merge_body, [_shape(16, 128, dtype=F32)], [values], "merge")[0]


def _copy_body(in_ref, out_ref):
    out_ref[...] = in_ref[...]


def _copy(value):
    return _kernel(_copy_body, [_shape(*value.shape)], [value], "copy", flops=2**36)[0]


def _sum_rows(et_ref, home):
    dp = lax.axis_index("dp")
    near, core = dp >> 1, dp & 1
    base = (near if home else 1 - near) * 512
    sent = et_ref[pl.ds(pl.multiple_of(base + (1 - core) * 256, 256), 256), :]
    kept = et_ref[pl.ds(pl.multiple_of(base + core * 256, 256), 256), :]
    return [sent, kept]


def _assign_part(where, start, width, p_refs, peaks, total_ref, a_ref, placed_ref, sem):
    copies = []
    for g in range(16):
        call, i = where[g]
        place = _place_of(g % 4, g // 4)
        row = peaks[call][i:i + 1, :] - _swap_far(total_ref[pl.ds(place, 1), :])
        scale = jnp.transpose(jnp.broadcast_to(jnp.exp2(row), (128, 128)))
        for j in range(width // 128):
            value = p_refs[g // 2][g % 2 * 128:(g % 2 + 1) * 128, start + j * 128:start + (j + 1) * 128] * scale
            a_ref[g * 128:(g + 1) * 128, j * 128:(j + 1) * 128] = value.astype(BF16)
        for t in range(2):
            row = pl.multiple_of(((_far() ^ t) * 16 + place) * 64, 64)
            copy = pltpu.make_async_copy(
                a_ref.at[pl.ds(g * 128 + t * 64, 64)],
                placed_ref.at[pl.ds(row, 64), pl.ds(start, width)],
                sem.at[2 * g + t],
            )
            copy.start()
            copies.append(copy)
    return copies


def _assign_body(where, width, calls, *refs):
    p_refs, peaks, refs = refs[:8], refs[8:8 + calls], refs[8 + calls:]
    total_ref, et_ref, a_ref, placed_ref, sent_ref, kept_ref, mass_ref, sem = refs
    copies = _assign_part(where, 0, width, p_refs, peaks, total_ref, a_ref, placed_ref, sem)
    rows = jnp.concatenate(_sum_rows(et_ref, False) + [jnp.ones((16, 2048), BF16)], axis=0)
    for n in range(width // 256):
        cols = slice(n * 256, (n + 1) * 256)
        out = jnp.dot(rows, a_ref[:, cols], preferred_element_type=F32)
        sent_ref[:, cols] = out[:256].astype(BF16)
        kept_ref[:, cols] = out[256:512].astype(BF16)
        mass_ref[:, cols] = out[512:513]
    for copy in copies:
        copy.wait()


def _assign(where, width, ps, peaks, total, et):
    return _kernel(
        functools.partial(_assign_body, where, width, len(peaks)),
        [_shape(2048, width), _shape(2048, 2048), _shape(256, width), _shape(256, width), _shape(1, width, dtype=F32)],
        [*ps, *peaks, total, et], "assign", scratch=[pltpu.SemaphoreType.DMA((32,))], hbm_out=(1,),
    )


def _rest_body(where, width, calls, n, *refs):
    p_refs, peaks, refs = refs[:8], refs[8:8 + calls], refs[8 + calls:]
    total_ref, et_ref, m0, _, placed_ref, a_ref = refs[:6]
    sent_refs, (kept_ref, mass_ref, sem) = refs[6:6 + n], refs[6 + n:]
    left = 2048 - width
    copies = _assign_part(where, width, left, p_refs, peaks, total_ref, a_ref, placed_ref, sem)
    rows = jnp.concatenate(_sum_rows(et_ref, False) + [jnp.ones((16, 2048), BF16)], axis=0)
    for j in range(left // 256):
        cols = slice(j * 256, (j + 1) * 256)
        out = jnp.dot(rows, a_ref[:, cols], preferred_element_type=F32)
        step = left // n
        sent_refs[j * 256 // step][:, j * 256 % step:j * 256 % step + 256] = out[:256].astype(BF16)
        kept_ref[:, cols] = out[256:512].astype(BF16)
        mass_ref[:, width + j * 256:width + (j + 1) * 256] = out[512:513]
    mass_ref[:, :width] = m0[...]
    for copy in copies:
        copy.wait()


def _rest(where, width, n, ps, peaks, total, et, m0, placed):
    left = 2048 - width
    inputs = [*ps, *peaks, total, et, m0, placed]
    outs = _kernel(
        functools.partial(_rest_body, where, width, len(peaks), n),
        [_shape(2048, 2048), _shape(2048, left)] + [_shape(256, left // n)] * n
        + [_shape(256, left), _shape(1, 2048, dtype=F32)],
        inputs, "rest", scratch=[pltpu.SemaphoreType.DMA((32,))],
        hbm_in=(len(inputs) - 1,), hbm_out=(0,), aliases={len(inputs) - 1: 0},
    )
    return outs[0], outs[1], outs[2:2 + n], outs[2 + n], outs[3 + n]


def _home_body(et_ref, a0, a1, sent_ref, kept_ref):
    rows = jnp.concatenate(_sum_rows(et_ref, True), axis=0)
    start = 0
    for a_ref in (a0, a1):
        for j in range(a_ref.shape[1] // 256):
            cols = slice(start + j * 256, start + (j + 1) * 256)
            out = jnp.dot(rows, a_ref[:, j * 256:(j + 1) * 256], preferred_element_type=F32)
            sent_ref[:, cols] = out[:256].astype(BF16)
            kept_ref[:, cols] = out[256:].astype(BF16)
        start += a_ref.shape[1]


def _home(*inputs):
    return _kernel(_home_body, [_shape(256, 2048), _shape(256, 2048)], inputs, "home", flops=1)


def _fold_body(kept_ref, *refs):
    start = 0
    for ref in refs[:-1]:
        cols = slice(start, start + ref.shape[1])
        start += ref.shape[1]
        refs[-1][:, cols] = (kept_ref[:, cols].astype(F32) + ref[...].astype(F32)).astype(BF16)


def _fold(kept, *sent):
    return _kernel(_fold_body, [_shape(*kept.shape)], [kept, *sent], "fold", flops=1)[0]


def _fold_mass_body(mass_ref, other_ref, *refs):
    _fold_body(*refs[:-1])
    refs[-1][...] = mass_ref[...] + other_ref[...]


def _fold_mass(mass, other, kept, *sent):
    outs = [_shape(*kept.shape), _shape(1, 2048, dtype=F32)]
    return _kernel(_fold_mass_body, outs, [mass, other, kept, *sent], "fold", flops=1)


def _final_body(in0, in1, home_ref, sent_ref, previous_ref, mass_ref, other_ref, out_ref, total_ref):
    total_ref[...] = mass_ref[...] + other_ref[...]
    start = 0
    for ref in (in0, in1):
        cols = slice(start, start + ref.shape[1])
        start += ref.shape[1]
        sums = home_ref[:, cols].astype(F32) + sent_ref[:, cols].astype(F32) + ref[...].astype(F32)
        sums = sums + PRIOR * previous_ref[:, cols].astype(F32)
        out_ref[:, cols] = (sums / (total_ref[:, cols] + PRIOR)).astype(BF16)


def _final(*inputs):
    return _kernel(_final_body, [_shape(256, 2048), _shape(1, 2048, dtype=F32)], inputs, "final")


def on_device(embeddings, centroids):
    width = 1024
    other = _send(embeddings, FAR)
    own = [embeddings] + [_send(embeddings, _first(-k)) for k in (1, 2, 3)]
    other = [other] + [_send(other, _first(-k)) for k in (1, 2, 3)]
    c = centroids
    e, previous = _load(embeddings, centroids)
    own[2], e = lax.optimization_barrier((own[2], e))
    own[0] = e
    e0a = _join(own[0], other[0], own[1], other[1])
    e0b = _join(own[2], other[2], own[3], other[3])
    e3a, e1b = _send(e0a, _second(1)), _send(e0b, _second(-1))
    calls = [_soft([e0a, e0b], (0, 1), c, None)]
    e0a, e0b, et = lax.optimization_barrier((e0a, e0b, calls[0][3]))
    e3b, e1a = _send(e0b, _second(1)), _send(e0a, _second(-1))
    e3a, e1b, et = lax.optimization_barrier((e3a, e1b, et))
    e2a, e2b = _send(e3a, _second(1)), _send(e1b, _second(-1))
    calls.append(_soft([e3a, e1b], (6, 3), c, et))
    calls.append(_soft([e3b, e1a], (7, 2), c, calls[1][3]))
    calls.append(_soft([e2a, e2b], (4, 5), c, calls[2][3]))
    et = calls[3][3]

    probs, where = [None] * 8, [None] * 16
    for n, (call, slots) in enumerate(zip(calls, ((0, 1), (6, 3), (7, 2), (4, 5)))):
        for i, slot in enumerate(slots):
            probs[slot] = call[0][i]
            where[2 * slot], where[2 * slot + 1] = (n, 2 * i), (n, 2 * i + 1)
    peaks = [call[1] for call in calls]
    parts = _pack([call[2] for call in calls], where)
    total = _merge(lax.all_to_all(parts, "cent", 0, 0).reshape(32, 16, 128))

    a0, placed, sent, kept, m0 = _assign(where, width, probs, peaks, total, et)
    out0 = _fold(kept, lax.ppermute(sent, "dp", CORE))
    out0, total = lax.optimization_barrier((out0, total))
    in0 = lax.ppermute(out0, "dp", NEAR)
    placed, a1, sent, kept, mass = _rest(where, width, 2, probs, peaks, total, et, m0, placed)
    other_mass = lax.ppermute(mass, "dp", CORE)
    out1, mass = _fold_mass(mass, other_mass, kept, *(lax.ppermute(part, "dp", CORE) for part in sent))
    in1 = _copy(lax.ppermute(out1, "dp", NEAR))
    a0, out1 = lax.optimization_barrier((a0, out1))
    sent, kept = _home(et, a0, a1)
    in0, sent = lax.optimization_barrier((_copy(in0), sent))
    sent = lax.ppermute(sent, "dp", CORE)
    result, mass = _final(in0, in1, kept, sent, previous, mass, lax.ppermute(mass, "dp", NEAR))
    return placed, mass.reshape(2048), result


def solution(mesh):
    placed = (P(("dp", "cent"), None), P("cent", None))
    return jax.shard_map(
        on_device,
        mesh=mesh,
        in_specs=placed,
        out_specs=(P("dp", "cent"), P("cent"), P("dp", "cent")),
        check_vma=False,
    )
```

time: 377 us -> 99.5 us (0.26)
  blocking collectives: 189 us -> 15.7 us
  waiting for transfers between devices: 113 us -> 18.3 us
  starting transfers between devices: 0.08 us -> 33.8 us
  Pallas kernels: 0 us -> 27.7 us
  matrix products: 25.5 us -> 0 us
  other arithmetic: 18.3 us -> 0 us
  local copies, waits for them, and re-layouts: 16.9 us -> 3.09 us
  between operations: 14.1 us -> 0.76 us
    psum x2 -> x0, blocking collectives: 110 us -> none  [the longest x1 76 us: on_device(): total = lax.psum(jnp.sum(jnp.exp(logits - peak[:, None]), axis=1), 'cent')]
    all_gather x1 -> x0, waiting for transfers between devices: 86.4 us -> none  [on_device(): gathered = lax.all_gather(embeddings, 'cent', axis=0, tiled=True)]
    pmax x1 -> x0, blocking collectives: 78.6 us -> none  [on_device(): peak = lax.pmax(jnp.max(logits, axis=1), 'cent')]
    ppermute x0 -> x21, starting transfers between devices: none -> 33.8 us  [the longest x13 21.2 us: _send(): return lax.ppermute(value, AXES, pairs)]
    pallas_call x0 -> x17, Pallas kernels: none -> 27.7 us  [_kernel(): pl.pallas_call(body, out_shape=outs, in_specs=[HBM if i in hbm_in else VM...]
    reduce_scatter x1 -> x0, waiting for transfers between devices: 25.7 us -> none  [on_device(): lax.psum_scatter(lax.dot_general(gathered, assignments, (((0,), (0,)), ((...]
    dot_general x2 -> x0, matrix products: 25.5 us -> none  [the longest x1 15.1 us: on_device(): lax.dot_general(gathered, centroids, (((1,), (1,)), ((), ())), preferred_...]
    ppermute x0 -> x21, waiting for transfers between devices: none -> 18.3 us  [the longest x1 9.11 us: on_device(): in1 = _copy(lax.ppermute(out1, 'dp', NEAR))]
  transfers between devices with their start and end apart: 2 -> 21, of which waited for: 2 -> 8; matrix products, arithmetic and copies ran while one was open for 3% -> 0% of each run, Pallas kernels for 0% -> 18%
where the time goes in v3:
time: 99.5 us; the launch traced here: 99.3 us
  starting transfers between devices  33.8 us (34%)
  Pallas kernels  27.7 us (28%)
  waiting for transfers between devices  18.3 us (18%)
  blocking collectives  15.7 us (16%)
  local copies, waits for them, and re-layouts  3.09 us (3%)
    pallas_call x17, Pallas kernels, _kernel(): pl.pallas_call(body, out_shape=outs, in_specs=[HBM if i in hbm_in else VM...  27.7 us
    ppermute x13, starting transfers between devices, _send(): return lax.ppermute(value, AXES, pairs)  21.2 us
    all_to_all x1, blocking collectives, on_device(): total = _merge(lax.all_to_all(parts, 'cent', 0, 0).reshape(32, 16, 128))  15.7 us
    ppermute x1, waiting for transfers between devices, on_device(): in1 = _copy(lax.ppermute(out1, 'dp', NEAR))  9.11 us
    ppermute x1, starting transfers between devices, on_device(): out0 = _fold(kept, lax.ppermute(sent, 'dp', CORE))  7.04 us
    ppermute x13, waiting for transfers between devices, _send(): return lax.ppermute(value, AXES, pairs)  6.1 us
    unnamed x6, local copies, waits for them, and re-layouts  3.09 us
    ppermute x1, starting transfers between devices, on_device(): sent = lax.ppermute(sent, 'dp', CORE)  2.08 us
  transfers between devices with their start and end apart: 21, of which 8 were waited for; matrix products, arithmetic and copies ran while one was open for 0% of the time, Pallas kernels for 18%

profile of v3, /device:TPU:1, one launch (start us, length us, event | category | flops | bytes accessed | tf_op | source)
XLA Modules:
  0.0 99.3 jit_solution(1273414731262989193)
XLA Ops:
  0.6 3.8 %collective-permute-start.1 = (bf16[64,1024]{1,0:T(8,128)(2,1)}, bf16[64,1024]{1,0:T(8,128)(2,1)S(1)}, u32[]{:S(2)}, u32[]{:S(2)}) collective-permute-start(bf16[64,1024]{1,0:T(8,128)(2,1)} %e_in.1), channel_id=1, source_target_pairs={{0,16},{1,17},{2,18},{3,19},{4,20},{5,21},{6,22},{7,23},{8,24},{9,... | collective-permute-start | bytes 393224 | tf_op jit(solution)/shard_map/ppermute | solution.py:48
  4.5 3.6 %collective-permute-start = (bf16[64,1024]{1,0:T(8,128)(2,1)}, bf16[64,1024]{1,0:T(8,128)(2,1)S(1)}, u32[]{:S(2)}, u32[]{:S(2)}) collective-permute-start(bf16[64,1024]{1,0:T(8,128)(2,1)} %e_in.1), channel_id=1, source_target_pairs={{0,8},{1,9},{2,10},{3,11},{4,12},{5,13},{6,14},{7,15},{8,0},{9,1},... | collective-permute-start | bytes 393224 | tf_op jit(solution)/shard_map/ppermute | solution.py:48
  8.1 0.7 collective-permute-start.5
  8.8 0.5 collective-permute-start.6
  9.3 3.3 %collective-permute-start.4 = (bf16[64,1024]{1,0:T(8,128)(2,1)S(1)}, bf16[64,1024]{1,0:T(8,128)(2,1)S(1)}, u32[]{:S(2)}, u32[]{:S(2)}) collective-permute-start(bf16[64,1024]{1,0:T(8,128)(2,1)S(1)} %collective-permute-done.1.refs_1_), channel_id=1, source_target_pairs={{0,8},{1,9},{2,10},{3,11},{4,12},{5,13},{6,14},{7,15},{8,0},{9,1},... | collective-permute-start | bytes 393224 | tf_op jit(solution)/shard_map/ppermute | solution.py:48
  12.6 0.7 collective-permute-start.2
  13.3 0.5 collective-permute-start.3
  13.7 2.2 %copy-done = bf16[2048,1024]{1,0:T(8,128)(2,1)S(1)} copy-done((bf16[2048,1024]{1,0:T(8,128)(2,1)S(1)}, bf16[2048,1024]{1,0:T(8,128)(2,1)}, u32[]{:S(2)}) %copy-start) | copy-done | bytes 4194328
  15.9 0.9 copy-done.2
  17.3 2.5 %collective-permute-start.10 = (bf16[256,1024]{1,0:T(8,128)(2,1)S(1)}, bf16[256,1024]{1,0:T(8,128)(2,1)S(1)}, u32[]{:S(2)}, u32[]{:S(2)}) collective-permute-start(bf16[256,1024]{1,0:T(8,128)(2,1)S(1)} %join.3.refs_1_), channel_id=1, source_target_pairs={{0,3},{1,0},{2,1},{3,2},{4,7},{5,4},{6,5},{7,6},{8,11},{9,8},{10,9... | collective-permute-start | bytes 1572872 | tf_op jit(solution)/shard_map/ppermute | solution.py:48
  20.0 3.1 %soft.4 = (f32[256,2048]{1,0:T(8,128)S(1)}, f32[256,2048]{1,0:T(8,128)S(1)}, f32[4,128]{1,0:T(4,128)S(1)}, f32[4,128]{1,0:T(4,128)S(1)}, bf16[1024,2048]{1,0:T(8,128)(2,1)S(1)}) custom-call(bf16[256,1024]{1,0:T(8,128)(2,1)S(1)} %join.2.refs_0_, bf16[256,1024]{1,0:T(8,128)(2,1)S(1)} %join.3.refs_1_, bf16[2048,1024]{1,0:T(8,128)(2,1)S(1)} %copy-done.1), custom_call_target="tpu_custom_call" | custom-call | tf_op jit(solution)/shard_map/soft/pallas_call | solution.py:56
  23.0 0.9 collective-permute-start.7
  23.9 1.9 %collective-permute-start.8 = (bf16[256,1024]{1,0:T(8,128)(2,1)S(1)}, bf16[256,1024]{1,0:T(8,128)(2,1)S(1)}, u32[]{:S(2)}, u32[]{:S(2)}) collective-permute-start(bf16[256,1024]{1,0:T(8,128)(2,1)S(1)} %join.2.refs_0_), channel_id=1, source_target_pairs={{0,3},{1,0},{2,1},{3,2},{4,7},{5,4},{6,5},{7,6},{8,11},{9,8},{10,9... | collective-permute-start | bytes 1572872 | tf_op jit(solution)/shard_map/ppermute | solution.py:48
  25.9 3.5 %collective-permute-done.9.refs_0_ = bf16[256,1024]{1,0:T(8,128)(2,1)S(1)} collective-permute-done((bf16[256,1024]{1,0:T(8,128)(2,1)S(1)}, bf16[256,1024]{1,0:T(8,128)(2,1)S(1)}, u32[]{:S(2)}, u32[]{:S(2)}) %collective-permute-start.9) | collective-permute-done | bytes 524320 | tf_op jit(solution)/shard_map/ppermute | solution.py:48
  29.5 2.7 %collective-permute-start.12 = (bf16[256,1024]{1,0:T(8,128)(2,1)S(1)}, bf16[256,1024]{1,0:T(8,128)(2,1)S(1)}, u32[]{:S(2)}, u32[]{:S(2)}) collective-permute-start(bf16[256,1024]{1,0:T(8,128)(2,1)S(1)} %collective-permute-done.10.refs_1_), channel_id=1, source_target_pairs={{0,3},{1,0},{2,1},{3,2},{4,7},{5,4},{6,5},{7,6},{8,11},{9,8},{10,9... | collective-permute-start | bytes 1572872 | tf_op jit(solution)/shard_map/ppermute | solution.py:48
  32.1 3.1 %soft.5 = (f32[256,2048]{1,0:T(8,128)S(1)}, f32[256,2048]{1,0:T(8,128)S(1)}, f32[4,128]{1,0:T(4,128)S(1)}, f32[4,128]{1,0:T(4,128)S(1)}, bf16[1024,2048]{1,0:T(8,128)(2,1)S(1)}) custom-call(bf16[256,1024]{1,0:T(8,128)(2,1)S(1)} %collective-permute-done.9.refs_0_, ...), custom_call_target="tpu_custom_call", output_to_operand_aliasing={{4}: (3, {})} | custom-call | tf_op jit(solution)/shard_map/soft/pallas_call | solution.py:56
  35.2 3.1 %soft.6 = (f32[256,2048]{1,0:T(8,128)S(1)}, f32[256,2048]{1,0:T(8,128)S(1)}, f32[4,128]{1,0:T(4,128)S(1)}, f32[4,128]{1,0:T(4,128)S(1)}, bf16[1024,2048]{1,0:T(8,128)(2,1)S(1)}) custom-call(bf16[256,1024]{1,0:T(8,128)(2,1)S(1)} %collective-permute-done.7.refs_0_, ...), custom_call_target="tpu_custom_call", output_to_operand_aliasing={{4}: (3, {})} | custom-call | tf_op jit(solution)/shard_map/soft/pallas_call | solution.py:56
  38.3 2.4 %collective-permute-done.11.refs_0_ = bf16[256,1024]{1,0:T(8,128)(2,1)S(1)} collective-permute-done((bf16[256,1024]{1,0:T(8,128)(2,1)S(1)}, bf16[256,1024]{1,0:T(8,128)(2,1)S(1)}, u32[]{:S(2)}, u32[]{:S(2)}) %collective-permute-start.11) | collective-permute-done | bytes 524320 | tf_op jit(solution)/shard_map/ppermute | solution.py:48
  40.7 3.1 %soft.7 = (f32[256,2048]{1,0:T(8,128)S(1)}, f32[256,2048]{1,0:T(8,128)S(1)}, f32[4,128]{1,0:T(4,128)S(1)}, f32[4,128]{1,0:T(4,128)S(1)}, bf16[1024,2048]{1,0:T(8,128)(2,1)S(1)}) custom-call(bf16[256,1024]{1,0:T(8,128)(2,1)S(1)} %collective-permute-done.11.refs_0_, ...), custom_call_target="tpu_custom_call", output_to_operand_aliasing={{4}: (3, {})} | custom-call | tf_op jit(solution)/shard_map/soft/pallas_call | solution.py:56
  43.9 15.7 %all_to_all.5.in_ref = f32[32,16,128]{2,1,0:T(8,128)S(1)} all-to-all(f32[32,16,128]{2,1,0:T(8,128)S(1)} %pack.1), channel_id=1, replica_groups=mesh['dp'=4,'cent'=32] {'cent'}, dimensions={0} | all-to-all | bytes 524288 | tf_op jit(solution)/shard_map/all_to_all | solution.py:356
  59.7 3.8 %assign.1 = (bf16[2048,1024]{1,0:T(8,128)(2,1)S(1)}, bf16[2048,2048]{1,0:T(8,128)(2,1)}, bf16[256,1024]{1,0:T(8,128)(2,1)S(1)}, bf16[256,1024]{1,0:T(8,128)(2,1)S(1)}, f32[1,1024]{1,0:T(1,128)S(1)}) custom-call(f32[256,2048]{1,0:T(8,128)S(1)} %get-tuple-element.58.refs_0_, f32[256,2048]{1,0:T(8,128)S(1)} %get-tuple-element.59.refs_1_, ...), custom_call_target="tpu_custom_call" | custom-call | tf_op jit(solution)/shard_map/assign/pallas_call | solution.py:56
  63.5 7.0 %collective-permute-start.13 = (bf16[256,1024]{1,0:T(8,128)(2,1)S(1)}, bf16[256,1024]{1,0:T(8,128)(2,1)S(1)}, u32[]{:S(2)}, u32[]{:S(2)}) collective-permute-start(bf16[256,1024]{1,0:T(8,128)(2,1)S(1)} %get-tuple-element.85), channel_id=1, source_target_pairs={{0,32},{32,0},{64,96},{96,64},{1,33},{33,1},{65,97},{97,65},{2,34}... | collective-permute-start | bytes 1572872 | tf_op jit(solution)/shard_map/ppermute | solution.py:359
  70.6 1.5 %collective-permute-done.13.refs_0_ = bf16[256,1024]{1,0:T(8,128)(2,1)S(1)} collective-permute-done((bf16[256,1024]{1,0:T(8,128)(2,1)S(1)}, bf16[256,1024]{1,0:T(8,128)(2,1)S(1)}, u32[]{:S(2)}, u32[]{:S(2)}) %collective-permute-start.13) | collective-permute-done | bytes 524320 | tf_op jit(solution)/shard_map/ppermute | solution.py:359
  72.2 0.7 collective-permute-start.14
  72.9 3.9 %rest.1 = (bf16[2048,2048]{1,0:T(8,128)(2,1)}, bf16[2048,1024]{1,0:T(8,128)(2,1)S(1)}, bf16[256,512]{1,0:T(8,128)(2,1)S(1)}, bf16[256,512]{1,0:T(8,128)(2,1)S(1)...) custom-call(f32[256,2048]{1,0:T(8,128)S(1)} %get-tuple-element.58.refs_0_, ...), custom_call_target="tpu_custom_call", output_to_operand_aliasing={{0}: (15, {})} | custom-call | tf_op jit(solution)/shard_map/rest/pallas_call | solution.py:56
  76.8 0.7 collective-permute-start.16
  78.0 1.0 %collective-permute-done.15.other_ref = f32[1,2048]{1,0:T(1,128)S(1)} collective-permute-done((f32[1,2048]{1,0:T(1,128)S(1)}, f32[1,2048]{1,0:T(1,128)S(1)}, u32[]{:S(2)}, u32[]{:S(2)}) %collective-permute-start.15) | collective-permute-done | bytes 8224 | tf_op jit(solution)/shard_map/ppermute | solution.py:363
  79.2 1.1 %collective-permute-start.18 = (bf16[256,1024]{1,0:T(8,128)(2,1)S(1)}, bf16[256,1024]{1,0:T(8,128)(2,1)S(1)}, u32[]{:S(2)}, u32[]{:S(2)}) collective-permute-start(bf16[256,1024]{1,0:T(8,128)(2,1)S(1)} %get-tuple-element.96), channel_id=1, source_target_pairs={{0,64},{32,96},{64,0},{96,32},{1,65},{33,97},{65,1},{97,33},{2,66}... | collective-permute-start | bytes 1572872 | tf_op jit(solution)/shard_map/ppermute | solution.py:365
  80.7 4.5 %home.1 = (bf16[256,2048]{1,0:T(8,128)(2,1)S(1)}, bf16[256,2048]{1,0:T(8,128)(2,1)S(1)}) custom-call(bf16[1024,2048]{1,0:T(8,128)(2,1)S(1)} %get-tuple-element.83.refs_13_.et_ref, bf16[2048,1024]{1,0:T(8,128)(2,1)S(1)} %get-tuple-element.97.a0, bf16[2048,1024]{1,0:T(8,128)(2,1)S(1)} %get-tuple-element.98.a1), custom_call_target="tpu_custom_call" | custom-call | flops 1 | tf_op jit(solution)/shard_map/home/pallas_call | solution.py:56
  85.7 2.1 %collective-permute-start.19 = (bf16[256,2048]{1,0:T(8,128)(2,1)S(1)}, bf16[256,2048]{1,0:T(8,128)(2,1)S(1)}, u32[]{:S(2)}, u32[]{:S(2)}) collective-permute-start(bf16[256,2048]{1,0:T(8,128)(2,1)S(1)} %get-tuple-element.102), channel_id=1, source_target_pairs={{0,32},{32,0},{64,96},{96,64},{1,33},{33,1},{65,97},{97,65},{2,34}... | collective-permute-start | bytes 3145736 | tf_op jit(solution)/shard_map/ppermute | solution.py:369
  87.8 9.1 %collective-permute-done.18.in_ref = bf16[256,1024]{1,0:T(8,128)(2,1)S(1)} collective-permute-done((bf16[256,1024]{1,0:T(8,128)(2,1)S(1)}, bf16[256,1024]{1,0:T(8,128)(2,1)S(1)}, u32[]{:S(2)}, u32[]{:S(2)}) %collective-permute-start.18) | collective-permute-done | bytes 524320 | tf_op jit(solution)/shard_map/ppermute | solution.py:365
  97.1 2.2 %final.1 = (bf16[256,2048]{1,0:T(8,128)(2,1)}, f32[1,2048]{1,0:T(1,128)}) custom-call(bf16[256,1024]{1,0:T(8,128)(2,1)S(1)} %copy.15.in0, bf16[256,1024]{1,0:T(8,128)(2,1)S(1)} %copy.16.in1, bf16[256,2048]{1,0:T(8,128)(2,1)S(1)} %get-tuple-element.101.home_ref, bf16[256,2048]{1,0:T(8,128)(2,1)S(1)} %collective-permute-done.19.sent_ref, ...), custom_call_target="tpu_custom_call" | custom-call | tf_op jit(solution)/shard_map/final/pallas_call | solution.py:56
  (34 shorter events, 2.7 us)
Async XLA Ops:
  0.6 8.2 %collective-permute-start.1 = (bf16[64,1024]{1,0:T(8,128)(2,1)}, bf16[64,1024]{1,0:T(8,128)(2,1)S(1)}, u32[]{:S(2)}, u32[]{:S(2)}) collective-permute-start(bf16[64,1024]{1,0:T(8,128)(2,1)} %e_in.1), channel_id=1, source_target_pairs={{0,16},{1,17},{2,18},{3,19},{4,20},{5,21},{6,22},{7,23},{8,24},{9,... | collective-permute-start | bytes 393224 | tf_op jit(solution)/shard_map/ppermute | solution.py:48
  4.5 8.8 %collective-permute-start = (bf16[64,1024]{1,0:T(8,128)(2,1)}, bf16[64,1024]{1,0:T(8,128)(2,1)S(1)}, u32[]{:S(2)}, u32[]{:S(2)}) collective-permute-start(bf16[64,1024]{1,0:T(8,128)(2,1)} %e_in.1), channel_id=1, source_target_pairs={{0,8},{1,9},{2,10},{3,11},{4,12},{5,13},{6,14},{7,15},{8,0},{9,1},... | collective-permute-start | bytes 393224 | tf_op jit(solution)/shard_map/ppermute | solution.py:48
  8.1 9.1 %collective-permute-start.5 = (bf16[64,1024]{1,0:T(8,128)(2,1)}, bf16[64,1024]{1,0:T(8,128)(2,1)S(1)}, u32[]{:S(2)}, u32[]{:S(2)}) collective-permute-start(bf16[64,1024]{1,0:T(8,128)(2,1)} %e_in.1), channel_id=1, source_target_pairs={{0,4},{1,5},{2,6},{3,7},{4,8},{5,9},{6,10},{7,11},{8,12},{9,13},{1... | collective-permute-start | bytes 393224 | tf_op jit(solution)/shard_map/ppermute | solution.py:48
  8.8 8.4 %collective-permute-start.6 = (bf16[64,1024]{1,0:T(8,128)(2,1)S(1)}, bf16[64,1024]{1,0:T(8,128)(2,1)S(1)}, u32[]{:S(2)}, u32[]{:S(2)}) collective-permute-start(bf16[64,1024]{1,0:T(8,128)(2,1)S(1)} %collective-permute-done.1.refs_1_), channel_id=1, source_target_pairs={{0,4},{1,5},{2,6},{3,7},{4,8},{5,9},{6,10},{7,11},{8,12},{9,13},{1... | collective-permute-start | bytes 393224 | tf_op jit(solution)/shard_map/ppermute | solution.py:48
  9.3 8.0 %collective-permute-start.4 = (bf16[64,1024]{1,0:T(8,128)(2,1)S(1)}, bf16[64,1024]{1,0:T(8,128)(2,1)S(1)}, u32[]{:S(2)}, u32[]{:S(2)}) collective-permute-start(bf16[64,1024]{1,0:T(8,128)(2,1)S(1)} %collective-permute-done.1.refs_1_), channel_id=1, source_target_pairs={{0,8},{1,9},{2,10},{3,11},{4,12},{5,13},{6,14},{7,15},{8,0},{9,1},... | collective-permute-start | bytes 393224 | tf_op jit(solution)/shard_map/ppermute | solution.py:48
  12.6 7.3 %collective-permute-start.2 = (bf16[64,1024]{1,0:T(8,128)(2,1)}, bf16[64,1024]{1,0:T(8,128)(2,1)S(1)}, u32[]{:S(2)}, u32[]{:S(2)}) collective-permute-start(bf16[64,1024]{1,0:T(8,128)(2,1)} %e_in.1), channel_id=1, source_target_pairs={{0,12},{1,13},{2,14},{3,15},{4,0},{5,1},{6,2},{7,3},{8,4},{9,5},{1... | collective-permute-start | bytes 393224 | tf_op jit(solution)/shard_map/ppermute | solution.py:48
  13.3 6.5 %collective-permute-start.3 = (bf16[64,1024]{1,0:T(8,128)(2,1)S(1)}, bf16[64,1024]{1,0:T(8,128)(2,1)S(1)}, u32[]{:S(2)}, u32[]{:S(2)}) collective-permute-start(bf16[64,1024]{1,0:T(8,128)(2,1)S(1)} %collective-permute-done.1.refs_1_), channel_id=1, source_target_pairs={{0,12},{1,13},{2,14},{3,15},{4,0},{5,1},{6,2},{7,3},{8,4},{9,5},{1... | collective-permute-start | bytes 393224 | tf_op jit(solution)/shard_map/ppermute | solution.py:48
  13.7 2.2 %copy-start = (bf16[2048,1024]{1,0:T(8,128)(2,1)S(1)}, bf16[2048,1024]{1,0:T(8,128)(2,1)}, u32[]{:S(2)}) copy-start(bf16[2048,1024]{1,0:T(8,128)(2,1)} %refs_2_.7) | copy-start | bytes 12582916
  15.9 0.9 copy-start.2
  16.8 3.1 %copy-start.1 = (bf16[2048,1024]{1,0:T(8,128)(2,1)S(1)}, bf16[2048,1024]{1,0:T(8,128)(2,1)}, u32[]{:S(2)}) copy-start(bf16[2048,1024]{1,0:T(8,128)(2,1)} %refs_2_.7) | copy-start | bytes 12582916
  17.3 8.7 %collective-permute-start.10 = (bf16[256,1024]{1,0:T(8,128)(2,1)S(1)}, bf16[256,1024]{1,0:T(8,128)(2,1)S(1)}, u32[]{:S(2)}, u32[]{:S(2)}) collective-permute-start(bf16[256,1024]{1,0:T(8,128)(2,1)S(1)} %join.3.refs_1_), channel_id=1, source_target_pairs={{0,3},{1,0},{2,1},{3,2},{4,7},{5,4},{6,5},{7,6},{8,11},{9,8},{10,9... | collective-permute-start | bytes 1572872 | tf_op jit(solution)/shard_map/ppermute | solution.py:48
  19.9 9.6 %collective-permute-start.9 = (bf16[256,1024]{1,0:T(8,128)(2,1)S(1)}, bf16[256,1024]{1,0:T(8,128)(2,1)S(1)}, u32[]{:S(2)}, u32[]{:S(2)}) collective-permute-start(bf16[256,1024]{1,0:T(8,128)(2,1)S(1)} %join.2.refs_0_), channel_id=1, source_target_pairs={{0,1},{1,2},{2,3},{3,0},{4,5},{5,6},{6,7},{7,4},{8,9},{9,10},{10,1... | collective-permute-start | bytes 1572872 | tf_op jit(solution)/shard_map/ppermute | solution.py:48
  23.0 12.2 %collective-permute-start.7 = (bf16[256,1024]{1,0:T(8,128)(2,1)S(1)}, bf16[256,1024]{1,0:T(8,128)(2,1)S(1)}, u32[]{:S(2)}, u32[]{:S(2)}) collective-permute-start(bf16[256,1024]{1,0:T(8,128)(2,1)S(1)} %join.3.refs_1_), channel_id=1, source_target_pairs={{0,1},{1,2},{2,3},{3,0},{4,5},{5,6},{6,7},{7,4},{8,9},{9,10},{10,1... | collective-permute-start | bytes 1572872 | tf_op jit(solution)/shard_map/ppermute | solution.py:48
  23.9 11.3 %collective-permute-start.8 = (bf16[256,1024]{1,0:T(8,128)(2,1)S(1)}, bf16[256,1024]{1,0:T(8,128)(2,1)S(1)}, u32[]{:S(2)}, u32[]{:S(2)}) collective-permute-start(bf16[256,1024]{1,0:T(8,128)(2,1)S(1)} %join.2.refs_0_), channel_id=1, source_target_pairs={{0,3},{1,0},{2,1},{3,2},{4,7},{5,4},{6,5},{7,6},{8,11},{9,8},{10,9... | collective-permute-start | bytes 1572872 | tf_op jit(solution)/shard_map/ppermute | solution.py:48
  29.5 11.2 %collective-permute-start.11 = (bf16[256,1024]{1,0:T(8,128)(2,1)S(1)}, bf16[256,1024]{1,0:T(8,128)(2,1)S(1)}, u32[]{:S(2)}, u32[]{:S(2)}) collective-permute-start(bf16[256,1024]{1,0:T(8,128)(2,1)S(1)} %collective-permute-done.9.refs_0_), channel_id=1, source_target_pairs={{0,1},{1,2},{2,3},{3,0},{4,5},{5,6},{6,7},{7,4},{8,9},{9,10},{10,1... | collective-permute-start | bytes 1572872 | tf_op jit(solution)/shard_map/ppermute | solution.py:48
  29.5 11.2 %collective-permute-start.12 = (bf16[256,1024]{1,0:T(8,128)(2,1)S(1)}, bf16[256,1024]{1,0:T(8,128)(2,1)S(1)}, u32[]{:S(2)}, u32[]{:S(2)}) collective-permute-start(bf16[256,1024]{1,0:T(8,128)(2,1)S(1)} %collective-permute-done.10.refs_1_), channel_id=1, source_target_pairs={{0,3},{1,0},{2,1},{3,2},{4,7},{5,4},{6,5},{7,6},{8,11},{9,8},{10,9... | collective-permute-start | bytes 1572872 | tf_op jit(solution)/shard_map/ppermute | solution.py:48
  63.5 8.6 %collective-permute-start.13 = (bf16[256,1024]{1,0:T(8,128)(2,1)S(1)}, bf16[256,1024]{1,0:T(8,128)(2,1)S(1)}, u32[]{:S(2)}, u32[]{:S(2)}) collective-permute-start(bf16[256,1024]{1,0:T(8,128)(2,1)S(1)} %get-tuple-element.85), channel_id=1, source_target_pairs={{0,32},{32,0},{64,96},{96,64},{1,33},{33,1},{65,97},{97,65},{2,34}... | collective-permute-start | bytes 1572872 | tf_op jit(solution)/shard_map/ppermute | solution.py:359
  72.2 13.4 %collective-permute-start.14 = (bf16[256,1024]{1,0:T(8,128)(2,1)S(1)}, bf16[256,1024]{1,0:T(8,128)(2,1)S(1)}, u32[]{:S(2)}, u32[]{:S(2)}) collective-permute-start(bf16[256,1024]{1,0:T(8,128)(2,1)S(1)} %fold.2), channel_id=1, source_target_pairs={{0,64},{32,96},{64,0},{96,32},{1,65},{33,97},{65,1},{97,33},{2,66}... | collective-permute-start | bytes 1572872 | tf_op jit(solution)/shard_map/ppermute | solution.py:361
  76.8 2.3 %collective-permute-start.16 = (bf16[256,512]{1,0:T(8,128)(2,1)S(1)}, bf16[256,512]{1,0:T(8,128)(2,1)S(1)}, u32[]{:S(2)}, u32[]{:S(2)}) collective-permute-start(bf16[256,512]{1,0:T(8,128)(2,1)S(1)} %get-tuple-element.94), channel_id=1, source_target_pairs={{0,32},{32,0},{64,96},{96,64},{1,33},{33,1},{65,97},{97,65},{2,34}... | collective-permute-start | bytes 786440 | tf_op jit(solution)/shard_map/ppermute | solution.py:364
  77.5 1.6 %collective-permute-start.17 = (bf16[256,512]{1,0:T(8,128)(2,1)S(1)}, bf16[256,512]{1,0:T(8,128)(2,1)S(1)}, u32[]{:S(2)}, u32[]{:S(2)}) collective-permute-start(bf16[256,512]{1,0:T(8,128)(2,1)S(1)} %get-tuple-element.95), channel_id=1, source_target_pairs={{0,32},{32,0},{64,96},{96,64},{1,33},{33,1},{65,97},{97,65},{2,34}... | collective-permute-start | bytes 786440 | tf_op jit(solution)/shard_map/ppermute | solution.py:364
  77.6 1.5 %collective-permute-start.15 = (f32[1,2048]{1,0:T(1,128)S(1)}, f32[1,2048]{1,0:T(1,128)S(1)}, u32[]{:S(2)}, u32[]{:S(2)}) collective-permute-start(f32[1,2048]{1,0:T(1,128)S(1)} %get-tuple-element.92.mass_ref), channel_id=1, source_target_pairs={{0,32},{32,0},{64,96},{96,64},{1,33},{33,1},{65,97},{97,65},{2,34}... | collective-permute-start | bytes 24584 | tf_op jit(solution)/shard_map/ppermute | solution.py:363
  79.2 17.7 %collective-permute-start.18 = (bf16[256,1024]{1,0:T(8,128)(2,1)S(1)}, bf16[256,1024]{1,0:T(8,128)(2,1)S(1)}, u32[]{:S(2)}, u32[]{:S(2)}) collective-permute-start(bf16[256,1024]{1,0:T(8,128)(2,1)S(1)} %get-tuple-element.96), channel_id=1, source_target_pairs={{0,64},{32,96},{64,0},{96,32},{1,65},{33,97},{65,1},{97,33},{2,66}... | collective-permute-start | bytes 1572872 | tf_op jit(solution)/shard_map/ppermute | solution.py:365
  80.4 16.7 %collective-permute-start.20 = (f32[1,2048]{1,0:T(1,128)S(1)}, f32[1,2048]{1,0:T(1,128)S(1)}, u32[]{:S(2)}, u32[]{:S(2)}) collective-permute-start(f32[1,2048]{1,0:T(1,128)S(1)} %get-tuple-element.104.mass_ref), channel_id=1, source_target_pairs={{0,64},{32,96},{64,0},{96,32},{1,65},{33,97},{65,1},{97,33},{2,66}... | collective-permute-start | bytes 24584 | tf_op jit(solution)/shard_map/ppermute | solution.py:370
  85.7 11.4 %collective-permute-start.19 = (bf16[256,2048]{1,0:T(8,128)(2,1)S(1)}, bf16[256,2048]{1,0:T(8,128)(2,1)S(1)}, u32[]{:S(2)}, u32[]{:S(2)}) collective-permute-start(bf16[256,2048]{1,0:T(8,128)(2,1)S(1)} %get-tuple-element.102), channel_id=1, source_target_pairs={{0,32},{32,0},{64,96},{96,64},{1,33},{33,1},{65,97},{97,65},{2,34}... | collective-permute-start | bytes 3145736 | tf_op jit(solution)/shard_map/ppermute | solution.py:369

commit v4 on v3

--- a/solution.py
+++ b/solution.py
@@ -14,6 +14,7 @@
 AXES = ("dp", "cent")
 VMEM = pl.BlockSpec(memory_space=pltpu.VMEM)
 HBM = pl.BlockSpec(memory_space=pltpu.HBM)
+HEAD, REST = (768,), (512, 512, 256)
 LIMIT = 16 * 2**20
 F32, BF16 = jnp.float32, jnp.bfloat16
 
@@ -94,20 +95,13 @@
     return _kernel(_join_body, [_shape(rows, 1024)], parts, "join")[0]
 
 
-def _load_body(e_in, c_ref, e_ref, previous_ref):
-    e_ref[...] = e_in[...]
-    width = previous_ref.shape[0]
-    offset = pl.multiple_of(lax.axis_index("dp") * width, width)
-    previous_ref[...] = jnp.transpose(c_ref[:, pl.ds(offset, width)])
-
-
-def _load(e, c):
-    return _kernel(_load_body, [_shape(*e.shape), _shape(256, 2048)], [e, c], "load")
-
-
 def _soft_body(n, slots, first, *refs):
     e_refs, c_ref, refs = refs[:n], refs[n], refs[n + (1 if first else 2):]
-    p_refs, (peak_ref, part_ref, et_ref, lg) = refs[:n], refs[n:]
+    p_refs, (peak_ref, part_ref, et_ref, *previous, lg) = refs[:n], refs[n:]
+    if first:
+        width = previous[0].shape[0]
+        offset = pl.multiple_of(lax.axis_index("dp") * width, width)
+        previous[0][...] = jnp.transpose(c_ref[:, pl.ds(offset, width)])
     for i in range(n):
         e = e_refs[i][...]
         et_ref[:, slots[i] * 256:(slots[i] + 1) * 256] = jnp.transpose(e)
@@ -145,8 +139,10 @@
     scratch = [pltpu.VMEM((256, 2048), F32)]
     body = functools.partial(_soft_body, n, slots, first)
     inputs, aliases = ([*pieces, c], None) if first else ([*pieces, c, et], {n + 1: n + 2})
+    if first:
+        outs.append(_shape(256, 2048))
     outs = _kernel(body, outs, inputs, "soft", scratch=scratch, aliases=aliases)
-    return outs[:n], outs[n], outs[n + 1], outs[n + 2]
+    return outs[:n], outs[n], outs[n + 1], outs[n + 2], outs[n + 3:]
 
 
 def _pack_body(where, *refs):
@@ -194,84 +190,67 @@
     return [sent, kept]
 
 
-def _assign_part(where, start, width, p_refs, peaks, total_ref, a_ref, placed_ref, sem):
-    copies = []
+def _assign_dot(where, start, width, p_refs, peaks, total_ref, scale_ref, a_ref, rows, store):
     for g in range(16):
         call, i = where[g]
-        place = _place_of(g % 4, g // 4)
-        row = peaks[call][i:i + 1, :] - _swap_far(total_ref[pl.ds(place, 1), :])
-        scale = jnp.transpose(jnp.broadcast_to(jnp.exp2(row), (128, 128)))
-        for j in range(width // 128):
-            value = p_refs[g // 2][g % 2 * 128:(g % 2 + 1) * 128, start + j * 128:start + (j + 1) * 128] * scale
-            a_ref[g * 128:(g + 1) * 128, j * 128:(j + 1) * 128] = value.astype(BF16)
-        for t in range(2):
-            row = pl.multiple_of(((_far() ^ t) * 16 + place) * 64, 64)
-            copy = pltpu.make_async_copy(
-                a_ref.at[pl.ds(g * 128 + t * 64, 64)],
-                placed_ref.at[pl.ds(row, 64), pl.ds(start, width)],
-                sem.at[2 * g + t],
-            )
-            copy.start()
-            copies.append(copy)
-    return copies
-
-
-def _assign_body(where, width, calls, *refs):
+        row = peaks[call][i:i + 1, :] - _swap_far(total_ref[pl.ds(_place_of(g % 4, g // 4), 1), :])
+        scale_ref[g * 128:(g + 1) * 128, :] = jnp.transpose(jnp.broadcast_to(jnp.exp2(row), (128, 128)))
+    for n in range(width // 256):
+        for g in range(16):
+            scale = scale_ref[g * 128:(g + 1) * 128, :]
+            for j in range(2 * n, 2 * n + 2):
+                value = p_refs[g // 2][g % 2 * 128:(g % 2 + 1) * 128, start + j * 128:start + (j + 1) * 128]
+                a_ref[g * 128:(g + 1) * 128, j * 128:(j + 1) * 128] = (value * scale).astype(BF16)
+        cols = slice(n * 256, (n + 1) * 256)
+        store(n, cols, jnp.dot(rows, a_ref[:, cols], preferred_element_type=F32))
+
+
+def _assign_body(where, start, width, parts, calls, *refs):
     p_refs, peaks, refs = refs[:8], refs[8:8 + calls], refs[8 + calls:]
-    total_ref, et_ref, a_ref, placed_ref, sent_ref, kept_ref, mass_ref, sem = refs
-    copies = _assign_part(where, 0, width, p_refs, peaks, total_ref, a_ref, placed_ref, sem)
+    total_ref, et_ref = refs[:2]
+    mass_in = refs[2] if start else None
+    a_ref, *refs = refs[3:] if start else refs[2:]
+    sent_refs, (kept_ref, mass_ref, scale_ref) = refs[:len(parts)], refs[len(parts):]
     rows = jnp.concatenate(_sum_rows(et_ref, False) + [jnp.ones((16, 2048), BF16)], axis=0)
-    for n in range(width // 256):
-        cols = slice(n * 256, (n + 1) * 256)
-        out = jnp.dot(rows, a_ref[:, cols], preferred_element_type=F32)
-        sent_ref[:, cols] = out[:256].astype(BF16)
+
+    def store(n, cols, out):
+        first, part = n * 256, 0
+        while first >= parts[part]:
+            first, part = first - parts[part], part + 1
+        sent_refs[part][:, first:first + 256] = out[:256].astype(BF16)
         kept_ref[:, cols] = out[256:512].astype(BF16)
-        mass_ref[:, cols] = out[512:513]
+        mass_ref[:, start + n * 256:start + (n + 1) * 256] = out[512:513]
+
+    _assign_dot(where, start, width, p_refs, peaks, total_ref, scale_ref, a_ref, rows, store)
+    if start:
+        mass_ref[:, :start] = mass_in[...]
+
+
+def _assign(where, start, parts, ps, peaks, total, et, *mass):
+    width, n = sum(parts), len(parts)
+    outs = _kernel(
+        functools.partial(_assign_body, where, start, width, parts, len(peaks)),
+        [_shape(2048, width)] + [_shape(256, part) for part in parts]
+        + [_shape(256, width), _shape(1, start + width, dtype=F32)],
+        [*ps, *peaks, total, et, *mass], "assign", scratch=[pltpu.VMEM((2048, 128), F32)],
+    )
+    return outs[0], outs[1:1 + n], outs[1 + n], outs[2 + n]
+
+
+def _home_body(et_ref, a0, a1, sent_ref, kept_ref, placed_ref, sem):
+    copies = []
+    for i in range(32):
+        row = pl.multiple_of(((_far() ^ (i % 2)) * 16 + _place_of(i // 2 % 4, i // 8)) * 64, 64)
+        start = 0
+        for n, a_ref in enumerate((a0, a1)):
+            copies.append(pltpu.make_async_copy(
+                a_ref.at[pl.ds(i * 64, 64)],
+                placed_ref.at[pl.ds(row, 64), pl.ds(start, a_ref.shape[1])],
+                sem.at[2 * i + n],
+            ))
+            start += a_ref.shape[1]
     for copy in copies:
-        copy.wait()
-
-
-def _assign(where, width, ps, peaks, total, et):
-    return _kernel(
-        functools.partial(_assign_body, where, width, len(peaks)),
-        [_shape(2048, width), _shape(2048, 2048), _shape(256, width), _shape(256, width), _shape(1, width, dtype=F32)],
-        [*ps, *peaks, total, et], "assign", scratch=[pltpu.SemaphoreType.DMA((32,))], hbm_out=(1,),
-    )
-
-
-def _rest_body(where, width, calls, n, *refs):
-    p_refs, peaks, refs = refs[:8], refs[8:8 + calls], refs[8 + calls:]
-    total_ref, et_ref, m0, _, placed_ref, a_ref = refs[:6]
-    sent_refs, (kept_ref, mass_ref, sem) = refs[6:6 + n], refs[6 + n:]
-    left = 2048 - width
-    copies = _assign_part(where, width, left, p_refs, peaks, total_ref, a_ref, placed_ref, sem)
-    rows = jnp.concatenate(_sum_rows(et_ref, False) + [jnp.ones((16, 2048), BF16)], axis=0)
-    for j in range(left // 256):
-        cols = slice(j * 256, (j + 1) * 256)
-        out = jnp.dot(rows, a_ref[:, cols], preferred_element_type=F32)
-        step = left // n
-        sent_refs[j * 256 // step][:, j * 256 % step:j * 256 % step + 256] = out[:256].astype(BF16)
-        kept_ref[:, cols] = out[256:512].astype(BF16)
-        mass_ref[:, width + j * 256:width + (j + 1) * 256] = out[512:513]
-    mass_ref[:, :width] = m0[...]
-    for copy in copies:
-        copy.wait()
-
-
-def _rest(where, width, n, ps, peaks, total, et, m0, placed):
-    left = 2048 - width
-    inputs = [*ps, *peaks, total, et, m0, placed]
-    outs = _kernel(
-        functools.partial(_rest_body, where, width, len(peaks), n),
-        [_shape(2048, 2048), _shape(2048, left)] + [_shape(256, left // n)] * n
-        + [_shape(256, left), _shape(1, 2048, dtype=F32)],
-        inputs, "rest", scratch=[pltpu.SemaphoreType.DMA((32,))],
-        hbm_in=(len(inputs) - 1,), hbm_out=(0,), aliases={len(inputs) - 1: 0},
-    )
-    return outs[0], outs[1], outs[2:2 + n], outs[2 + n], outs[3 + n]
-
-
-def _home_body(et_ref, a0, a1, sent_ref, kept_ref):
+        copy.start()
     rows = jnp.concatenate(_sum_rows(et_ref, True), axis=0)
     start = 0
     for a_ref in (a0, a1):
@@ -281,10 +260,15 @@
             sent_ref[:, cols] = out[:256].astype(BF16)
             kept_ref[:, cols] = out[256:].astype(BF16)
         start += a_ref.shape[1]
+    for copy in copies:
+        copy.wait()
 
 
 def _home(*inputs):
-    return _kernel(_home_body, [_shape(256, 2048), _shape(256, 2048)], inputs, "home", flops=1)
+    return _kernel(
+        _home_body, [_shape(256, 2048), _shape(256, 2048), _shape(2048, 2048)], inputs, "home",
+        scratch=[pltpu.SemaphoreType.DMA((64,))], hbm_out=(2,), flops=1,
+    )
 
 
 def _fold_body(kept_ref, *refs):
@@ -315,9 +299,9 @@
     for ref in (in0, in1):
         cols = slice(start, start + ref.shape[1])
         start += ref.shape[1]
+        inverse = 1.0 / (total_ref[:, cols] + PRIOR)
         sums = home_ref[:, cols].astype(F32) + sent_ref[:, cols].astype(F32) + ref[...].astype(F32)
-        sums = sums + PRIOR * previous_ref[:, cols].astype(F32)
-        out_ref[:, cols] = (sums / (total_ref[:, cols] + PRIOR)).astype(BF16)
+        out_ref[:, cols] = ((sums + PRIOR * previous_ref[:, cols].astype(F32)) * inverse).astype(BF16)
 
 
 def _final(*inputs):
@@ -325,29 +309,26 @@
 
 
 def on_device(embeddings, centroids):
-    width = 1024
-    other = _send(embeddings, FAR)
+    other = _copy(_send(embeddings, FAR))
     own = [embeddings] + [_send(embeddings, _first(-k)) for k in (1, 2, 3)]
     other = [other] + [_send(other, _first(-k)) for k in (1, 2, 3)]
     c = centroids
-    e, previous = _load(embeddings, centroids)
-    own[2], e = lax.optimization_barrier((own[2], e))
-    own[0] = e
+    own, other = lax.optimization_barrier((own, other))
     e0a = _join(own[0], other[0], own[1], other[1])
     e0b = _join(own[2], other[2], own[3], other[3])
+    e3b, e1a = _send(e0b, _second(1)), _send(e0a, _second(-1))
     e3a, e1b = _send(e0a, _second(1)), _send(e0b, _second(-1))
     calls = [_soft([e0a, e0b], (0, 1), c, None)]
-    e0a, e0b, et = lax.optimization_barrier((e0a, e0b, calls[0][3]))
-    e3b, e1a = _send(e0b, _second(1)), _send(e0a, _second(-1))
-    e3a, e1b, et = lax.optimization_barrier((e3a, e1b, et))
-    e2a, e2b = _send(e3a, _second(1)), _send(e1b, _second(-1))
-    calls.append(_soft([e3a, e1b], (6, 3), c, et))
-    calls.append(_soft([e3b, e1a], (7, 2), c, calls[1][3]))
+    previous, et = calls[0][4][0], calls[0][3]
+    e3b, e1a, et = lax.optimization_barrier((e3b, e1a, et))
+    e2b, e2a = _send(e3b, _second(1)), _send(e1a, _second(-1))
+    calls.append(_soft([e3b, e1a], (7, 2), c, et))
+    calls.append(_soft([e3a, e1b], (6, 3), c, calls[1][3]))
     calls.append(_soft([e2a, e2b], (4, 5), c, calls[2][3]))
     et = calls[3][3]
 
     probs, where = [None] * 8, [None] * 16
-    for n, (call, slots) in enumerate(zip(calls, ((0, 1), (6, 3), (7, 2), (4, 5)))):
+    for n, (call, slots) in enumerate(zip(calls, ((0, 1), (7, 2), (6, 3), (4, 5)))):
         for i, slot in enumerate(slots):
             probs[slot] = call[0][i]
             where[2 * slot], where[2 * slot + 1] = (n, 2 * i), (n, 2 * i + 1)
@@ -355,16 +336,16 @@
     parts = _pack([call[2] for call in calls], where)
     total = _merge(lax.all_to_all(parts, "cent", 0, 0).reshape(32, 16, 128))
 
-    a0, placed, sent, kept, m0 = _assign(where, width, probs, peaks, total, et)
-    out0 = _fold(kept, lax.ppermute(sent, "dp", CORE))
+    a0, sent, kept, mass = _assign(where, 0, HEAD, probs, peaks, total, et)
+    out0 = _fold(kept, *(lax.ppermute(part, "dp", CORE) for part in sent))
     out0, total = lax.optimization_barrier((out0, total))
     in0 = lax.ppermute(out0, "dp", NEAR)
-    placed, a1, sent, kept, mass = _rest(where, width, 2, probs, peaks, total, et, m0, placed)
+    a1, sent, kept, mass = _assign(where, sum(HEAD), REST, probs, peaks, total, et, mass)
     other_mass = lax.ppermute(mass, "dp", CORE)
     out1, mass = _fold_mass(mass, other_mass, kept, *(lax.ppermute(part, "dp", CORE) for part in sent))
     in1 = _copy(lax.ppermute(out1, "dp", NEAR))
     a0, out1 = lax.optimization_barrier((a0, out1))
-    sent, kept = _home(et, a0, a1)
+    sent, kept, placed = _home(et, a0, a1)
     in0, sent = lax.optimization_barrier((_copy(in0), sent))
     sent = lax.ppermute(sent, "dp", CORE)
     result, mass = _final(in0, in1, kept, sent, previous, mass, lax.ppermute(mass, "dp", NEAR))

time: 99.5 us -> 96.1 us (0.966)
  starting transfers between devices: 33.8 us -> 30.2 us
  local copies, waits for them, and re-layouts: 3.09 us -> 0.01 us
  waiting for transfers between devices: 18.3 us -> 21.1 us
  Pallas kernels: 27.7 us -> 29.3 us
  blocking collectives: 15.7 us -> 14.7 us
    ppermute x13, waiting for transfers between devices: 6.1 us -> 11.4 us  [_send(): return lax.ppermute(value, AXES, pairs)]
    unnamed x6 -> x4, local copies, waits for them, and re-layouts: 3.09 us -> 0.01 us
    ppermute x1, waiting for transfers between devices: 9.11 us -> 7.08 us  [on_device(): in1 = _copy(lax.ppermute(out1, 'dp', NEAR))]
    pallas_call x17, Pallas kernels: 27.7 us -> 29.3 us  [_kernel(): pl.pallas_call(body, out_shape=outs, in_specs=[HBM if i in hbm_in else VM...]
    ppermute x13, starting transfers between devices: 21.2 us -> 19.6 us  [_send(): return lax.ppermute(value, AXES, pairs)]
    ppermute x1, starting transfers between devices: 2.08 us -> 1.01 us  [on_device(): sent = lax.ppermute(sent, 'dp', CORE)]
    ppermute x1, starting transfers between devices: 7.04 us -> 6.03 us  [on_device(): out0 = _fold(kept, *(lax.ppermute(part, 'dp', CORE) for part in sent))]
  transfers between devices with their start and end apart: 21 -> 22, of which waited for: 8 -> 12; matrix products, arithmetic and copies ran while one was open for 0% -> 0% of each run, Pallas kernels for 18% -> 22%
where the time goes in v4:
time: 96.1 us; the launch traced here: 96 us
  starting transfers between devices  30.2 us (31%)
  Pallas kernels  29.3 us (30%)
  waiting for transfers between devices  21.1 us (22%)
  blocking collectives  14.7 us (15%)
    pallas_call x17, Pallas kernels, _kernel(): pl.pallas_call(body, out_shape=outs, in_specs=[HBM if i in hbm_in else VM...  29.3 us
    ppermute x13, starting transfers between devices, _send(): return lax.ppermute(value, AXES, pairs)  19.6 us
    all_to_all x1, blocking collectives, on_device(): total = _merge(lax.all_to_all(parts, 'cent', 0, 0).reshape(32, 16, 128))  14.7 us
    ppermute x13, waiting for transfers between devices, _send(): return lax.ppermute(value, AXES, pairs)  11.4 us
    ppermute x1, waiting for transfers between devices, on_device(): in1 = _copy(lax.ppermute(out1, 'dp', NEAR))  7.08 us
    ppermute x1, starting transfers between devices, on_device(): out0 = _fold(kept, *(lax.ppermute(part, 'dp', CORE) for part in sent))  6.03 us
  transfers between devices with their start and end apart: 22, of which 12 were waited for; matrix products, arithmetic and copies ran while one was open for 0% of the time, Pallas kernels for 22%

profile of v4, /device:TPU:1, one launch (start us, length us, event | category | flops | bytes accessed | tf_op | source)
XLA Modules:
  0.0 96.0 jit_solution(3763038854552567948)
XLA Ops:
  0.6 3.8 %collective-permute-start.3 = (bf16[64,1024]{1,0:T(8,128)(2,1)}, bf16[64,1024]{1,0:T(8,128)(2,1)S(1)}, u32[]{:S(2)}, u32[]{:S(2)}) collective-permute-start(bf16[64,1024]{1,0:T(8,128)(2,1)} %refs_0_), channel_id=1, source_target_pairs={{0,16},{1,17},{2,18},{3,19},{4,20},{5,21},{6,22},{7,23},{8,24},{9,... | collective-permute-start | bytes 393224 | tf_op jit(solution)/shard_map/ppermute | solution.py:49
  4.5 1.6 %collective-permute-start.2 = (bf16[64,1024]{1,0:T(8,128)(2,1)}, bf16[64,1024]{1,0:T(8,128)(2,1)S(1)}, u32[]{:S(2)}, u32[]{:S(2)}) collective-permute-start(bf16[64,1024]{1,0:T(8,128)(2,1)} %refs_0_), channel_id=1, source_target_pairs={{0,4},{1,5},{2,6},{3,7},{4,8},{5,9},{6,10},{7,11},{8,12},{9,13},{1... | collective-permute-start | bytes 393224 | tf_op jit(solution)/shard_map/ppermute | solution.py:49
  6.1 3.3 %collective-permute-start.1 = (bf16[64,1024]{1,0:T(8,128)(2,1)}, bf16[64,1024]{1,0:T(8,128)(2,1)S(1)}, u32[]{:S(2)}, u32[]{:S(2)}) collective-permute-start(bf16[64,1024]{1,0:T(8,128)(2,1)} %refs_0_), channel_id=1, source_target_pairs={{0,8},{1,9},{2,10},{3,11},{4,12},{5,13},{6,14},{7,15},{8,0},{9,1},... | collective-permute-start | bytes 393224 | tf_op jit(solution)/shard_map/ppermute | solution.py:49
  9.4 0.7 collective-permute-start
  10.2 0.8 collective-permute-start.6
  11.0 1.7 %collective-permute-start.5 = (bf16[64,1024]{1,0:T(8,128)(2,1)S(1)}, bf16[64,1024]{1,0:T(8,128)(2,1)S(1)}, u32[]{:S(2)}, u32[]{:S(2)}) collective-permute-start(bf16[64,1024]{1,0:T(8,128)(2,1)S(1)} %copy.14.refs_1_), channel_id=1, source_target_pairs={{0,8},{1,9},{2,10},{3,11},{4,12},{5,13},{6,14},{7,15},{8,0},{9,1},... | collective-permute-start | bytes 393224 | tf_op jit(solution)/shard_map/ppermute | solution.py:49
  12.7 0.8 collective-permute-start.4
  13.7 3.2 %collective-permute-done.6.refs_3_ = bf16[64,1024]{1,0:T(8,128)(2,1)S(1)} collective-permute-done((bf16[64,1024]{1,0:T(8,128)(2,1)S(1)}, bf16[64,1024]{1,0:T(8,128)(2,1)S(1)}, u32[]{:S(2)}, u32[]{:S(2)}) %collective-permute-start.6) | collective-permute-done | bytes 131104 | tf_op jit(solution)/shard_map/ppermute | solution.py:49
  17.0 0.6 collective-permute-done.4.refs_3_
  17.6 2.5 %collective-permute-start.8 = (bf16[256,1024]{1,0:T(8,128)(2,1)S(1)}, bf16[256,1024]{1,0:T(8,128)(2,1)S(1)}, u32[]{:S(2)}, u32[]{:S(2)}) collective-permute-start(bf16[256,1024]{1,0:T(8,128)(2,1)S(1)} %join.3.refs_0_), channel_id=1, source_target_pairs={{0,3},{1,0},{2,1},{3,2},{4,7},{5,4},{6,5},{7,6},{8,11},{9,8},{10,9... | collective-permute-start | bytes 1572872 | tf_op jit(solution)/shard_map/ppermute | solution.py:49
  20.4 2.6 %collective-permute-start.12 = (bf16[256,1024]{1,0:T(8,128)(2,1)S(1)}, bf16[256,1024]{1,0:T(8,128)(2,1)S(1)}, u32[]{:S(2)}, u32[]{:S(2)}) collective-permute-start(bf16[256,1024]{1,0:T(8,128)(2,1)S(1)} %join.2.refs_1_), channel_id=1, source_target_pairs={{0,3},{1,0},{2,1},{3,2},{4,7},{5,4},{6,5},{7,6},{8,11},{9,8},{10,9... | collective-permute-start | bytes 1572872 | tf_op jit(solution)/shard_map/ppermute | solution.py:49
  23.0 3.1 %soft.4 = (f32[256,2048]{1,0:T(8,128)S(1)}, f32[256,2048]{1,0:T(8,128)S(1)}, f32[4,128]{1,0:T(4,128)S(1)}, f32[4,128]{1,0:T(4,128)S(1)}, bf16[1024,2048]{1,0:T(8,128)(2,1)S(1)}, /*index=5*/bf16[256,2048]{1,0:T(8,128)(2,1)S(1)}) custom-call(bf16[256,1024]{1,0:T(8,128)(2,1)S(1)} %join.3.refs_0_, bf16[256,1024]{1,0:T(8,128)(2,1)S(1)} %join.2.refs_1_, ...), custom_call_target="tpu_custom_call" | custom-call | tf_op jit(solution)/shard_map/soft/pallas_call | solution.py:57
  26.2 3.5 %collective-permute-done.7.refs_0_ = bf16[256,1024]{1,0:T(8,128)(2,1)S(1)} collective-permute-done((bf16[256,1024]{1,0:T(8,128)(2,1)S(1)}, bf16[256,1024]{1,0:T(8,128)(2,1)S(1)}, u32[]{:S(2)}, u32[]{:S(2)}) %collective-permute-start.7) | collective-permute-done | bytes 524320 | tf_op jit(solution)/shard_map/ppermute | solution.py:49
  29.8 1.5 %collective-permute-start.10 = (bf16[256,1024]{1,0:T(8,128)(2,1)S(1)}, bf16[256,1024]{1,0:T(8,128)(2,1)S(1)}, u32[]{:S(2)}, u32[]{:S(2)}) collective-permute-start(bf16[256,1024]{1,0:T(8,128)(2,1)S(1)} %collective-permute-done.7.refs_0_), channel_id=1, source_target_pairs={{0,1},{1,2},{2,3},{3,0},{4,5},{5,6},{6,7},{7,4},{8,9},{9,10},{10,1... | collective-permute-start | bytes 1572872 | tf_op jit(solution)/shard_map/ppermute | solution.py:49
  31.2 3.1 %soft.5 = (f32[256,2048]{1,0:T(8,128)S(1)}, f32[256,2048]{1,0:T(8,128)S(1)}, f32[4,128]{1,0:T(4,128)S(1)}, f32[4,128]{1,0:T(4,128)S(1)}, bf16[1024,2048]{1,0:T(8,128)(2,1)S(1)}) custom-call(bf16[256,1024]{1,0:T(8,128)(2,1)S(1)} %collective-permute-done.7.refs_0_, ...), custom_call_target="tpu_custom_call", output_to_operand_aliasing={{4}: (3, {})} | custom-call | tf_op jit(solution)/shard_map/soft/pallas_call | solution.py:57
  34.3 1.1 %collective-permute-done.11.refs_0_ = bf16[256,1024]{1,0:T(8,128)(2,1)S(1)} collective-permute-done((bf16[256,1024]{1,0:T(8,128)(2,1)S(1)}, bf16[256,1024]{1,0:T(8,128)(2,1)S(1)}, u32[]{:S(2)}, u32[]{:S(2)}) %collective-permute-start.11) | collective-permute-done | bytes 524320 | tf_op jit(solution)/shard_map/ppermute | solution.py:49
  35.4 3.1 %soft.6 = (f32[256,2048]{1,0:T(8,128)S(1)}, f32[256,2048]{1,0:T(8,128)S(1)}, f32[4,128]{1,0:T(4,128)S(1)}, f32[4,128]{1,0:T(4,128)S(1)}, bf16[1024,2048]{1,0:T(8,128)(2,1)S(1)}) custom-call(bf16[256,1024]{1,0:T(8,128)(2,1)S(1)} %collective-permute-done.11.refs_0_, ...), custom_call_target="tpu_custom_call", output_to_operand_aliasing={{4}: (3, {})} | custom-call | tf_op jit(solution)/shard_map/soft/pallas_call | solution.py:57
  38.4 2.6 %collective-permute-done.10.refs_1_ = bf16[256,1024]{1,0:T(8,128)(2,1)S(1)} collective-permute-done((bf16[256,1024]{1,0:T(8,128)(2,1)S(1)}, bf16[256,1024]{1,0:T(8,128)(2,1)S(1)}, u32[]{:S(2)}, u32[]{:S(2)}) %collective-permute-start.10) | collective-permute-done | bytes 524320 | tf_op jit(solution)/shard_map/ppermute | solution.py:49
  41.0 3.1 %soft.7 = (f32[256,2048]{1,0:T(8,128)S(1)}, f32[256,2048]{1,0:T(8,128)S(1)}, f32[4,128]{1,0:T(4,128)S(1)}, f32[4,128]{1,0:T(4,128)S(1)}, bf16[1024,2048]{1,0:T(8,128)(2,1)S(1)}) custom-call(bf16[256,1024]{1,0:T(8,128)(2,1)S(1)} %collective-permute-done.9.refs_0_, ...), custom_call_target="tpu_custom_call", output_to_operand_aliasing={{4}: (3, {})} | custom-call | tf_op jit(solution)/shard_map/soft/pallas_call | solution.py:57
  44.2 14.7 %all_to_all.5.in_ref = f32[32,16,128]{2,1,0:T(8,128)S(1)} all-to-all(f32[32,16,128]{2,1,0:T(8,128)S(1)} %pack.1), channel_id=1, replica_groups=mesh['dp'=4,'cent'=32] {'cent'}, dimensions={0} | all-to-all | bytes 524288 | tf_op jit(solution)/shard_map/all_to_all | solution.py:337
  59.0 2.5 %assign.2 = (bf16[2048,768]{1,0:T(8,128)(2,1)S(1)}, bf16[256,768]{1,0:T(8,128)(2,1)S(1)}, bf16[256,768]{1,0:T(8,128)(2,1)S(1)}, f32[1,768]{1,0:T(1,128)S(1)}) custom-call(f32[256,2048]{1,0:T(8,128)S(1)} %get-tuple-element.72.refs_0_, f32[256,2048]{1,0:T(8,128)S(1)} %get-tuple-element.73.refs_1_, f32[256,2048]{1,0:T(8,128)S(1)} %get-tuple-element.74.refs_2_, ...), custom_call_target="tpu_custom_call" | custom-call | tf_op jit(solution)/shard_map/assign/pallas_call | solution.py:57
  61.4 6.0 %collective-permute-start.13 = (bf16[256,768]{1,0:T(8,128)(2,1)S(1)}, bf16[256,768]{1,0:T(8,128)(2,1)S(1)}, u32[]{:S(2)}, u32[]{:S(2)}) collective-permute-start(bf16[256,768]{1,0:T(8,128)(2,1)S(1)} %get-tuple-element.90), channel_id=1, source_target_pairs={{0,32},{32,0},{64,96},{96,64},{1,33},{33,1},{65,97},{97,65},{2,34}... | collective-permute-start | bytes 1179656 | tf_op jit(solution)/shard_map/ppermute | solution.py:340
  67.5 1.3 %collective-permute-done.13.refs_0_ = bf16[256,768]{1,0:T(8,128)(2,1)S(1)} collective-permute-done((bf16[256,768]{1,0:T(8,128)(2,1)S(1)}, bf16[256,768]{1,0:T(8,128)(2,1)S(1)}, u32[]{:S(2)}, u32[]{:S(2)}) %collective-permute-start.13) | collective-permute-done | bytes 393248 | tf_op jit(solution)/shard_map/ppermute | solution.py:340
  68.9 0.7 collective-permute-start.18
  69.6 3.9 %assign.3 = (bf16[2048,1280]{1,0:T(8,128)(2,1)S(1)}, bf16[256,512]{1,0:T(8,128)(2,1)S(1)}, bf16[256,512]{1,0:T(8,128)(2,1)S(1)}, bf16[256,256]{1,0:T(8,128)(2,1)...) custom-call(f32[256,2048]{1,0:T(8,128)S(1)} %get-tuple-element.72.refs_0_, ...), custom_call_target="tpu_custom_call" | custom-call | tf_op jit(solution)/shard_map/assign/pallas_call | solution.py:57
  73.5 0.7 collective-permute-start.15
  74.9 1.1 %collective-permute-done.14.other_ref = f32[1,2048]{1,0:T(1,128)S(1)} collective-permute-done((f32[1,2048]{1,0:T(1,128)S(1)}, f32[1,2048]{1,0:T(1,128)S(1)}, u32[]{:S(2)}, u32[]{:S(2)}) %collective-permute-start.14) | collective-permute-done | bytes 8224 | tf_op jit(solution)/shard_map/ppermute | solution.py:344
  76.2 1.1 %collective-permute-start.19 = (bf16[256,1280]{1,0:T(8,128)(2,1)S(1)}, bf16[256,1280]{1,0:T(8,128)(2,1)S(1)}, u32[]{:S(2)}, u32[]{:S(2)}) collective-permute-start(bf16[256,1280]{1,0:T(8,128)(2,1)S(1)} %get-tuple-element.98), channel_id=1, source_target_pairs={{0,64},{32,96},{64,0},{96,32},{1,65},{33,97},{65,1},{97,33},{2,66}... | collective-permute-start | bytes 1966088 | tf_op jit(solution)/shard_map/ppermute | solution.py:346
  77.7 7.7 %home.1 = (bf16[256,2048]{1,0:T(8,128)(2,1)S(1)}, bf16[256,2048]{1,0:T(8,128)(2,1)S(1)}, bf16[2048,2048]{1,0:T(8,128)(2,1)}) custom-call(bf16[1024,2048]{1,0:T(8,128)(2,1)S(1)} %get-tuple-element.71.refs_13_.et_ref, bf16[2048,768]{1,0:T(8,128)(2,1)S(1)} %get-tuple-element.99.a0, bf16[2048,1280]{1,0:T(8,128)(2,1)S(1)} %get-tuple-element.100.a1), custom_call_target="tpu_custom_call" | custom-call | flops 1 | tf_op jit(solution)/shard_map/home/pallas_call | solution.py:57
  85.5 1.0 %collective-permute-start.20 = (bf16[256,2048]{1,0:T(8,128)(2,1)S(1)}, bf16[256,2048]{1,0:T(8,128)(2,1)S(1)}, u32[]{:S(2)}, u32[]{:S(2)}) collective-permute-start(bf16[256,2048]{1,0:T(8,128)(2,1)S(1)} %get-tuple-element.106), channel_id=1, source_target_pairs={{0,32},{32,0},{64,96},{96,64},{1,33},{33,1},{65,97},{97,65},{2,34}... | collective-permute-start | bytes 3145736 | tf_op jit(solution)/shard_map/ppermute | solution.py:350
  86.5 7.1 %collective-permute-done.19.in_ref = bf16[256,1280]{1,0:T(8,128)(2,1)S(1)} collective-permute-done((bf16[256,1280]{1,0:T(8,128)(2,1)S(1)}, bf16[256,1280]{1,0:T(8,128)(2,1)S(1)}, u32[]{:S(2)}, u32[]{:S(2)}) %collective-permute-start.19) | collective-permute-done | bytes 655392 | tf_op jit(solution)/shard_map/ppermute | solution.py:346
  93.8 2.2 %final.1 = (bf16[256,2048]{1,0:T(8,128)(2,1)}, f32[1,2048]{1,0:T(1,128)}) custom-call(bf16[256,768]{1,0:T(8,128)(2,1)S(1)} %copy.15.in0, bf16[256,1280]{1,0:T(8,128)(2,1)S(1)} %copy.16.in1, bf16[256,2048]{1,0:T(8,128)(2,1)S(1)} %get-tuple-element.105.home_ref, bf16[256,2048]{1,0:T(8,128)(2,1)S(1)} %collective-permute-done.20.sent_ref, ...), custom_call_target="tpu_custom_call" | custom-call | tf_op jit(solution)/shard_map/final/pallas_call | solution.py:57
  (34 shorter events, 2.5 us)
Async XLA Ops:
  0.6 16.9 %copy-start.1 = (bf16[64,1024]{1,0:T(8,128)(2,1)S(1)}, bf16[64,1024]{1,0:T(8,128)(2,1)}, u32[]{:S(2)}) copy-start(bf16[64,1024]{1,0:T(8,128)(2,1)} %refs_0_) | copy-start | bytes 393220
  0.6 9.5 %collective-permute-start.3 = (bf16[64,1024]{1,0:T(8,128)(2,1)}, bf16[64,1024]{1,0:T(8,128)(2,1)S(1)}, u32[]{:S(2)}, u32[]{:S(2)}) collective-permute-start(bf16[64,1024]{1,0:T(8,128)(2,1)} %refs_0_), channel_id=1, source_target_pairs={{0,16},{1,17},{2,18},{3,19},{4,20},{5,21},{6,22},{7,23},{8,24},{9,... | collective-permute-start | bytes 393224 | tf_op jit(solution)/shard_map/ppermute | solution.py:49
  4.5 8.2 %collective-permute-start.2 = (bf16[64,1024]{1,0:T(8,128)(2,1)}, bf16[64,1024]{1,0:T(8,128)(2,1)S(1)}, u32[]{:S(2)}, u32[]{:S(2)}) collective-permute-start(bf16[64,1024]{1,0:T(8,128)(2,1)} %refs_0_), channel_id=1, source_target_pairs={{0,4},{1,5},{2,6},{3,7},{4,8},{5,9},{6,10},{7,11},{8,12},{9,13},{1... | collective-permute-start | bytes 393224 | tf_op jit(solution)/shard_map/ppermute | solution.py:49
  6.1 7.6 %collective-permute-start.1 = (bf16[64,1024]{1,0:T(8,128)(2,1)}, bf16[64,1024]{1,0:T(8,128)(2,1)S(1)}, u32[]{:S(2)}, u32[]{:S(2)}) collective-permute-start(bf16[64,1024]{1,0:T(8,128)(2,1)} %refs_0_), channel_id=1, source_target_pairs={{0,8},{1,9},{2,10},{3,11},{4,12},{5,13},{6,14},{7,15},{8,0},{9,1},... | collective-permute-start | bytes 393224 | tf_op jit(solution)/shard_map/ppermute | solution.py:49
  9.4 4.3 %collective-permute-start = (bf16[64,1024]{1,0:T(8,128)(2,1)}, bf16[64,1024]{1,0:T(8,128)(2,1)S(1)}, u32[]{:S(2)}, u32[]{:S(2)}) collective-permute-start(bf16[64,1024]{1,0:T(8,128)(2,1)} %refs_0_), channel_id=1, source_target_pairs={{0,12},{1,13},{2,14},{3,15},{4,0},{5,1},{6,2},{7,3},{8,4},{9,5},{1... | collective-permute-start | bytes 393224 | tf_op jit(solution)/shard_map/ppermute | solution.py:49
  10.1 12.9 %copy-start = (bf16[2048,1024]{1,0:T(8,128)(2,1)S(1)}, bf16[2048,1024]{1,0:T(8,128)(2,1)}, u32[]{:S(2)}) copy-start(bf16[2048,1024]{1,0:T(8,128)(2,1)} %refs_2_.7) | copy-start | bytes 12582916
  10.2 6.8 %collective-permute-start.6 = (bf16[64,1024]{1,0:T(8,128)(2,1)S(1)}, bf16[64,1024]{1,0:T(8,128)(2,1)S(1)}, u32[]{:S(2)}, u32[]{:S(2)}) collective-permute-start(bf16[64,1024]{1,0:T(8,128)(2,1)S(1)} %copy.14.refs_1_), channel_id=1, source_target_pairs={{0,4},{1,5},{2,6},{3,7},{4,8},{5,9},{6,10},{7,11},{8,12},{9,13},{1... | collective-permute-start | bytes 393224 | tf_op jit(solution)/shard_map/ppermute | solution.py:49
  11.0 6.0 %collective-permute-start.5 = (bf16[64,1024]{1,0:T(8,128)(2,1)S(1)}, bf16[64,1024]{1,0:T(8,128)(2,1)S(1)}, u32[]{:S(2)}, u32[]{:S(2)}) collective-permute-start(bf16[64,1024]{1,0:T(8,128)(2,1)S(1)} %copy.14.refs_1_), channel_id=1, source_target_pairs={{0,8},{1,9},{2,10},{3,11},{4,12},{5,13},{6,14},{7,15},{8,0},{9,1},... | collective-permute-start | bytes 393224 | tf_op jit(solution)/shard_map/ppermute | solution.py:49
  12.7 4.9 %collective-permute-start.4 = (bf16[64,1024]{1,0:T(8,128)(2,1)S(1)}, bf16[64,1024]{1,0:T(8,128)(2,1)S(1)}, u32[]{:S(2)}, u32[]{:S(2)}) collective-permute-start(bf16[64,1024]{1,0:T(8,128)(2,1)S(1)} %copy.14.refs_1_), channel_id=1, source_target_pairs={{0,12},{1,13},{2,14},{3,15},{4,0},{5,1},{6,2},{7,3},{8,4},{9,5},{1... | collective-permute-start | bytes 393224 | tf_op jit(solution)/shard_map/ppermute | solution.py:49
  17.6 8.7 %collective-permute-start.8 = (bf16[256,1024]{1,0:T(8,128)(2,1)S(1)}, bf16[256,1024]{1,0:T(8,128)(2,1)S(1)}, u32[]{:S(2)}, u32[]{:S(2)}) collective-permute-start(bf16[256,1024]{1,0:T(8,128)(2,1)S(1)} %join.3.refs_0_), channel_id=1, source_target_pairs={{0,3},{1,0},{2,1},{3,2},{4,7},{5,4},{6,5},{7,6},{8,11},{9,8},{10,9... | collective-permute-start | bytes 1572872 | tf_op jit(solution)/shard_map/ppermute | solution.py:49
  20.2 9.6 %collective-permute-start.7 = (bf16[256,1024]{1,0:T(8,128)(2,1)S(1)}, bf16[256,1024]{1,0:T(8,128)(2,1)S(1)}, u32[]{:S(2)}, u32[]{:S(2)}) collective-permute-start(bf16[256,1024]{1,0:T(8,128)(2,1)S(1)} %join.2.refs_1_), channel_id=1, source_target_pairs={{0,1},{1,2},{2,3},{3,0},{4,5},{5,6},{6,7},{7,4},{8,9},{9,10},{10,1... | collective-permute-start | bytes 1572872 | tf_op jit(solution)/shard_map/ppermute | solution.py:49
  20.2 15.1 %collective-permute-start.11 = (bf16[256,1024]{1,0:T(8,128)(2,1)S(1)}, bf16[256,1024]{1,0:T(8,128)(2,1)S(1)}, u32[]{:S(2)}, u32[]{:S(2)}) collective-permute-start(bf16[256,1024]{1,0:T(8,128)(2,1)S(1)} %join.3.refs_0_), channel_id=1, source_target_pairs={{0,1},{1,2},{2,3},{3,0},{4,5},{5,6},{6,7},{7,4},{8,9},{9,10},{10,1... | collective-permute-start | bytes 1572872 | tf_op jit(solution)/shard_map/ppermute | solution.py:49
  20.4 15.0 %collective-permute-start.12 = (bf16[256,1024]{1,0:T(8,128)(2,1)S(1)}, bf16[256,1024]{1,0:T(8,128)(2,1)S(1)}, u32[]{:S(2)}, u32[]{:S(2)}) collective-permute-start(bf16[256,1024]{1,0:T(8,128)(2,1)S(1)} %join.2.refs_1_), channel_id=1, source_target_pairs={{0,3},{1,0},{2,1},{3,2},{4,7},{5,4},{6,5},{7,6},{8,11},{9,8},{10,9... | collective-permute-start | bytes 1572872 | tf_op jit(solution)/shard_map/ppermute | solution.py:49
  29.8 8.7 %collective-permute-start.9 = (bf16[256,1024]{1,0:T(8,128)(2,1)S(1)}, bf16[256,1024]{1,0:T(8,128)(2,1)S(1)}, u32[]{:S(2)}, u32[]{:S(2)}) collective-permute-start(bf16[256,1024]{1,0:T(8,128)(2,1)S(1)} %collective-permute-done.8.refs_1_), channel_id=1, source_target_pairs={{0,3},{1,0},{2,1},{3,2},{4,7},{5,4},{6,5},{7,6},{8,11},{9,8},{10,9... | collective-permute-start | bytes 1572872 | tf_op jit(solution)/shard_map/ppermute | solution.py:49
  29.8 11.2 %collective-permute-start.10 = (bf16[256,1024]{1,0:T(8,128)(2,1)S(1)}, bf16[256,1024]{1,0:T(8,128)(2,1)S(1)}, u32[]{:S(2)}, u32[]{:S(2)}) collective-permute-start(bf16[256,1024]{1,0:T(8,128)(2,1)S(1)} %collective-permute-done.7.refs_0_), channel_id=1, source_target_pairs={{0,1},{1,2},{2,3},{3,0},{4,5},{5,6},{6,7},{7,4},{8,9},{9,10},{10,1... | collective-permute-start | bytes 1572872 | tf_op jit(solution)/shard_map/ppermute | solution.py:49
  61.4 7.4 %collective-permute-start.13 = (bf16[256,768]{1,0:T(8,128)(2,1)S(1)}, bf16[256,768]{1,0:T(8,128)(2,1)S(1)}, u32[]{:S(2)}, u32[]{:S(2)}) collective-permute-start(bf16[256,768]{1,0:T(8,128)(2,1)S(1)} %get-tuple-element.90), channel_id=1, source_target_pairs={{0,32},{32,0},{64,96},{96,64},{1,33},{33,1},{65,97},{97,65},{2,34}... | collective-permute-start | bytes 1179656 | tf_op jit(solution)/shard_map/ppermute | solution.py:340
  68.9 16.5 %collective-permute-start.18 = (bf16[256,768]{1,0:T(8,128)(2,1)S(1)}, bf16[256,768]{1,0:T(8,128)(2,1)S(1)}, u32[]{:S(2)}, u32[]{:S(2)}) collective-permute-start(bf16[256,768]{1,0:T(8,128)(2,1)S(1)} %fold.2), channel_id=1, source_target_pairs={{0,64},{32,96},{64,0},{96,32},{1,65},{33,97},{65,1},{97,33},{2,66}... | collective-permute-start | bytes 1179656 | tf_op jit(solution)/shard_map/ppermute | solution.py:342
  73.5 2.5 %collective-permute-start.15 = (bf16[256,512]{1,0:T(8,128)(2,1)S(1)}, bf16[256,512]{1,0:T(8,128)(2,1)S(1)}, u32[]{:S(2)}, u32[]{:S(2)}) collective-permute-start(bf16[256,512]{1,0:T(8,128)(2,1)S(1)} %get-tuple-element.95), channel_id=1, source_target_pairs={{0,32},{32,0},{64,96},{96,64},{1,33},{33,1},{65,97},{97,65},{2,34}... | collective-permute-start | bytes 786440 | tf_op jit(solution)/shard_map/ppermute | solution.py:345
  74.2 1.7 %collective-permute-start.16 = (bf16[256,512]{1,0:T(8,128)(2,1)S(1)}, bf16[256,512]{1,0:T(8,128)(2,1)S(1)}, u32[]{:S(2)}, u32[]{:S(2)}) collective-permute-start(bf16[256,512]{1,0:T(8,128)(2,1)S(1)} %get-tuple-element.96), channel_id=1, source_target_pairs={{0,32},{32,0},{64,96},{96,64},{1,33},{33,1},{65,97},{97,65},{2,34}... | collective-permute-start | bytes 786440 | tf_op jit(solution)/shard_map/ppermute | solution.py:345
  74.3 1.6 %collective-permute-start.17 = (bf16[256,256]{1,0:T(8,128)(2,1)S(1)}, bf16[256,256]{1,0:T(8,128)(2,1)S(1)}, u32[]{:S(2)}, u32[]{:S(2)}) collective-permute-start(bf16[256,256]{1,0:T(8,128)(2,1)S(1)} %get-tuple-element.97), channel_id=1, source_target_pairs={{0,32},{32,0},{64,96},{96,64},{1,33},{33,1},{65,97},{97,65},{2,34}... | collective-permute-start | bytes 393224 | tf_op jit(solution)/shard_map/ppermute | solution.py:345
  74.8 1.2 %collective-permute-start.14 = (f32[1,2048]{1,0:T(1,128)S(1)}, f32[1,2048]{1,0:T(1,128)S(1)}, u32[]{:S(2)}, u32[]{:S(2)}) collective-permute-start(f32[1,2048]{1,0:T(1,128)S(1)} %get-tuple-element.93.mass_ref), channel_id=1, source_target_pairs={{0,32},{32,0},{64,96},{96,64},{1,33},{33,1},{65,97},{97,65},{2,34}... | collective-permute-start | bytes 24584 | tf_op jit(solution)/shard_map/ppermute | solution.py:344
  76.2 17.4 %collective-permute-start.19 = (bf16[256,1280]{1,0:T(8,128)(2,1)S(1)}, bf16[256,1280]{1,0:T(8,128)(2,1)S(1)}, u32[]{:S(2)}, u32[]{:S(2)}) collective-permute-start(bf16[256,1280]{1,0:T(8,128)(2,1)S(1)} %get-tuple-element.98), channel_id=1, source_target_pairs={{0,64},{32,96},{64,0},{96,32},{1,65},{33,97},{65,1},{97,33},{2,66}... | collective-permute-start | bytes 1966088 | tf_op jit(solution)/shard_map/ppermute | solution.py:346
  77.3 16.4 %collective-permute-start.21 = (f32[1,2048]{1,0:T(1,128)S(1)}, f32[1,2048]{1,0:T(1,128)S(1)}, u32[]{:S(2)}, u32[]{:S(2)}) collective-permute-start(f32[1,2048]{1,0:T(1,128)S(1)} %get-tuple-element.108.mass_ref), channel_id=1, source_target_pairs={{0,64},{32,96},{64,0},{96,32},{1,65},{33,97},{65,1},{97,33},{2,66}... | collective-permute-start | bytes 24584 | tf_op jit(solution)/shard_map/ppermute | solution.py:351
  85.5 8.3 %collective-permute-start.20 = (bf16[256,2048]{1,0:T(8,128)(2,1)S(1)}, bf16[256,2048]{1,0:T(8,128)(2,1)S(1)}, u32[]{:S(2)}, u32[]{:S(2)}) collective-permute-start(bf16[256,2048]{1,0:T(8,128)(2,1)S(1)} %get-tuple-element.106), channel_id=1, source_target_pairs={{0,32},{32,0},{64,96},{96,64},{1,33},{33,1},{65,97},{97,65},{2,34}... | collective-permute-start | bytes 3145736 | tf_op jit(solution)/shard_map/ppermute | solution.py:350

commit v5 on v4

--- a/solution.py
+++ b/solution.py
@@ -25,9 +25,9 @@
         for cent in range(32):
             core = dp & 1
             far, x, z = cent >> 4, (cent >> 2) & 3, cent & 3
-            first, second = (x, z) if core == 0 else (z, x)
+            first, second = (z, x) if core == 0 else (x, z)
             far, first, second = move(far, first, second)
-            x, z = (first, second) if core == 0 else (second, first)
+            x, z = (second, first) if core == 0 else (first, second)
             pairs.append((dp * 32 + cent, dp * 32 + (far % 2) * 16 + (x % 4) * 4 + z % 4))
     return pairs
 
@@ -70,9 +70,9 @@
 def _place_of(a, b):
     core, cent = lax.axis_index("dp") & 1, lax.axis_index("cent")
     x, z = (cent >> 2) & 3, cent & 3
-    first = (jnp.where(core == 0, x, z) + a) & 3
-    second = (jnp.where(core == 0, z, x) + b) & 3
-    return jnp.where(core == 0, first, second) * 4 + jnp.where(core == 0, second, first)
+    first = (jnp.where(core == 0, z, x) + a) & 3
+    second = (jnp.where(core == 0, x, z) + b) & 3
+    return jnp.where(core == 0, second, first) * 4 + jnp.where(core == 0, first, second)
 
 
 def _far():
@@ -293,19 +293,45 @@
     return _kernel(_fold_mass_body, outs, [mass, other, kept, *sent], "fold", flops=1)
 
 
-def _final_body(in0, in1, home_ref, sent_ref, previous_ref, mass_ref, other_ref, out_ref, total_ref):
-    total_ref[...] = mass_ref[...] + other_ref[...]
-    start = 0
-    for ref in (in0, in1):
-        cols = slice(start, start + ref.shape[1])
-        start += ref.shape[1]
-        inverse = 1.0 / (total_ref[:, cols] + PRIOR)
-        sums = home_ref[:, cols].astype(F32) + sent_ref[:, cols].astype(F32) + ref[...].astype(F32)
-        out_ref[:, cols] = ((sums + PRIOR * previous_ref[:, cols].astype(F32)) * inverse).astype(BF16)
+def _base_body(in_ref, home_ref, previous_ref, out_ref):
+    width = in_ref.shape[1]
+    for n in range(0, 2048, 256):
+        cols = slice(n, n + 256)
+        value = home_ref[:, cols].astype(F32) + PRIOR * previous_ref[:, cols].astype(F32)
+        if n < width:
+            value = value + in_ref[:, cols].astype(F32)
+        out_ref[:, cols] = value
+
+
+def _base(*inputs):
+    return _kernel(_base_body, [_shape(256, 2048, dtype=F32)], inputs, "base", flops=2**36)[0]
+
+
+def _final_body(base_ref, in_ref, sent_ref, mass_ref, other_ref, out_ref, total_ref, result, sem):
+    total = mass_ref[...] + other_ref[...]
+    total_ref[...] = total
+    inverse = 1.0 / (total + PRIOR)
+    start = 2048 - in_ref.shape[1]
+    copies = []
+    for n in range(4):
+        rows = slice(n * 64, (n + 1) * 64)
+        head = base_ref[rows, :start] + sent_ref[rows, :start].astype(F32)
+        result[rows, :start] = (head * inverse[:, :start]).astype(BF16)
+        rest = base_ref[rows, start:] + sent_ref[rows, start:].astype(F32) + in_ref[rows, :].astype(F32)
+        result[rows, start:] = (rest * inverse[:, start:]).astype(BF16)
+        copies.append(pltpu.make_async_copy(
+            result.at[pl.ds(n * 64, 64)], out_ref.at[pl.ds(n * 64, 64)], sem.at[n]
+        ))
+        copies[-1].start()
+    for copy in copies:
+        copy.wait()
 
 
 def _final(*inputs):
-    return _kernel(_final_body, [_shape(256, 2048), _shape(1, 2048, dtype=F32)], inputs, "final")
+    return _kernel(
+        _final_body, [_shape(256, 2048), _shape(1, 2048, dtype=F32)], inputs, "final",
+        scratch=[pltpu.VMEM((256, 2048), BF16), pltpu.SemaphoreType.DMA((4,))], hbm_out=(0,),
+    )
 
 
 def on_device(embeddings, centroids):
@@ -346,9 +372,9 @@
     in1 = _copy(lax.ppermute(out1, "dp", NEAR))
     a0, out1 = lax.optimization_barrier((a0, out1))
     sent, kept, placed = _home(et, a0, a1)
-    in0, sent = lax.optimization_barrier((_copy(in0), sent))
+    base, sent = lax.optimization_barrier((_base(in0, kept, previous), sent))
     sent = lax.ppermute(sent, "dp", CORE)
-    result, mass = _final(in0, in1, kept, sent, previous, mass, lax.ppermute(mass, "dp", NEAR))
+    result, mass = _final(base, in1, sent, mass, lax.ppermute(mass, "dp", NEAR))
     return placed, mass.reshape(2048), result
 
 

time: 96.1 us -> 95.3 us (level)
  transfers between devices with their start and end apart: 22 -> 22, of which waited for: 12 -> 10; matrix products, arithmetic and copies ran while one was open for 0% -> 0% of each run, Pallas kernels for 22% -> 23%
where the time goes in v5:
time: 95.3 us; the launch traced here: 95.2 us
  starting transfers between devices  29.7 us (31%)
  Pallas kernels  29 us (30%)
  waiting for transfers between devices  20.8 us (22%)
  blocking collectives  14.7 us (15%)
    pallas_call x17, Pallas kernels, _kernel(): pl.pallas_call(body, out_shape=outs, in_specs=[HBM if i in hbm_in else VM...  29 us
    ppermute x13, starting transfers between devices, _send(): return lax.ppermute(value, AXES, pairs)  20 us
    all_to_all x1, blocking collectives, on_device(): total = _merge(lax.all_to_all(parts, 'cent', 0, 0).reshape(32, 16, 128))  14.7 us
    ppermute x13, waiting for transfers between devices, _send(): return lax.ppermute(value, AXES, pairs)  11.4 us
    ppermute x1, waiting for transfers between devices, on_device(): in1 = _copy(lax.ppermute(out1, 'dp', NEAR))  6.78 us
    ppermute x1, starting transfers between devices, on_device(): out0 = _fold(kept, *(lax.ppermute(part, 'dp', CORE) for part in sent))  5.16 us
  transfers between devices with their start and end apart: 22, of which 10 were waited for; matrix products, arithmetic and copies ran while one was open for 0% of the time, Pallas kernels for 23%

profile of v5, /device:TPU:1, one launch (start us, length us, event | category | flops | bytes accessed | tf_op | source)
XLA Modules:
  0.0 95.2 jit_solution(419212279628107502)
XLA Ops:
  0.6 3.8 %collective-permute-start.3 = (bf16[64,1024]{1,0:T(8,128)(2,1)}, bf16[64,1024]{1,0:T(8,128)(2,1)S(1)}, u32[]{:S(2)}, u32[]{:S(2)}) collective-permute-start(bf16[64,1024]{1,0:T(8,128)(2,1)} %refs_0_), channel_id=1, source_target_pairs={{0,16},{1,17},{2,18},{3,19},{4,20},{5,21},{6,22},{7,23},{8,24},{9,... | collective-permute-start | bytes 393224 | tf_op jit(solution)/shard_map/ppermute | solution.py:49
  4.5 1.2 %collective-permute-start.2 = (bf16[64,1024]{1,0:T(8,128)(2,1)}, bf16[64,1024]{1,0:T(8,128)(2,1)S(1)}, u32[]{:S(2)}, u32[]{:S(2)}) collective-permute-start(bf16[64,1024]{1,0:T(8,128)(2,1)} %refs_0_), channel_id=1, source_target_pairs={{0,1},{1,2},{2,3},{3,0},{4,5},{5,6},{6,7},{7,4},{8,9},{9,10},{10,1... | collective-permute-start | bytes 393224 | tf_op jit(solution)/shard_map/ppermute | solution.py:49
  5.7 2.5 %collective-permute-start.1 = (bf16[64,1024]{1,0:T(8,128)(2,1)}, bf16[64,1024]{1,0:T(8,128)(2,1)S(1)}, u32[]{:S(2)}, u32[]{:S(2)}) collective-permute-start(bf16[64,1024]{1,0:T(8,128)(2,1)} %refs_0_), channel_id=1, source_target_pairs={{0,2},{1,3},{2,0},{3,1},{4,6},{5,7},{6,4},{7,5},{8,10},{9,11},{10,... | collective-permute-start | bytes 393224 | tf_op jit(solution)/shard_map/ppermute | solution.py:49
  8.1 1.2 %collective-permute-start = (bf16[64,1024]{1,0:T(8,128)(2,1)}, bf16[64,1024]{1,0:T(8,128)(2,1)S(1)}, u32[]{:S(2)}, u32[]{:S(2)}) collective-permute-start(bf16[64,1024]{1,0:T(8,128)(2,1)} %refs_0_), channel_id=1, source_target_pairs={{0,3},{1,0},{2,1},{3,2},{4,7},{5,4},{6,5},{7,6},{8,11},{9,8},{10,9... | collective-permute-start | bytes 393224 | tf_op jit(solution)/shard_map/ppermute | solution.py:49
  9.7 1.7 %collective-permute-start.5 = (bf16[64,1024]{1,0:T(8,128)(2,1)S(1)}, bf16[64,1024]{1,0:T(8,128)(2,1)S(1)}, u32[]{:S(2)}, u32[]{:S(2)}) collective-permute-start(bf16[64,1024]{1,0:T(8,128)(2,1)S(1)} %copy.13.refs_1_), channel_id=1, source_target_pairs={{0,2},{1,3},{2,0},{3,1},{4,6},{5,7},{6,4},{7,5},{8,10},{9,11},{10,... | collective-permute-start | bytes 393224 | tf_op jit(solution)/shard_map/ppermute | solution.py:49
  11.4 1.2 %collective-permute-start.4 = (bf16[64,1024]{1,0:T(8,128)(2,1)S(1)}, bf16[64,1024]{1,0:T(8,128)(2,1)S(1)}, u32[]{:S(2)}, u32[]{:S(2)}) collective-permute-start(bf16[64,1024]{1,0:T(8,128)(2,1)S(1)} %copy.13.refs_1_), channel_id=1, source_target_pairs={{0,3},{1,0},{2,1},{3,2},{4,7},{5,4},{6,5},{7,6},{8,11},{9,8},{10,9... | collective-permute-start | bytes 393224 | tf_op jit(solution)/shard_map/ppermute | solution.py:49
  12.5 3.3 %collective-permute-done.6.refs_3_ = bf16[64,1024]{1,0:T(8,128)(2,1)S(1)} collective-permute-done((bf16[64,1024]{1,0:T(8,128)(2,1)S(1)}, bf16[64,1024]{1,0:T(8,128)(2,1)S(1)}, u32[]{:S(2)}, u32[]{:S(2)}) %collective-permute-start.6) | collective-permute-done | bytes 131104 | tf_op jit(solution)/shard_map/ppermute | solution.py:49
  15.8 0.9 collective-permute-done.4.refs_3_
  16.7 3.8 %collective-permute-start.8 = (bf16[256,1024]{1,0:T(8,128)(2,1)S(1)}, bf16[256,1024]{1,0:T(8,128)(2,1)S(1)}, u32[]{:S(2)}, u32[]{:S(2)}) collective-permute-start(bf16[256,1024]{1,0:T(8,128)(2,1)S(1)} %join.3.refs_0_), channel_id=1, source_target_pairs={{0,12},{1,13},{2,14},{3,15},{4,0},{5,1},{6,2},{7,3},{8,4},{9,5},{1... | collective-permute-start | bytes 1572872 | tf_op jit(solution)/shard_map/ppermute | solution.py:49
  20.7 2.7 %collective-permute-start.12 = (bf16[256,1024]{1,0:T(8,128)(2,1)S(1)}, bf16[256,1024]{1,0:T(8,128)(2,1)S(1)}, u32[]{:S(2)}, u32[]{:S(2)}) collective-permute-start(bf16[256,1024]{1,0:T(8,128)(2,1)S(1)} %join.2.refs_1_), channel_id=1, source_target_pairs={{0,12},{1,13},{2,14},{3,15},{4,0},{5,1},{6,2},{7,3},{8,4},{9,5},{1... | collective-permute-start | bytes 1572872 | tf_op jit(solution)/shard_map/ppermute | solution.py:49
  23.4 3.1 %soft.4 = (f32[256,2048]{1,0:T(8,128)S(1)}, f32[256,2048]{1,0:T(8,128)S(1)}, f32[4,128]{1,0:T(4,128)S(1)}, f32[4,128]{1,0:T(4,128)S(1)}, bf16[1024,2048]{1,0:T(8,128)(2,1)S(1)}, /*index=5*/bf16[256,2048]{1,0:T(8,128)(2,1)S(1)}) custom-call(bf16[256,1024]{1,0:T(8,128)(2,1)S(1)} %join.3.refs_0_, bf16[256,1024]{1,0:T(8,128)(2,1)S(1)} %join.2.refs_1_, ...), custom_call_target="tpu_custom_call" | custom-call | tf_op jit(solution)/shard_map/soft/pallas_call | solution.py:57
  26.7 3.5 %collective-permute-done.7.refs_0_ = bf16[256,1024]{1,0:T(8,128)(2,1)S(1)} collective-permute-done((bf16[256,1024]{1,0:T(8,128)(2,1)S(1)}, bf16[256,1024]{1,0:T(8,128)(2,1)S(1)}, u32[]{:S(2)}, u32[]{:S(2)}) %collective-permute-start.7) | collective-permute-done | bytes 524320 | tf_op jit(solution)/shard_map/ppermute | solution.py:49
  30.2 1.5 %collective-permute-start.10 = (bf16[256,1024]{1,0:T(8,128)(2,1)S(1)}, bf16[256,1024]{1,0:T(8,128)(2,1)S(1)}, u32[]{:S(2)}, u32[]{:S(2)}) collective-permute-start(bf16[256,1024]{1,0:T(8,128)(2,1)S(1)} %collective-permute-done.7.refs_0_), channel_id=1, source_target_pairs={{0,4},{1,5},{2,6},{3,7},{4,8},{5,9},{6,10},{7,11},{8,12},{9,13},{1... | collective-permute-start | bytes 1572872 | tf_op jit(solution)/shard_map/ppermute | solution.py:49
  31.7 3.1 %soft.5 = (f32[256,2048]{1,0:T(8,128)S(1)}, f32[256,2048]{1,0:T(8,128)S(1)}, f32[4,128]{1,0:T(4,128)S(1)}, f32[4,128]{1,0:T(4,128)S(1)}, bf16[1024,2048]{1,0:T(8,128)(2,1)S(1)}) custom-call(bf16[256,1024]{1,0:T(8,128)(2,1)S(1)} %collective-permute-done.7.refs_0_, ...), custom_call_target="tpu_custom_call", output_to_operand_aliasing={{4}: (3, {})} | custom-call | tf_op jit(solution)/shard_map/soft/pallas_call | solution.py:57
  34.7 1.1 %collective-permute-done.11.refs_0_ = bf16[256,1024]{1,0:T(8,128)(2,1)S(1)} collective-permute-done((bf16[256,1024]{1,0:T(8,128)(2,1)S(1)}, bf16[256,1024]{1,0:T(8,128)(2,1)S(1)}, u32[]{:S(2)}, u32[]{:S(2)}) %collective-permute-start.11) | collective-permute-done | bytes 524320 | tf_op jit(solution)/shard_map/ppermute | solution.py:49
  35.8 3.1 %soft.6 = (f32[256,2048]{1,0:T(8,128)S(1)}, f32[256,2048]{1,0:T(8,128)S(1)}, f32[4,128]{1,0:T(4,128)S(1)}, f32[4,128]{1,0:T(4,128)S(1)}, bf16[1024,2048]{1,0:T(8,128)(2,1)S(1)}) custom-call(bf16[256,1024]{1,0:T(8,128)(2,1)S(1)} %collective-permute-done.11.refs_0_, ...), custom_call_target="tpu_custom_call", output_to_operand_aliasing={{4}: (3, {})} | custom-call | tf_op jit(solution)/shard_map/soft/pallas_call | solution.py:57
  38.9 2.5 %collective-permute-done.10.refs_1_ = bf16[256,1024]{1,0:T(8,128)(2,1)S(1)} collective-permute-done((bf16[256,1024]{1,0:T(8,128)(2,1)S(1)}, bf16[256,1024]{1,0:T(8,128)(2,1)S(1)}, u32[]{:S(2)}, u32[]{:S(2)}) %collective-permute-start.10) | collective-permute-done | bytes 524320 | tf_op jit(solution)/shard_map/ppermute | solution.py:49
  41.4 3.1 %soft.7 = (f32[256,2048]{1,0:T(8,128)S(1)}, f32[256,2048]{1,0:T(8,128)S(1)}, f32[4,128]{1,0:T(4,128)S(1)}, f32[4,128]{1,0:T(4,128)S(1)}, bf16[1024,2048]{1,0:T(8,128)(2,1)S(1)}) custom-call(bf16[256,1024]{1,0:T(8,128)(2,1)S(1)} %collective-permute-done.9.refs_0_, ...), custom_call_target="tpu_custom_call", output_to_operand_aliasing={{4}: (3, {})} | custom-call | tf_op jit(solution)/shard_map/soft/pallas_call | solution.py:57
  44.6 14.7 %all_to_all.5.in_ref = f32[32,16,128]{2,1,0:T(8,128)S(1)} all-to-all(f32[32,16,128]{2,1,0:T(8,128)S(1)} %pack.1), channel_id=1, replica_groups=mesh['dp'=4,'cent'=32] {'cent'}, dimensions={0} | all-to-all | bytes 524288 | tf_op jit(solution)/shard_map/all_to_all | solution.py:363
  59.4 2.5 %assign.2 = (bf16[2048,768]{1,0:T(8,128)(2,1)S(1)}, bf16[256,768]{1,0:T(8,128)(2,1)S(1)}, bf16[256,768]{1,0:T(8,128)(2,1)S(1)}, f32[1,768]{1,0:T(1,128)S(1)}) custom-call(f32[256,2048]{1,0:T(8,128)S(1)} %get-tuple-element.72.refs_0_, f32[256,2048]{1,0:T(8,128)S(1)} %get-tuple-element.73.refs_1_, f32[256,2048]{1,0:T(8,128)S(1)} %get-tuple-element.74.refs_2_, ...), custom_call_target="tpu_custom_call" | custom-call | tf_op jit(solution)/shard_map/assign/pallas_call | solution.py:57
  61.9 5.2 %collective-permute-start.13 = (bf16[256,768]{1,0:T(8,128)(2,1)S(1)}, bf16[256,768]{1,0:T(8,128)(2,1)S(1)}, u32[]{:S(2)}, u32[]{:S(2)}) collective-permute-start(bf16[256,768]{1,0:T(8,128)(2,1)S(1)} %get-tuple-element.90), channel_id=1, source_target_pairs={{0,32},{32,0},{64,96},{96,64},{1,33},{33,1},{65,97},{97,65},{2,34}... | collective-permute-start | bytes 1179656 | tf_op jit(solution)/shard_map/ppermute | solution.py:366
  67.0 1.3 %collective-permute-done.13.refs_0_ = bf16[256,768]{1,0:T(8,128)(2,1)S(1)} collective-permute-done((bf16[256,768]{1,0:T(8,128)(2,1)S(1)}, bf16[256,768]{1,0:T(8,128)(2,1)S(1)}, u32[]{:S(2)}, u32[]{:S(2)}) %collective-permute-start.13) | collective-permute-done | bytes 393248 | tf_op jit(solution)/shard_map/ppermute | solution.py:366
  68.5 0.7 collective-permute-start.18
  69.2 3.9 %assign.3 = (bf16[2048,1280]{1,0:T(8,128)(2,1)S(1)}, bf16[256,512]{1,0:T(8,128)(2,1)S(1)}, bf16[256,512]{1,0:T(8,128)(2,1)S(1)}, bf16[256,256]{1,0:T(8,128)(2,1)...) custom-call(f32[256,2048]{1,0:T(8,128)S(1)} %get-tuple-element.72.refs_0_, ...), custom_call_target="tpu_custom_call" | custom-call | tf_op jit(solution)/shard_map/assign/pallas_call | solution.py:57
  73.1 0.7 collective-permute-start.15
  73.9 0.4 collective-permute-start.17
  74.4 1.1 %collective-permute-done.14.other_ref = f32[1,2048]{1,0:T(1,128)S(1)} collective-permute-done((f32[1,2048]{1,0:T(1,128)S(1)}, f32[1,2048]{1,0:T(1,128)S(1)}, u32[]{:S(2)}, u32[]{:S(2)}) %collective-permute-start.14) | collective-permute-done | bytes 8224 | tf_op jit(solution)/shard_map/ppermute | solution.py:370
  75.7 1.1 %collective-permute-start.19 = (bf16[256,1280]{1,0:T(8,128)(2,1)S(1)}, bf16[256,1280]{1,0:T(8,128)(2,1)S(1)}, u32[]{:S(2)}, u32[]{:S(2)}) collective-permute-start(bf16[256,1280]{1,0:T(8,128)(2,1)S(1)} %get-tuple-element.98), channel_id=1, source_target_pairs={{0,64},{32,96},{64,0},{96,32},{1,65},{33,97},{65,1},{97,33},{2,66}... | collective-permute-start | bytes 1966088 | tf_op jit(solution)/shard_map/ppermute | solution.py:372
  77.3 7.7 %home.1 = (bf16[256,2048]{1,0:T(8,128)(2,1)S(1)}, bf16[256,2048]{1,0:T(8,128)(2,1)S(1)}, bf16[2048,2048]{1,0:T(8,128)(2,1)}) custom-call(bf16[1024,2048]{1,0:T(8,128)(2,1)S(1)} %get-tuple-element.71.refs_13_.et_ref, bf16[2048,768]{1,0:T(8,128)(2,1)S(1)} %get-tuple-element.99.a0, bf16[2048,1280]{1,0:T(8,128)(2,1)S(1)} %get-tuple-element.100.a1), custom_call_target="tpu_custom_call" | custom-call | flops 1 | tf_op jit(solution)/shard_map/home/pallas_call | solution.py:57
  85.3 1.0 %collective-permute-start.20 = (bf16[256,2048]{1,0:T(8,128)(2,1)S(1)}, bf16[256,2048]{1,0:T(8,128)(2,1)S(1)}, u32[]{:S(2)}, u32[]{:S(2)}) collective-permute-start(bf16[256,2048]{1,0:T(8,128)(2,1)S(1)} %get-tuple-element.107), channel_id=1, source_target_pairs={{0,32},{32,0},{64,96},{96,64},{1,33},{33,1},{65,97},{97,65},{2,34}... | collective-permute-start | bytes 3145736 | tf_op jit(solution)/shard_map/ppermute | solution.py:376
  86.4 6.8 %collective-permute-done.19.in_ref = bf16[256,1280]{1,0:T(8,128)(2,1)S(1)} collective-permute-done((bf16[256,1280]{1,0:T(8,128)(2,1)S(1)}, bf16[256,1280]{1,0:T(8,128)(2,1)S(1)}, u32[]{:S(2)}, u32[]{:S(2)}) %collective-permute-start.19) | collective-permute-done | bytes 655392 | tf_op jit(solution)/shard_map/ppermute | solution.py:372
  93.3 1.7 %final.1 = (bf16[256,2048]{1,0:T(8,128)(2,1)}, f32[1,2048]{1,0:T(1,128)}) custom-call(f32[256,2048]{1,0:T(8,128)S(1)} %base.1.base_ref, bf16[256,1280]{1,0:T(8,128)(2,1)S(1)} %copy.14.in_ref, bf16[256,2048]{1,0:T(8,128)(2,1)S(1)} %collective-permute-done.20.sent_ref, f32[1,2048]{1,0:T(1,128)S(1)} %get-tuple-element.108.mass_ref, ...), custom_call_target="tpu_custom_call" | custom-call | tf_op jit(solution)/shard_map/final/pallas_call | solution.py:57
  (34 shorter events, 2.3 us)
Async XLA Ops:
  0.6 16.0 %copy-start.1 = (bf16[64,1024]{1,0:T(8,128)(2,1)S(1)}, bf16[64,1024]{1,0:T(8,128)(2,1)}, u32[]{:S(2)}) copy-start(bf16[64,1024]{1,0:T(8,128)(2,1)} %refs_0_) | copy-start | bytes 393220
  0.6 8.6 %collective-permute-start.3 = (bf16[64,1024]{1,0:T(8,128)(2,1)}, bf16[64,1024]{1,0:T(8,128)(2,1)S(1)}, u32[]{:S(2)}, u32[]{:S(2)}) collective-permute-start(bf16[64,1024]{1,0:T(8,128)(2,1)} %refs_0_), channel_id=1, source_target_pairs={{0,16},{1,17},{2,18},{3,19},{4,20},{5,21},{6,22},{7,23},{8,24},{9,... | collective-permute-start | bytes 393224 | tf_op jit(solution)/shard_map/ppermute | solution.py:49
  4.5 6.9 %collective-permute-start.2 = (bf16[64,1024]{1,0:T(8,128)(2,1)}, bf16[64,1024]{1,0:T(8,128)(2,1)S(1)}, u32[]{:S(2)}, u32[]{:S(2)}) collective-permute-start(bf16[64,1024]{1,0:T(8,128)(2,1)} %refs_0_), channel_id=1, source_target_pairs={{0,1},{1,2},{2,3},{3,0},{4,5},{5,6},{6,7},{7,4},{8,9},{9,10},{10,1... | collective-permute-start | bytes 393224 | tf_op jit(solution)/shard_map/ppermute | solution.py:49
  5.7 6.9 %collective-permute-start.1 = (bf16[64,1024]{1,0:T(8,128)(2,1)}, bf16[64,1024]{1,0:T(8,128)(2,1)S(1)}, u32[]{:S(2)}, u32[]{:S(2)}) collective-permute-start(bf16[64,1024]{1,0:T(8,128)(2,1)} %refs_0_), channel_id=1, source_target_pairs={{0,2},{1,3},{2,0},{3,1},{4,6},{5,7},{6,4},{7,5},{8,10},{9,11},{10,... | collective-permute-start | bytes 393224 | tf_op jit(solution)/shard_map/ppermute | solution.py:49
  8.1 4.4 %collective-permute-start = (bf16[64,1024]{1,0:T(8,128)(2,1)}, bf16[64,1024]{1,0:T(8,128)(2,1)S(1)}, u32[]{:S(2)}, u32[]{:S(2)}) collective-permute-start(bf16[64,1024]{1,0:T(8,128)(2,1)} %refs_0_), channel_id=1, source_target_pairs={{0,3},{1,0},{2,1},{3,2},{4,7},{5,4},{6,5},{7,6},{8,11},{9,8},{10,9... | collective-permute-start | bytes 393224 | tf_op jit(solution)/shard_map/ppermute | solution.py:49
  9.3 14.1 %copy-start = (bf16[2048,1024]{1,0:T(8,128)(2,1)S(1)}, bf16[2048,1024]{1,0:T(8,128)(2,1)}, u32[]{:S(2)}) copy-start(bf16[2048,1024]{1,0:T(8,128)(2,1)} %refs_2_.7) | copy-start | bytes 12582916
  9.3 6.5 %collective-permute-start.6 = (bf16[64,1024]{1,0:T(8,128)(2,1)S(1)}, bf16[64,1024]{1,0:T(8,128)(2,1)S(1)}, u32[]{:S(2)}, u32[]{:S(2)}) collective-permute-start(bf16[64,1024]{1,0:T(8,128)(2,1)S(1)} %copy.13.refs_1_), channel_id=1, source_target_pairs={{0,1},{1,2},{2,3},{3,0},{4,5},{5,6},{6,7},{7,4},{8,9},{9,10},{10,1... | collective-permute-start | bytes 393224 | tf_op jit(solution)/shard_map/ppermute | solution.py:49
  9.7 6.1 %collective-permute-start.5 = (bf16[64,1024]{1,0:T(8,128)(2,1)S(1)}, bf16[64,1024]{1,0:T(8,128)(2,1)S(1)}, u32[]{:S(2)}, u32[]{:S(2)}) collective-permute-start(bf16[64,1024]{1,0:T(8,128)(2,1)S(1)} %copy.13.refs_1_), channel_id=1, source_target_pairs={{0,2},{1,3},{2,0},{3,1},{4,6},{5,7},{6,4},{7,5},{8,10},{9,11},{10,... | collective-permute-start | bytes 393224 | tf_op jit(solution)/shard_map/ppermute | solution.py:49
  11.4 5.3 %collective-permute-start.4 = (bf16[64,1024]{1,0:T(8,128)(2,1)S(1)}, bf16[64,1024]{1,0:T(8,128)(2,1)S(1)}, u32[]{:S(2)}, u32[]{:S(2)}) collective-permute-start(bf16[64,1024]{1,0:T(8,128)(2,1)S(1)} %copy.13.refs_1_), channel_id=1, source_target_pairs={{0,3},{1,0},{2,1},{3,2},{4,7},{5,4},{6,5},{7,6},{8,11},{9,8},{10,9... | collective-permute-start | bytes 393224 | tf_op jit(solution)/shard_map/ppermute | solution.py:49
  16.7 10.0 %collective-permute-start.8 = (bf16[256,1024]{1,0:T(8,128)(2,1)S(1)}, bf16[256,1024]{1,0:T(8,128)(2,1)S(1)}, u32[]{:S(2)}, u32[]{:S(2)}) collective-permute-start(bf16[256,1024]{1,0:T(8,128)(2,1)S(1)} %join.3.refs_0_), channel_id=1, source_target_pairs={{0,12},{1,13},{2,14},{3,15},{4,0},{5,1},{6,2},{7,3},{8,4},{9,5},{1... | collective-permute-start | bytes 1572872 | tf_op jit(solution)/shard_map/ppermute | solution.py:49
  20.6 9.6 %collective-permute-start.7 = (bf16[256,1024]{1,0:T(8,128)(2,1)S(1)}, bf16[256,1024]{1,0:T(8,128)(2,1)S(1)}, u32[]{:S(2)}, u32[]{:S(2)}) collective-permute-start(bf16[256,1024]{1,0:T(8,128)(2,1)S(1)} %join.2.refs_1_), channel_id=1, source_target_pairs={{0,4},{1,5},{2,6},{3,7},{4,8},{5,9},{6,10},{7,11},{8,12},{9,13},{1... | collective-permute-start | bytes 1572872 | tf_op jit(solution)/shard_map/ppermute | solution.py:49
  20.7 15.1 %collective-permute-start.11 = (bf16[256,1024]{1,0:T(8,128)(2,1)S(1)}, bf16[256,1024]{1,0:T(8,128)(2,1)S(1)}, u32[]{:S(2)}, u32[]{:S(2)}) collective-permute-start(bf16[256,1024]{1,0:T(8,128)(2,1)S(1)} %join.3.refs_0_), channel_id=1, source_target_pairs={{0,4},{1,5},{2,6},{3,7},{4,8},{5,9},{6,10},{7,11},{8,12},{9,13},{1... | collective-permute-start | bytes 1572872 | tf_op jit(solution)/shard_map/ppermute | solution.py:49
  20.7 15.1 %collective-permute-start.12 = (bf16[256,1024]{1,0:T(8,128)(2,1)S(1)}, bf16[256,1024]{1,0:T(8,128)(2,1)S(1)}, u32[]{:S(2)}, u32[]{:S(2)}) collective-permute-start(bf16[256,1024]{1,0:T(8,128)(2,1)S(1)} %join.2.refs_1_), channel_id=1, source_target_pairs={{0,12},{1,13},{2,14},{3,15},{4,0},{5,1},{6,2},{7,3},{8,4},{9,5},{1... | collective-permute-start | bytes 1572872 | tf_op jit(solution)/shard_map/ppermute | solution.py:49
  30.2 8.7 %collective-permute-start.9 = (bf16[256,1024]{1,0:T(8,128)(2,1)S(1)}, bf16[256,1024]{1,0:T(8,128)(2,1)S(1)}, u32[]{:S(2)}, u32[]{:S(2)}) collective-permute-start(bf16[256,1024]{1,0:T(8,128)(2,1)S(1)} %collective-permute-done.8.refs_1_), channel_id=1, source_target_pairs={{0,12},{1,13},{2,14},{3,15},{4,0},{5,1},{6,2},{7,3},{8,4},{9,5},{1... | collective-permute-start | bytes 1572872 | tf_op jit(solution)/shard_map/ppermute | solution.py:49
  30.2 11.2 %collective-permute-start.10 = (bf16[256,1024]{1,0:T(8,128)(2,1)S(1)}, bf16[256,1024]{1,0:T(8,128)(2,1)S(1)}, u32[]{:S(2)}, u32[]{:S(2)}) collective-permute-start(bf16[256,1024]{1,0:T(8,128)(2,1)S(1)} %collective-permute-done.7.refs_0_), channel_id=1, source_target_pairs={{0,4},{1,5},{2,6},{3,7},{4,8},{5,9},{6,10},{7,11},{8,12},{9,13},{1... | collective-permute-start | bytes 1572872 | tf_op jit(solution)/shard_map/ppermute | solution.py:49
  61.9 6.5 %collective-permute-start.13 = (bf16[256,768]{1,0:T(8,128)(2,1)S(1)}, bf16[256,768]{1,0:T(8,128)(2,1)S(1)}, u32[]{:S(2)}, u32[]{:S(2)}) collective-permute-start(bf16[256,768]{1,0:T(8,128)(2,1)S(1)} %get-tuple-element.90), channel_id=1, source_target_pairs={{0,32},{32,0},{64,96},{96,64},{1,33},{33,1},{65,97},{97,65},{2,34}... | collective-permute-start | bytes 1179656 | tf_op jit(solution)/shard_map/ppermute | solution.py:366
  68.5 16.5 %collective-permute-start.18 = (bf16[256,768]{1,0:T(8,128)(2,1)S(1)}, bf16[256,768]{1,0:T(8,128)(2,1)S(1)}, u32[]{:S(2)}, u32[]{:S(2)}) collective-permute-start(bf16[256,768]{1,0:T(8,128)(2,1)S(1)} %fold.2), channel_id=1, source_target_pairs={{0,64},{32,96},{64,0},{96,32},{1,65},{33,97},{65,1},{97,33},{2,66}... | collective-permute-start | bytes 1179656 | tf_op jit(solution)/shard_map/ppermute | solution.py:368
  73.1 2.5 %collective-permute-start.15 = (bf16[256,512]{1,0:T(8,128)(2,1)S(1)}, bf16[256,512]{1,0:T(8,128)(2,1)S(1)}, u32[]{:S(2)}, u32[]{:S(2)}) collective-permute-start(bf16[256,512]{1,0:T(8,128)(2,1)S(1)} %get-tuple-element.95), channel_id=1, source_target_pairs={{0,32},{32,0},{64,96},{96,64},{1,33},{33,1},{65,97},{97,65},{2,34}... | collective-permute-start | bytes 786440 | tf_op jit(solution)/shard_map/ppermute | solution.py:371
  73.8 1.7 %collective-permute-start.16 = (bf16[256,512]{1,0:T(8,128)(2,1)S(1)}, bf16[256,512]{1,0:T(8,128)(2,1)S(1)}, u32[]{:S(2)}, u32[]{:S(2)}) collective-permute-start(bf16[256,512]{1,0:T(8,128)(2,1)S(1)} %get-tuple-element.96), channel_id=1, source_target_pairs={{0,32},{32,0},{64,96},{96,64},{1,33},{33,1},{65,97},{97,65},{2,34}... | collective-permute-start | bytes 786440 | tf_op jit(solution)/shard_map/ppermute | solution.py:371
  73.9 1.6 %collective-permute-start.17 = (bf16[256,256]{1,0:T(8,128)(2,1)S(1)}, bf16[256,256]{1,0:T(8,128)(2,1)S(1)}, u32[]{:S(2)}, u32[]{:S(2)}) collective-permute-start(bf16[256,256]{1,0:T(8,128)(2,1)S(1)} %get-tuple-element.97), channel_id=1, source_target_pairs={{0,32},{32,0},{64,96},{96,64},{1,33},{33,1},{65,97},{97,65},{2,34}... | collective-permute-start | bytes 393224 | tf_op jit(solution)/shard_map/ppermute | solution.py:371
  74.3 1.2 %collective-permute-start.14 = (f32[1,2048]{1,0:T(1,128)S(1)}, f32[1,2048]{1,0:T(1,128)S(1)}, u32[]{:S(2)}, u32[]{:S(2)}) collective-permute-start(f32[1,2048]{1,0:T(1,128)S(1)} %get-tuple-element.93.mass_ref), channel_id=1, source_target_pairs={{0,32},{32,0},{64,96},{96,64},{1,33},{33,1},{65,97},{97,65},{2,34}... | collective-permute-start | bytes 24584 | tf_op jit(solution)/shard_map/ppermute | solution.py:370
  75.7 17.4 %collective-permute-start.19 = (bf16[256,1280]{1,0:T(8,128)(2,1)S(1)}, bf16[256,1280]{1,0:T(8,128)(2,1)S(1)}, u32[]{:S(2)}, u32[]{:S(2)}) collective-permute-start(bf16[256,1280]{1,0:T(8,128)(2,1)S(1)} %get-tuple-element.98), channel_id=1, source_target_pairs={{0,64},{32,96},{64,0},{96,32},{1,65},{33,97},{65,1},{97,33},{2,66}... | collective-permute-start | bytes 1966088 | tf_op jit(solution)/shard_map/ppermute | solution.py:372
  76.9 16.4 %collective-permute-start.21 = (f32[1,2048]{1,0:T(1,128)S(1)}, f32[1,2048]{1,0:T(1,128)S(1)}, u32[]{:S(2)}, u32[]{:S(2)}) collective-permute-start(f32[1,2048]{1,0:T(1,128)S(1)} %get-tuple-element.108.mass_ref), channel_id=1, source_target_pairs={{0,64},{32,96},{64,0},{96,32},{1,65},{33,97},{65,1},{97,33},{2,66}... | collective-permute-start | bytes 24584 | tf_op jit(solution)/shard_map/ppermute | solution.py:377
  85.3 8.0 %collective-permute-start.20 = (bf16[256,2048]{1,0:T(8,128)(2,1)S(1)}, bf16[256,2048]{1,0:T(8,128)(2,1)S(1)}, u32[]{:S(2)}, u32[]{:S(2)}) collective-permute-start(bf16[256,2048]{1,0:T(8,128)(2,1)S(1)} %get-tuple-element.107), channel_id=1, source_target_pairs={{0,32},{32,0},{64,96},{96,64},{1,33},{33,1},{65,97},{97,65},{2,34}... | collective-permute-start | bytes 3145736 | tf_op jit(solution)/shard_map/ppermute | solution.py:376

commit v6 on v5

--- a/solution.py
+++ b/solution.py
@@ -346,8 +346,8 @@
     e3a, e1b = _send(e0a, _second(1)), _send(e0b, _second(-1))
     calls = [_soft([e0a, e0b], (0, 1), c, None)]
     previous, et = calls[0][4][0], calls[0][3]
+    e2b, e2a = _send(e3b, _second(1)), _send(e1a, _second(-1))
     e3b, e1a, et = lax.optimization_barrier((e3b, e1a, et))
-    e2b, e2a = _send(e3b, _second(1)), _send(e1a, _second(-1))
     calls.append(_soft([e3b, e1a], (7, 2), c, et))
     calls.append(_soft([e3a, e1b], (6, 3), c, calls[1][3]))
     calls.append(_soft([e2a, e2b], (4, 5), c, calls[2][3]))

time: 95.3 us -> 95 us (level)
  waiting for transfers between devices: 20.8 us -> 18.8 us
  blocking collectives: 14.7 us -> 16.3 us
    ppermute x13, waiting for transfers between devices: 11.4 us -> 9.42 us  [_send(): return lax.ppermute(value, AXES, pairs)]
    all_to_all x1, blocking collectives: 14.7 us -> 16.3 us  [on_device(): total = _merge(lax.all_to_all(parts, 'cent', 0, 0).reshape(32, 16, 128))]
  transfers between devices with their start and end apart: 22 -> 22, of which waited for: 10 -> 7; matrix products, arithmetic and copies ran while one was open for 0% -> 0% of each run, Pallas kernels for 23% -> 23%
where the time goes in v6:
time: 95 us; the launch traced here: 94.9 us
  starting transfers between devices  29.8 us (31%)
  Pallas kernels  29.1 us (31%)
  waiting for transfers between devices  18.8 us (20%)
  blocking collectives  16.3 us (17%)
    pallas_call x17, Pallas kernels, _kernel(): pl.pallas_call(body, out_shape=outs, in_specs=[HBM if i in hbm_in else VM...  29.1 us
    ppermute x13, starting transfers between devices, _send(): return lax.ppermute(value, AXES, pairs)  20.1 us
    all_to_all x1, blocking collectives, on_device(): total = _merge(lax.all_to_all(parts, 'cent', 0, 0).reshape(32, 16, 128))  16.3 us
    ppermute x13, waiting for transfers between devices, _send(): return lax.ppermute(value, AXES, pairs)  9.42 us
    ppermute x1, waiting for transfers between devices, on_device(): in1 = _copy(lax.ppermute(out1, 'dp', NEAR))  6.78 us
    ppermute x1, starting transfers between devices, on_device(): out0 = _fold(kept, *(lax.ppermute(part, 'dp', CORE) for part in sent))  5.34 us
  transfers between devices with their start and end apart: 22, of which 7 were waited for; matrix products, arithmetic and copies ran while one was open for 0% of the time, Pallas kernels for 23%

profile of v6, /device:TPU:1, one launch (start us, length us, event | category | flops | bytes accessed | tf_op | source)
XLA Modules:
  0.0 94.9 jit_solution(512383403272878493)
XLA Ops:
  0.6 3.8 %collective-permute-start.3 = (bf16[64,1024]{1,0:T(8,128)(2,1)}, bf16[64,1024]{1,0:T(8,128)(2,1)S(1)}, u32[]{:S(2)}, u32[]{:S(2)}) collective-permute-start(bf16[64,1024]{1,0:T(8,128)(2,1)} %refs_0_), channel_id=1, source_target_pairs={{0,16},{1,17},{2,18},{3,19},{4,20},{5,21},{6,22},{7,23},{8,24},{9,... | collective-permute-start | bytes 393224 | tf_op jit(solution)/shard_map/ppermute | solution.py:49
  4.5 1.2 %collective-permute-start.2 = (bf16[64,1024]{1,0:T(8,128)(2,1)}, bf16[64,1024]{1,0:T(8,128)(2,1)S(1)}, u32[]{:S(2)}, u32[]{:S(2)}) collective-permute-start(bf16[64,1024]{1,0:T(8,128)(2,1)} %refs_0_), channel_id=1, source_target_pairs={{0,1},{1,2},{2,3},{3,0},{4,5},{5,6},{6,7},{7,4},{8,9},{9,10},{10,1... | collective-permute-start | bytes 393224 | tf_op jit(solution)/shard_map/ppermute | solution.py:49
  5.7 2.5 %collective-permute-start.1 = (bf16[64,1024]{1,0:T(8,128)(2,1)}, bf16[64,1024]{1,0:T(8,128)(2,1)S(1)}, u32[]{:S(2)}, u32[]{:S(2)}) collective-permute-start(bf16[64,1024]{1,0:T(8,128)(2,1)} %refs_0_), channel_id=1, source_target_pairs={{0,2},{1,3},{2,0},{3,1},{4,6},{5,7},{6,4},{7,5},{8,10},{9,11},{10,... | collective-permute-start | bytes 393224 | tf_op jit(solution)/shard_map/ppermute | solution.py:49
  8.1 1.2 %collective-permute-start = (bf16[64,1024]{1,0:T(8,128)(2,1)}, bf16[64,1024]{1,0:T(8,128)(2,1)S(1)}, u32[]{:S(2)}, u32[]{:S(2)}) collective-permute-start(bf16[64,1024]{1,0:T(8,128)(2,1)} %refs_0_), channel_id=1, source_target_pairs={{0,3},{1,0},{2,1},{3,2},{4,7},{5,4},{6,5},{7,6},{8,11},{9,8},{10,9... | collective-permute-start | bytes 393224 | tf_op jit(solution)/shard_map/ppermute | solution.py:49
  9.7 1.7 %collective-permute-start.5 = (bf16[64,1024]{1,0:T(8,128)(2,1)S(1)}, bf16[64,1024]{1,0:T(8,128)(2,1)S(1)}, u32[]{:S(2)}, u32[]{:S(2)}) collective-permute-start(bf16[64,1024]{1,0:T(8,128)(2,1)S(1)} %copy.13.refs_1_), channel_id=1, source_target_pairs={{0,2},{1,3},{2,0},{3,1},{4,6},{5,7},{6,4},{7,5},{8,10},{9,11},{10,... | collective-permute-start | bytes 393224 | tf_op jit(solution)/shard_map/ppermute | solution.py:49
  11.4 1.2 %collective-permute-start.4 = (bf16[64,1024]{1,0:T(8,128)(2,1)S(1)}, bf16[64,1024]{1,0:T(8,128)(2,1)S(1)}, u32[]{:S(2)}, u32[]{:S(2)}) collective-permute-start(bf16[64,1024]{1,0:T(8,128)(2,1)S(1)} %copy.13.refs_1_), channel_id=1, source_target_pairs={{0,3},{1,0},{2,1},{3,2},{4,7},{5,4},{6,5},{7,6},{8,11},{9,8},{10,9... | collective-permute-start | bytes 393224 | tf_op jit(solution)/shard_map/ppermute | solution.py:49
  12.5 3.3 %collective-permute-done.6.refs_3_ = bf16[64,1024]{1,0:T(8,128)(2,1)S(1)} collective-permute-done((bf16[64,1024]{1,0:T(8,128)(2,1)S(1)}, bf16[64,1024]{1,0:T(8,128)(2,1)S(1)}, u32[]{:S(2)}, u32[]{:S(2)}) %collective-permute-start.6) | collective-permute-done | bytes 131104 | tf_op jit(solution)/shard_map/ppermute | solution.py:49
  15.8 0.9 collective-permute-done.4.refs_3_
  16.7 1.7 %collective-permute-start.9 = (bf16[256,1024]{1,0:T(8,128)(2,1)S(1)}, bf16[256,1024]{1,0:T(8,128)(2,1)S(1)}, u32[]{:S(2)}, u32[]{:S(2)}) collective-permute-start(bf16[256,1024]{1,0:T(8,128)(2,1)S(1)} %join.3.refs_1_), channel_id=1, source_target_pairs={{0,4},{1,5},{2,6},{3,7},{4,8},{5,9},{6,10},{7,11},{8,12},{9,13},{1... | collective-permute-start | bytes 1572872 | tf_op jit(solution)/shard_map/ppermute | solution.py:49
  18.5 2.2 %collective-permute-start.7 = (bf16[256,1024]{1,0:T(8,128)(2,1)S(1)}, bf16[256,1024]{1,0:T(8,128)(2,1)S(1)}, u32[]{:S(2)}, u32[]{:S(2)}) collective-permute-start(bf16[256,1024]{1,0:T(8,128)(2,1)S(1)} %join.2.refs_0_), channel_id=1, source_target_pairs={{0,12},{1,13},{2,14},{3,15},{4,0},{5,1},{6,2},{7,3},{8,4},{9,5},{1... | collective-permute-start | bytes 1572872 | tf_op jit(solution)/shard_map/ppermute | solution.py:49
  20.7 1.4 %collective-permute-start.12 = (bf16[256,1024]{1,0:T(8,128)(2,1)S(1)}, bf16[256,1024]{1,0:T(8,128)(2,1)S(1)}, u32[]{:S(2)}, u32[]{:S(2)}) collective-permute-start(bf16[256,1024]{1,0:T(8,128)(2,1)S(1)} %join.3.refs_1_), channel_id=1, source_target_pairs={{0,12},{1,13},{2,14},{3,15},{4,0},{5,1},{6,2},{7,3},{8,4},{9,5},{1... | collective-permute-start | bytes 1572872 | tf_op jit(solution)/shard_map/ppermute | solution.py:49
  22.1 5.3 %collective-permute-done.9.refs_0_ = bf16[256,1024]{1,0:T(8,128)(2,1)S(1)} collective-permute-done((bf16[256,1024]{1,0:T(8,128)(2,1)S(1)}, bf16[256,1024]{1,0:T(8,128)(2,1)S(1)}, u32[]{:S(2)}, u32[]{:S(2)}) %collective-permute-start.9) | collective-permute-done | bytes 524320 | tf_op jit(solution)/shard_map/ppermute | solution.py:49
  27.4 2.8 %collective-permute-start.8 = (bf16[256,1024]{1,0:T(8,128)(2,1)S(1)}, bf16[256,1024]{1,0:T(8,128)(2,1)S(1)}, u32[]{:S(2)}, u32[]{:S(2)}) collective-permute-start(bf16[256,1024]{1,0:T(8,128)(2,1)S(1)} %collective-permute-done.7.refs_1_), channel_id=1, source_target_pairs={{0,12},{1,13},{2,14},{3,15},{4,0},{5,1},{6,2},{7,3},{8,4},{9,5},{1... | collective-permute-start | bytes 1572872 | tf_op jit(solution)/shard_map/ppermute | solution.py:49
  30.2 3.1 %soft.4 = (f32[256,2048]{1,0:T(8,128)S(1)}, f32[256,2048]{1,0:T(8,128)S(1)}, f32[4,128]{1,0:T(4,128)S(1)}, f32[4,128]{1,0:T(4,128)S(1)}, bf16[1024,2048]{1,0:T(8,128)(2,1)S(1)}, /*index=5*/bf16[256,2048]{1,0:T(8,128)(2,1)S(1)}) custom-call(bf16[256,1024]{1,0:T(8,128)(2,1)S(1)} %join.2.refs_0_, bf16[256,1024]{1,0:T(8,128)(2,1)S(1)} %join.3.refs_1_, ...), custom_call_target="tpu_custom_call" | custom-call | tf_op jit(solution)/shard_map/soft/pallas_call | solution.py:57
  33.4 3.1 %soft.5 = (f32[256,2048]{1,0:T(8,128)S(1)}, f32[256,2048]{1,0:T(8,128)S(1)}, f32[4,128]{1,0:T(4,128)S(1)}, f32[4,128]{1,0:T(4,128)S(1)}, bf16[1024,2048]{1,0:T(8,128)(2,1)S(1)}) custom-call(bf16[256,1024]{1,0:T(8,128)(2,1)S(1)} %collective-permute-done.9.refs_0_, ...), custom_call_target="tpu_custom_call", output_to_operand_aliasing={{4}: (3, {})} | custom-call | tf_op jit(solution)/shard_map/soft/pallas_call | solution.py:57
  36.4 3.1 %soft.6 = (f32[256,2048]{1,0:T(8,128)S(1)}, f32[256,2048]{1,0:T(8,128)S(1)}, f32[4,128]{1,0:T(4,128)S(1)}, f32[4,128]{1,0:T(4,128)S(1)}, bf16[1024,2048]{1,0:T(8,128)(2,1)S(1)}) custom-call(bf16[256,1024]{1,0:T(8,128)(2,1)S(1)} %collective-permute-done.11.refs_0_, ...), custom_call_target="tpu_custom_call", output_to_operand_aliasing={{4}: (3, {})} | custom-call | tf_op jit(solution)/shard_map/soft/pallas_call | solution.py:57
  39.6 3.1 %soft.7 = (f32[256,2048]{1,0:T(8,128)S(1)}, f32[256,2048]{1,0:T(8,128)S(1)}, f32[4,128]{1,0:T(4,128)S(1)}, f32[4,128]{1,0:T(4,128)S(1)}, bf16[1024,2048]{1,0:T(8,128)(2,1)S(1)}) custom-call(bf16[256,1024]{1,0:T(8,128)(2,1)S(1)} %collective-permute-done.8.refs_0_, ...), custom_call_target="tpu_custom_call", output_to_operand_aliasing={{4}: (3, {})} | custom-call | tf_op jit(solution)/shard_map/soft/pallas_call | solution.py:57
  42.8 16.3 %all_to_all.5.in_ref = f32[32,16,128]{2,1,0:T(8,128)S(1)} all-to-all(f32[32,16,128]{2,1,0:T(8,128)S(1)} %pack.1), channel_id=1, replica_groups=mesh['dp'=4,'cent'=32] {'cent'}, dimensions={0} | all-to-all | bytes 524288 | tf_op jit(solution)/shard_map/all_to_all | solution.py:363
  59.2 2.5 %assign.2 = (bf16[2048,768]{1,0:T(8,128)(2,1)S(1)}, bf16[256,768]{1,0:T(8,128)(2,1)S(1)}, bf16[256,768]{1,0:T(8,128)(2,1)S(1)}, f32[1,768]{1,0:T(1,128)S(1)}) custom-call(f32[256,2048]{1,0:T(8,128)S(1)} %get-tuple-element.72.refs_0_, f32[256,2048]{1,0:T(8,128)S(1)} %get-tuple-element.73.refs_1_, f32[256,2048]{1,0:T(8,128)S(1)} %get-tuple-element.74.refs_2_, ...), custom_call_target="tpu_custom_call" | custom-call | tf_op jit(solution)/shard_map/assign/pallas_call | solution.py:57
  61.6 5.3 %collective-permute-start.13 = (bf16[256,768]{1,0:T(8,128)(2,1)S(1)}, bf16[256,768]{1,0:T(8,128)(2,1)S(1)}, u32[]{:S(2)}, u32[]{:S(2)}) collective-permute-start(bf16[256,768]{1,0:T(8,128)(2,1)S(1)} %get-tuple-element.90), channel_id=1, source_target_pairs={{0,32},{32,0},{64,96},{96,64},{1,33},{33,1},{65,97},{97,65},{2,34}... | collective-permute-start | bytes 1179656 | tf_op jit(solution)/shard_map/ppermute | solution.py:366
  67.0 1.3 %collective-permute-done.13.refs_0_ = bf16[256,768]{1,0:T(8,128)(2,1)S(1)} collective-permute-done((bf16[256,768]{1,0:T(8,128)(2,1)S(1)}, bf16[256,768]{1,0:T(8,128)(2,1)S(1)}, u32[]{:S(2)}, u32[]{:S(2)}) %collective-permute-start.13) | collective-permute-done | bytes 393248 | tf_op jit(solution)/shard_map/ppermute | solution.py:366
  68.4 0.5 collective-permute-start.18
  68.9 3.9 %assign.3 = (bf16[2048,1280]{1,0:T(8,128)(2,1)S(1)}, bf16[256,512]{1,0:T(8,128)(2,1)S(1)}, bf16[256,512]{1,0:T(8,128)(2,1)S(1)}, bf16[256,256]{1,0:T(8,128)(2,1)...) custom-call(f32[256,2048]{1,0:T(8,128)S(1)} %get-tuple-element.72.refs_0_, ...), custom_call_target="tpu_custom_call" | custom-call | tf_op jit(solution)/shard_map/assign/pallas_call | solution.py:57
  72.8 0.7 collective-permute-start.15
  73.6 0.4 collective-permute-start.17
  74.1 1.1 %collective-permute-done.14.other_ref = f32[1,2048]{1,0:T(1,128)S(1)} collective-permute-done((f32[1,2048]{1,0:T(1,128)S(1)}, f32[1,2048]{1,0:T(1,128)S(1)}, u32[]{:S(2)}, u32[]{:S(2)}) %collective-permute-start.14) | collective-permute-done | bytes 8224 | tf_op jit(solution)/shard_map/ppermute | solution.py:370
  75.4 1.1 %collective-permute-start.19 = (bf16[256,1280]{1,0:T(8,128)(2,1)S(1)}, bf16[256,1280]{1,0:T(8,128)(2,1)S(1)}, u32[]{:S(2)}, u32[]{:S(2)}) collective-permute-start(bf16[256,1280]{1,0:T(8,128)(2,1)S(1)} %get-tuple-element.98), channel_id=1, source_target_pairs={{0,64},{32,96},{64,0},{96,32},{1,65},{33,97},{65,1},{97,33},{2,66}... | collective-permute-start | bytes 1966088 | tf_op jit(solution)/shard_map/ppermute | solution.py:372
  76.6 0.4 collective-permute-start.21
  77.0 7.7 %home.1 = (bf16[256,2048]{1,0:T(8,128)(2,1)S(1)}, bf16[256,2048]{1,0:T(8,128)(2,1)S(1)}, bf16[2048,2048]{1,0:T(8,128)(2,1)}) custom-call(bf16[1024,2048]{1,0:T(8,128)(2,1)S(1)} %get-tuple-element.71.refs_13_.et_ref, bf16[2048,768]{1,0:T(8,128)(2,1)S(1)} %get-tuple-element.99.a0, bf16[2048,1280]{1,0:T(8,128)(2,1)S(1)} %get-tuple-element.100.a1), custom_call_target="tpu_custom_call" | custom-call | flops 1 | tf_op jit(solution)/shard_map/home/pallas_call | solution.py:57
  85.1 1.0 %collective-permute-start.20 = (bf16[256,2048]{1,0:T(8,128)(2,1)S(1)}, bf16[256,2048]{1,0:T(8,128)(2,1)S(1)}, u32[]{:S(2)}, u32[]{:S(2)}) collective-permute-start(bf16[256,2048]{1,0:T(8,128)(2,1)S(1)} %get-tuple-element.107), channel_id=1, source_target_pairs={{0,32},{32,0},{64,96},{96,64},{1,33},{33,1},{65,97},{97,65},{2,34}... | collective-permute-start | bytes 3145736 | tf_op jit(solution)/shard_map/ppermute | solution.py:376
  86.1 6.8 %collective-permute-done.19.in_ref = bf16[256,1280]{1,0:T(8,128)(2,1)S(1)} collective-permute-done((bf16[256,1280]{1,0:T(8,128)(2,1)S(1)}, bf16[256,1280]{1,0:T(8,128)(2,1)S(1)}, u32[]{:S(2)}, u32[]{:S(2)}) %collective-permute-start.19) | collective-permute-done | bytes 655392 | tf_op jit(solution)/shard_map/ppermute | solution.py:372
  93.0 1.7 %final.1 = (bf16[256,2048]{1,0:T(8,128)(2,1)}, f32[1,2048]{1,0:T(1,128)}) custom-call(f32[256,2048]{1,0:T(8,128)S(1)} %base.1.base_ref, bf16[256,1280]{1,0:T(8,128)(2,1)S(1)} %copy.14.in_ref, bf16[256,2048]{1,0:T(8,128)(2,1)S(1)} %collective-permute-done.20.sent_ref, f32[1,2048]{1,0:T(1,128)S(1)} %get-tuple-element.108.mass_ref, ...), custom_call_target="tpu_custom_call" | custom-call | tf_op jit(solution)/shard_map/final/pallas_call | solution.py:57
  (34 shorter events, 1.7 us)
Async XLA Ops:
  0.6 17.8 %copy-start.1 = (bf16[64,1024]{1,0:T(8,128)(2,1)S(1)}, bf16[64,1024]{1,0:T(8,128)(2,1)}, u32[]{:S(2)}) copy-start(bf16[64,1024]{1,0:T(8,128)(2,1)} %refs_0_) | copy-start | bytes 393220
  0.6 8.6 %collective-permute-start.3 = (bf16[64,1024]{1,0:T(8,128)(2,1)}, bf16[64,1024]{1,0:T(8,128)(2,1)S(1)}, u32[]{:S(2)}, u32[]{:S(2)}) collective-permute-start(bf16[64,1024]{1,0:T(8,128)(2,1)} %refs_0_), channel_id=1, source_target_pairs={{0,16},{1,17},{2,18},{3,19},{4,20},{5,21},{6,22},{7,23},{8,24},{9,... | collective-permute-start | bytes 393224 | tf_op jit(solution)/shard_map/ppermute | solution.py:49
  4.5 6.9 %collective-permute-start.2 = (bf16[64,1024]{1,0:T(8,128)(2,1)}, bf16[64,1024]{1,0:T(8,128)(2,1)S(1)}, u32[]{:S(2)}, u32[]{:S(2)}) collective-permute-start(bf16[64,1024]{1,0:T(8,128)(2,1)} %refs_0_), channel_id=1, source_target_pairs={{0,1},{1,2},{2,3},{3,0},{4,5},{5,6},{6,7},{7,4},{8,9},{9,10},{10,1... | collective-permute-start | bytes 393224 | tf_op jit(solution)/shard_map/ppermute | solution.py:49
  5.7 6.9 %collective-permute-start.1 = (bf16[64,1024]{1,0:T(8,128)(2,1)}, bf16[64,1024]{1,0:T(8,128)(2,1)S(1)}, u32[]{:S(2)}, u32[]{:S(2)}) collective-permute-start(bf16[64,1024]{1,0:T(8,128)(2,1)} %refs_0_), channel_id=1, source_target_pairs={{0,2},{1,3},{2,0},{3,1},{4,6},{5,7},{6,4},{7,5},{8,10},{9,11},{10,... | collective-permute-start | bytes 393224 | tf_op jit(solution)/shard_map/ppermute | solution.py:49
  8.1 4.4 %collective-permute-start = (bf16[64,1024]{1,0:T(8,128)(2,1)}, bf16[64,1024]{1,0:T(8,128)(2,1)S(1)}, u32[]{:S(2)}, u32[]{:S(2)}) collective-permute-start(bf16[64,1024]{1,0:T(8,128)(2,1)} %refs_0_), channel_id=1, source_target_pairs={{0,3},{1,0},{2,1},{3,2},{4,7},{5,4},{6,5},{7,6},{8,11},{9,8},{10,9... | collective-permute-start | bytes 393224 | tf_op jit(solution)/shard_map/ppermute | solution.py:49
  9.3 20.9 %copy-start = (bf16[2048,1024]{1,0:T(8,128)(2,1)S(1)}, bf16[2048,1024]{1,0:T(8,128)(2,1)}, u32[]{:S(2)}) copy-start(bf16[2048,1024]{1,0:T(8,128)(2,1)} %refs_2_.7) | copy-start | bytes 12582916
  9.3 6.5 %collective-permute-start.6 = (bf16[64,1024]{1,0:T(8,128)(2,1)S(1)}, bf16[64,1024]{1,0:T(8,128)(2,1)S(1)}, u32[]{:S(2)}, u32[]{:S(2)}) collective-permute-start(bf16[64,1024]{1,0:T(8,128)(2,1)S(1)} %copy.13.refs_1_), channel_id=1, source_target_pairs={{0,1},{1,2},{2,3},{3,0},{4,5},{5,6},{6,7},{7,4},{8,9},{9,10},{10,1... | collective-permute-start | bytes 393224 | tf_op jit(solution)/shard_map/ppermute | solution.py:49
  9.7 6.1 %collective-permute-start.5 = (bf16[64,1024]{1,0:T(8,128)(2,1)S(1)}, bf16[64,1024]{1,0:T(8,128)(2,1)S(1)}, u32[]{:S(2)}, u32[]{:S(2)}) collective-permute-start(bf16[64,1024]{1,0:T(8,128)(2,1)S(1)} %copy.13.refs_1_), channel_id=1, source_target_pairs={{0,2},{1,3},{2,0},{3,1},{4,6},{5,7},{6,4},{7,5},{8,10},{9,11},{10,... | collective-permute-start | bytes 393224 | tf_op jit(solution)/shard_map/ppermute | solution.py:49
  11.4 5.3 %collective-permute-start.4 = (bf16[64,1024]{1,0:T(8,128)(2,1)S(1)}, bf16[64,1024]{1,0:T(8,128)(2,1)S(1)}, u32[]{:S(2)}, u32[]{:S(2)}) collective-permute-start(bf16[64,1024]{1,0:T(8,128)(2,1)S(1)} %copy.13.refs_1_), channel_id=1, source_target_pairs={{0,3},{1,0},{2,1},{3,2},{4,7},{5,4},{6,5},{7,6},{8,11},{9,8},{10,9... | collective-permute-start | bytes 393224 | tf_op jit(solution)/shard_map/ppermute | solution.py:49
  16.7 10.7 %collective-permute-start.9 = (bf16[256,1024]{1,0:T(8,128)(2,1)S(1)}, bf16[256,1024]{1,0:T(8,128)(2,1)S(1)}, u32[]{:S(2)}, u32[]{:S(2)}) collective-permute-start(bf16[256,1024]{1,0:T(8,128)(2,1)S(1)} %join.3.refs_1_), channel_id=1, source_target_pairs={{0,4},{1,5},{2,6},{3,7},{4,8},{5,9},{6,10},{7,11},{8,12},{9,13},{1... | collective-permute-start | bytes 1572872 | tf_op jit(solution)/shard_map/ppermute | solution.py:49
  18.5 9.0 %collective-permute-start.7 = (bf16[256,1024]{1,0:T(8,128)(2,1)S(1)}, bf16[256,1024]{1,0:T(8,128)(2,1)S(1)}, u32[]{:S(2)}, u32[]{:S(2)}) collective-permute-start(bf16[256,1024]{1,0:T(8,128)(2,1)S(1)} %join.2.refs_0_), channel_id=1, source_target_pairs={{0,12},{1,13},{2,14},{3,15},{4,0},{5,1},{6,2},{7,3},{8,4},{9,5},{1... | collective-permute-start | bytes 1572872 | tf_op jit(solution)/shard_map/ppermute | solution.py:49
  20.7 15.8 %collective-permute-start.12 = (bf16[256,1024]{1,0:T(8,128)(2,1)S(1)}, bf16[256,1024]{1,0:T(8,128)(2,1)S(1)}, u32[]{:S(2)}, u32[]{:S(2)}) collective-permute-start(bf16[256,1024]{1,0:T(8,128)(2,1)S(1)} %join.3.refs_1_), channel_id=1, source_target_pairs={{0,12},{1,13},{2,14},{3,15},{4,0},{5,1},{6,2},{7,3},{8,4},{9,5},{1... | collective-permute-start | bytes 1572872 | tf_op jit(solution)/shard_map/ppermute | solution.py:49
  22.1 14.3 %collective-permute-start.11 = (bf16[256,1024]{1,0:T(8,128)(2,1)S(1)}, bf16[256,1024]{1,0:T(8,128)(2,1)S(1)}, u32[]{:S(2)}, u32[]{:S(2)}) collective-permute-start(bf16[256,1024]{1,0:T(8,128)(2,1)S(1)} %join.2.refs_0_), channel_id=1, source_target_pairs={{0,4},{1,5},{2,6},{3,7},{4,8},{5,9},{6,10},{7,11},{8,12},{9,13},{1... | collective-permute-start | bytes 1572872 | tf_op jit(solution)/shard_map/ppermute | solution.py:49
  27.4 12.1 %collective-permute-start.10 = (bf16[256,1024]{1,0:T(8,128)(2,1)S(1)}, bf16[256,1024]{1,0:T(8,128)(2,1)S(1)}, u32[]{:S(2)}, u32[]{:S(2)}) collective-permute-start(bf16[256,1024]{1,0:T(8,128)(2,1)S(1)} %collective-permute-done.9.refs_0_), channel_id=1, source_target_pairs={{0,4},{1,5},{2,6},{3,7},{4,8},{5,9},{6,10},{7,11},{8,12},{9,13},{1... | collective-permute-start | bytes 1572872 | tf_op jit(solution)/shard_map/ppermute | solution.py:49
  27.4 12.1 %collective-permute-start.8 = (bf16[256,1024]{1,0:T(8,128)(2,1)S(1)}, bf16[256,1024]{1,0:T(8,128)(2,1)S(1)}, u32[]{:S(2)}, u32[]{:S(2)}) collective-permute-start(bf16[256,1024]{1,0:T(8,128)(2,1)S(1)} %collective-permute-done.7.refs_1_), channel_id=1, source_target_pairs={{0,12},{1,13},{2,14},{3,15},{4,0},{5,1},{6,2},{7,3},{8,4},{9,5},{1... | collective-permute-start | bytes 1572872 | tf_op jit(solution)/shard_map/ppermute | solution.py:49
  61.6 6.7 %collective-permute-start.13 = (bf16[256,768]{1,0:T(8,128)(2,1)S(1)}, bf16[256,768]{1,0:T(8,128)(2,1)S(1)}, u32[]{:S(2)}, u32[]{:S(2)}) collective-permute-start(bf16[256,768]{1,0:T(8,128)(2,1)S(1)} %get-tuple-element.90), channel_id=1, source_target_pairs={{0,32},{32,0},{64,96},{96,64},{1,33},{33,1},{65,97},{97,65},{2,34}... | collective-permute-start | bytes 1179656 | tf_op jit(solution)/shard_map/ppermute | solution.py:366
  68.4 16.3 %collective-permute-start.18 = (bf16[256,768]{1,0:T(8,128)(2,1)S(1)}, bf16[256,768]{1,0:T(8,128)(2,1)S(1)}, u32[]{:S(2)}, u32[]{:S(2)}) collective-permute-start(bf16[256,768]{1,0:T(8,128)(2,1)S(1)} %fold.2), channel_id=1, source_target_pairs={{0,64},{32,96},{64,0},{96,32},{1,65},{33,97},{65,1},{97,33},{2,66}... | collective-permute-start | bytes 1179656 | tf_op jit(solution)/shard_map/ppermute | solution.py:368
  72.8 2.5 %collective-permute-start.15 = (bf16[256,512]{1,0:T(8,128)(2,1)S(1)}, bf16[256,512]{1,0:T(8,128)(2,1)S(1)}, u32[]{:S(2)}, u32[]{:S(2)}) collective-permute-start(bf16[256,512]{1,0:T(8,128)(2,1)S(1)} %get-tuple-element.95), channel_id=1, source_target_pairs={{0,32},{32,0},{64,96},{96,64},{1,33},{33,1},{65,97},{97,65},{2,34}... | collective-permute-start | bytes 786440 | tf_op jit(solution)/shard_map/ppermute | solution.py:371
  73.5 1.7 %collective-permute-start.16 = (bf16[256,512]{1,0:T(8,128)(2,1)S(1)}, bf16[256,512]{1,0:T(8,128)(2,1)S(1)}, u32[]{:S(2)}, u32[]{:S(2)}) collective-permute-start(bf16[256,512]{1,0:T(8,128)(2,1)S(1)} %get-tuple-element.96), channel_id=1, source_target_pairs={{0,32},{32,0},{64,96},{96,64},{1,33},{33,1},{65,97},{97,65},{2,34}... | collective-permute-start | bytes 786440 | tf_op jit(solution)/shard_map/ppermute | solution.py:371
  73.6 1.6 %collective-permute-start.17 = (bf16[256,256]{1,0:T(8,128)(2,1)S(1)}, bf16[256,256]{1,0:T(8,128)(2,1)S(1)}, u32[]{:S(2)}, u32[]{:S(2)}) collective-permute-start(bf16[256,256]{1,0:T(8,128)(2,1)S(1)} %get-tuple-element.97), channel_id=1, source_target_pairs={{0,32},{32,0},{64,96},{96,64},{1,33},{33,1},{65,97},{97,65},{2,34}... | collective-permute-start | bytes 393224 | tf_op jit(solution)/shard_map/ppermute | solution.py:371
  74.0 1.2 %collective-permute-start.14 = (f32[1,2048]{1,0:T(1,128)S(1)}, f32[1,2048]{1,0:T(1,128)S(1)}, u32[]{:S(2)}, u32[]{:S(2)}) collective-permute-start(f32[1,2048]{1,0:T(1,128)S(1)} %get-tuple-element.93.mass_ref), channel_id=1, source_target_pairs={{0,32},{32,0},{64,96},{96,64},{1,33},{33,1},{65,97},{97,65},{2,34}... | collective-permute-start | bytes 24584 | tf_op jit(solution)/shard_map/ppermute | solution.py:370
  75.4 17.4 %collective-permute-start.19 = (bf16[256,1280]{1,0:T(8,128)(2,1)S(1)}, bf16[256,1280]{1,0:T(8,128)(2,1)S(1)}, u32[]{:S(2)}, u32[]{:S(2)}) collective-permute-start(bf16[256,1280]{1,0:T(8,128)(2,1)S(1)} %get-tuple-element.98), channel_id=1, source_target_pairs={{0,64},{32,96},{64,0},{96,32},{1,65},{33,97},{65,1},{97,33},{2,66}... | collective-permute-start | bytes 1966088 | tf_op jit(solution)/shard_map/ppermute | solution.py:372
  76.6 16.4 %collective-permute-start.21 = (f32[1,2048]{1,0:T(1,128)S(1)}, f32[1,2048]{1,0:T(1,128)S(1)}, u32[]{:S(2)}, u32[]{:S(2)}) collective-permute-start(f32[1,2048]{1,0:T(1,128)S(1)} %get-tuple-element.108.mass_ref), channel_id=1, source_target_pairs={{0,64},{32,96},{64,0},{96,32},{1,65},{33,97},{65,1},{97,33},{2,66}... | collective-permute-start | bytes 24584 | tf_op jit(solution)/shard_map/ppermute | solution.py:377
  85.1 8.0 %collective-permute-start.20 = (bf16[256,2048]{1,0:T(8,128)(2,1)S(1)}, bf16[256,2048]{1,0:T(8,128)(2,1)S(1)}, u32[]{:S(2)}, u32[]{:S(2)}) collective-permute-start(bf16[256,2048]{1,0:T(8,128)(2,1)S(1)} %get-tuple-element.107), channel_id=1, source_target_pairs={{0,32},{32,0},{64,96},{96,64},{1,33},{33,1},{65,97},{97,65},{2,34}... | collective-permute-start | bytes 3145736 | tf_op jit(solution)/shard_map/ppermute | solution.py:376
